TPU v7x, 32 devices: a whole 2x2x4 slice. The times are simulated.
32 devices in a mesh: groups: 2 (over y), row: 4 (over z), tile: 4 (over x, core).
Axes of the slice: x: 2, y: 2, z: 4, core: 2. Of those that a mesh axis runs over, the one named last changes fastest.
Arguments:
- blocks: bfloat16 [512, 4, 128, 128], P(('groups', 'row', 'tile')), parts along dimension 0, may hold values from -0.4375 to 0.4375
- block_cols: int32 [512, 4], P(('groups', 'row')), parts along dimension 0, may hold values from -1 to 511, as said below
- pair_low: int32 [8], P('groups'), parts along dimension 0, may hold values from 0 to 248, as said below
Outputs:
- gram_band: float32 [8, 2048, 128], P(('groups', 'tile'), 'row'), parts along dimension 0
There are 2 independent parts, one for each index of `groups`. A program takes and returns all parts, laid end to end along the dimension named above; each array names one. Nothing has to cross between parts.
Inputs may be any that keep to these rules, and one draw needn't show every extreme that they name: Entries are distinct multiples of 8; the partner block row of pair_low[p] is 511 - pair_low[p]. `block_cols`: in each panel the entries other than -1 are distinct and lie within 8 consecutive column blocks; each panel has at least two of them, and exactly one of them equals a block row of some pair (pair_low[p] or 511 - pair_low[p]). Among the 16 panels of one device (aligned blocks of 16 panels), exactly 4 hold a block row of a pair p with p = t, for each t from 0 to 3.
All inputs are finite; a program needn't handle non-finite values.
Results may differ from a plain program's by a relative error of at most 0.0003.
Values may be sent and summed in bfloat16 or wider, within the bound.
No kernel may reach another device: no remote copies, remote signals or barrier semaphores. Data moves between devices by JAX's collectives and lax.ppermute only.
A program may use at most 64 MiB of HBM per device.

v0:
```python
import functools

import jax
import jax.numpy as jnp
from jax import lax
from jax.experimental import pallas as pl
from jax.experimental.pallas import tpu as pltpu
from jax.sharding import PartitionSpec as P

NB = 512
SPAN = 8
STRIP = 2 * SPAN
TRASH = 2 * STRIP
EXTRA = 16

VMEM = pl.BlockSpec(memory_space=pltpu.VMEM)
SMEM = pl.BlockSpec(memory_space=pltpu.SMEM)
ANY = pl.BlockSpec(memory_space=pl.ANY)
PARAMS = pltpu.CompilerParams(vmem_limit_bytes=32 * 1024 * 1024)


def encode(block):
    top = jnp.max(jnp.abs(block), axis=0, keepdims=True)
    power = jnp.ceil(jnp.log2(jnp.maximum(top, 1e-30)))
    scaled = jnp.round(block * jnp.exp2(15.0 - power))
    codes = jnp.clip(scaled, -32767.0, 32767.0).astype(jnp.int32).astype(jnp.int16)
    return codes, power


def pack(blocks, message_ref, power_ref):
    size = blocks[0].shape[0]
    power_ref[...] = jnp.zeros_like(power_ref)
    for at, block in enumerate(blocks):
        codes, power = encode(block)
        message_ref[at * size : (at + 1) * size, :] = codes
        power_ref[at : at + 1, :] = power
    message_ref[len(blocks) * size :, :] = power_ref[...].astype(jnp.int32).astype(jnp.int16)


def powers_of(message_ref):
    rows = message_ref.shape[0]
    power = message_ref[rows - EXTRA :, :].astype(jnp.int32).astype(jnp.float32)
    return jnp.exp2(power - 15.0)


def unpack(message_ref, scales, at, size):
    codes = message_ref[at * size : (at + 1) * size, :].astype(jnp.int32).astype(jnp.float32)
    return codes * scales[at : at + 1, :]


def plan_kernel(panels_here, cols_ref, low_ref, plan_ref, count_ref):
    here = lax.axis_index("tile")
    for at in range(4):
        count_ref[at] = 0
    quota = panels_here // lax.axis_size("tile")

    def one(step, carry):
        mate = step // panels_here
        panel = step % panels_here
        row = (here ^ mate) * panels_here + panel
        cols = [cols_ref[row, slot] for slot in range(4)]
        tile = jnp.int32(0)
        slot_hit = jnp.int32(0)
        target = jnp.int32(0)
        for slot, col in enumerate(cols):
            folded = jnp.minimum(col, NB - 1 - col)
            for index in range(low_ref.shape[0]):
                hit = folded == low_ref[index]
                tile = jnp.where(hit, index, tile)
                slot_hit = jnp.where(hit, slot, slot_hit)
                target = jnp.where(hit, col, target)
        apart = tile ^ here
        half = jnp.where(target >= NB // 2, SPAN, 0)
        local = jnp.where(apart == 0, 1, 0)

        @pl.when((apart == 0) | (apart == 2))
        def _():
            group = local * 2 + mate
            entry = group * quota + count_ref[group]
            count_ref[group] = count_ref[group] + 1
            plan_ref[entry, 0] = panel
            plan_ref[entry, 1] = slot_hit
            for slot, col in enumerate(cols):
                place = col - target + SPAN - 1
                good = (col >= 0) & (place >= 0) & (place < SPAN)
                plan_ref[entry, 2 + slot] = jnp.where(good, local * STRIP + half + place, TRASH)

        return carry

    lax.fori_loop(0, 2 * panels_here, one, 0)


def products(plan_ref, own_ref, mate_ref, held, sums, sems):
    entries = held.shape[0]
    quota = entries // 4
    copies = []
    for entry in range(entries):
        source = mate_ref if entry // quota % 2 else own_ref
        copies.append(pltpu.make_async_copy(source.at[plan_ref[entry, 0]], held.at[entry], sems.at[entry]))
        copies[-1].start()
    sums[...] = jnp.zeros_like(sums)
    for entry in range(entries):
        copies[entry].wait()
        column = held[entry, plan_ref[entry, 1]]
        for slot in range(held.shape[1]):
            place = plan_ref[entry, 2 + slot]
            sums[place] += lax.dot_general(
                column, held[entry, slot], (((0,), (0,)), ((), ())), preferred_element_type=jnp.float32
            )


def split_kernel(plan_ref, own_ref, mate_ref, x_ref, z1_ref, z2_ref, z3_ref, keep_p, keep_q, held, sums, power, sems):
    products(plan_ref, own_ref, mate_ref, held, sums, sems)
    here = lax.axis_index("row")
    pack([sums[4 * owner + i] for owner in range(4) for i in range(2)], x_ref, power)
    for apart, z_ref in ((1, z1_ref), (2, z2_ref), (3, z3_ref)):
        first = 4 * (here ^ apart) + 2
        pack([sums[first], sums[first + 1], sums[STRIP + first], sums[STRIP + first + 1]], z_ref, power)
    for owner in range(4):
        for i in range(2):
            keep_p[2 * owner + i] = sums[STRIP + 4 * owner + i]
    for i in range(2):
        keep_q[i] = sums[4 * here + 2 + i]
        keep_q[2 + i] = sums[STRIP + 4 * here + 2 + i]


def after_x_kernel(keep_p, x_ref, z1_ref, z2_ref, z3_ref, own_ref, sums, power):
    here = lax.axis_index("row")
    size = keep_p.shape[1]
    scales = powers_of(x_ref)
    for at in range(keep_p.shape[0]):
        sums[at] = keep_p[at] + unpack(x_ref, scales, at, size)
    for apart, z_ref in ((1, z1_ref), (2, z2_ref), (3, z3_ref)):
        first = 2 * (here ^ apart)
        pack([sums[first], sums[first + 1]], z_ref, power)
    for i in range(2):
        own_ref[i] = sums[2 * here + i]


def after_z_kernel(keep_q, z1_ref, z2_ref, z3_ref, x_ref, own_ref, power):
    size = keep_q.shape[1]
    scales = [powers_of(ref) for ref in (z1_ref, z2_ref, z3_ref)]
    totals = []
    for at in range(4):
        total = keep_q[at]
        for ref, scale in zip((z1_ref, z2_ref, z3_ref), scales):
            total = total + unpack(ref, scale, at, size)
        totals.append(total)
    pack(totals[:2], x_ref, power)
    own_ref[0] = totals[2]
    own_ref[1] = totals[3]


def last_kernel(own_p, z1_ref, z2_ref, z3_ref, own_q, x_ref, out_ref):
    size = own_p.shape[1]
    odd = lax.axis_index("row") % 2
    scales = [powers_of(ref) for ref in (z1_ref, z2_ref, z3_ref)]
    for at in range(2):
        total = own_p[at]
        for ref, scale in zip((z1_ref, z2_ref, z3_ref), scales):
            total = total + unpack(ref, scale, at, size)
        out_ref[0, at * size : (at + 1) * size, :] = total
    scale = powers_of(x_ref)
    for at in range(2):
        total = own_q[at] + unpack(x_ref, scale, at, size)
        if at == 1:
            rows = lax.broadcasted_iota(jnp.int32, total.shape, 0)
            columns = lax.broadcasted_iota(jnp.int32, total.shape, 1)
            total = total + jnp.where((rows == columns) & (odd == 1), 1.0, 0.0)
        out_ref[0, (2 + at) * size : (3 + at) * size, :] = total


def full_kernel(plan_ref, own_ref, mate_ref, x_ref, keep_ref, held, sums, power, sems):
    products(plan_ref, own_ref, mate_ref, held, sums, sems)
    pack([sums[at] for at in range(STRIP)], x_ref, power)
    keep_ref[...] = sums[STRIP : 2 * STRIP]


def add_kernel(keep_ref, x_ref, sum_ref):
    size = keep_ref.shape[1]
    scales = powers_of(x_ref)
    for at in range(STRIP):
        sum_ref[at] = keep_ref[at] + unpack(x_ref, scales, at, size)


def call(kernel, outs, operands, specs, scratch=(), flops=0, size=1 << 20):
    return pl.pallas_call(
        kernel,
        out_shape=outs,
        in_specs=specs,
        out_specs=jax.tree.map(lambda _: VMEM, outs),
        scratch_shapes=list(scratch),
        compiler_params=PARAMS,
        cost_estimate=pl.CostEstimate(flops=flops, bytes_accessed=size, transcendentals=0),
    )(*operands)


def on_device(blocks, block_cols, pair_low):
    panels_here, slots, size, _ = blocks.shape
    tiles_count = lax.axis_size("tile")
    rows_count = lax.axis_size("row")
    assert tiles_count == 4 and pair_low.shape[0] == 4 and slots == 4
    entries = panels_here

    def swap(value, axis, apart):
        return lax.ppermute(value, axis, [(i, i ^ apart) for i in range(lax.axis_size(axis))])

    def message(count):
        return jax.ShapeDtypeStruct((count * size + EXTRA, size), jnp.int16)

    def full(count):
        return jax.ShapeDtypeStruct((count, size, size), jnp.float32)

    mate = swap(blocks, "tile", 1)
    plan = pl.pallas_call(
        functools.partial(plan_kernel, panels_here),
        out_shape=jax.ShapeDtypeStruct((entries, 8), jnp.int32),
        in_specs=[SMEM, SMEM],
        out_specs=SMEM,
        scratch_shapes=[pltpu.SMEM((4,), jnp.int32)],
        cost_estimate=pl.CostEstimate(flops=0, bytes_accessed=1 << 22, transcendentals=0),
    )(block_cols, pair_low)

    power = pltpu.VMEM((EXTRA, size), jnp.float32)
    scratch = [
        pltpu.VMEM((entries, slots, size, size), blocks.dtype),
        pltpu.VMEM((2 * STRIP + 1, size, size), jnp.float32),
        power,
        pltpu.SemaphoreType.DMA((entries,)),
    ]
    operands = (plan, blocks, mate)
    specs = [SMEM, ANY, ANY]

    if rows_count != 4:
        across, keep = call(full_kernel, [message(STRIP), full(STRIP)], operands, specs, scratch, 1 << 28, 4 << 20)
        strip = call(add_kernel, full(STRIP), (keep, swap(across, "tile", 2)), [VMEM, VMEM])
        share = lax.psum_scatter(strip.reshape(1, STRIP * size, size), "row", scatter_dimension=1, tiled=True)
        rows = lax.axis_index("row") * share.shape[1] + jnp.arange(share.shape[1], dtype=jnp.int32)
        unit = (rows // size % SPAN == SPAN - 1)[:, None] & ((rows % size)[:, None] == jnp.arange(size)[None, :])
        return share + unit.astype(jnp.float32)[None]

    x_p, q1, q2, q3, keep_p, keep_q = call(
        split_kernel,
        [message(8), message(4), message(4), message(4), full(8), full(4)],
        operands, specs, scratch, 1 << 28, 4 << 20,
    )
    q3 = swap(q3, "row", 3)
    q2 = swap(q2, "row", 2)
    x_p = swap(x_p, "tile", 2)
    q1 = swap(q1, "row", 1)
    p1, p2, p3, own_p = call(
        after_x_kernel, [message(2)] * 3 + [full(2)], (keep_p, x_p), [VMEM] * 2, [pltpu.VMEM((8, size, size), jnp.float32), power]
    )
    p3 = swap(p3, "row", 3)
    p2 = swap(p2, "row", 2)
    p1 = swap(p1, "row", 1)
    x_q, own_q = call(after_z_kernel, [message(2), full(2)], (keep_q, q1, q2, q3), [VMEM] * 4, [power])
    x_q = swap(x_q, "tile", 2)
    return call(
        last_kernel, jax.ShapeDtypeStruct((1, 4 * size, size), jnp.float32), (own_p, p1, p2, p3, own_q, x_q), [VMEM] * 6
    )


def solution(mesh):
    return jax.shard_map(
        on_device,
        mesh=mesh,
        in_specs=(
            P(("groups", "row", "tile"), None, None, None),
            P(("groups", "row"), None),
            P("groups"),
        ),
        out_specs=P(("groups", "tile"), "row", None),
        check_vma=False,
    )
```

profile of v0, /device:TPU:0, one launch (start us, length us, event | category | flops | bytes accessed | tf_op | source)
XLA Modules:
  0.0 44.5 jit_solution(7647220033670592377)
XLA Ops:
  0.0 0.5 %collective-permute-start = (bf16[16,4,128,128]{3,2,1,0:T(8,128)(2,1)}, bf16[16,4,128,128]{3,2,1,0:T(8,128)(2,1)S(1)}, u32[]{:S(2)}, u32[]{:S(2)}) collective-permute-start(bf16[16,4,128,128]{3,2,1,0:T(8,128)(2,1)} %own_ref.1), channel_id=1, source_target_pairs={{0,1},{1,0},{2,3},{3,2},{4,5},{5,4},{6,7},{7,6},{8,9},{9,8},{10,11... | collective-permute-start | bytes 6291464 | tf_op jit(solution)/shard_map/ppermute | solution.py:206
  0.5 1.4 %copy.4.cols_ref = s32[64,4]{1,0:T(8,128)} copy(s32[64,4]{0,1:T(4,128)} %param.4) | data formatting | bytes 2048 | tf_op args[1]
  1.8 3.8 %shard_map.37.plan_ref = s32[16,8]{1,0:T(8,128)} custom-call(s32[64,4]{1,0:T(8,128)} %copy.4.cols_ref, s32[4]{0:T(128)} %low_ref.1), custom_call_target="tpu_custom_call" | custom-call | bytes 4194304 | tf_op jit(solution)/shard_map/pallas_call | solution.py:215
  5.6 0.0 collective-permute-done.mate_ref
  5.7 0.0 copy-start
  5.7 1.6 %copy-done = bf16[16,4,128,128]{3,2,1,0:T(8,128)(2,1)S(1)} copy-done((bf16[16,4,128,128]{3,2,1,0:T(8,128)(2,1)S(1)}, bf16[16,4,128,128]{3,2,1,0:T(8,128)(2,1)}, u32[]{:S(2)}) %copy-start) | copy-done | bytes 2097176
  7.3 0.0 copy-start.1
  7.3 0.7 %copy-done.1 = s32[16,8]{1,0:T(8,128)S(1)} copy-done((s32[16,8]{1,0:T(8,128)S(1)}, s32[16,8]{1,0:T(8,128)}, u32[]{:S(2)}) %copy-start.1) | copy-done | bytes 536
  8.0 7.6 %shard_map.38 = (s16[1040,128]{1,0:T(8,128)(2,1)S(1)}, s16[528,128]{1,0:T(8,128)(2,1)S(1)}, s16[528,128]{1,0:T(8,128)(2,1)S(1)}, s16[528,128]{1,0:T(8,128)(2,1)S...) custom-call(s32[16,8]{1,0:T(8,128)S(1)} %copy-done.1, bf16[16,4,128,128]{3,2,1,0:T(8,128)(2,1)S(1)} %copy-done, ...), custom_call_target="tpu_custom_call" | custom-call | flops 268435456 | bytes 4194304 | tf_op jit(solution)/shard_map/pallas_call | solution.py:187
  15.6 2.6 %collective-permute-start.1 = (s16[1040,128]{1,0:T(8,128)(2,1)S(1)}, s16[1040,128]{1,0:T(8,128)(2,1)S(1)}, u32[]{:S(2)}, u32[]{:S(2)}) collective-permute-start(s16[1040,128]{1,0:T(8,128)(2,1)S(1)} %get-tuple-element.18), channel_id=1, source_target_pairs={{0,2},{1,3},{2,0},{3,1},{4,6},{5,7},{6,4},{7,5},{8,10},{9,11},{10,... | collective-permute-start | bytes 798728 | tf_op jit(solution)/shard_map/ppermute | solution.py:206
  18.2 1.6 %collective-permute-start.5 = (s16[528,128]{1,0:T(8,128)(2,1)S(1)}, s16[528,128]{1,0:T(8,128)(2,1)S(1)}, u32[]{:S(2)}, u32[]{:S(2)}) collective-permute-start(s16[528,128]{1,0:T(8,128)(2,1)S(1)} %get-tuple-element.24), channel_id=1, source_target_pairs={{0,4},{4,0},{8,12},{12,8},{1,5},{5,1},{9,13},{13,9},{2,6},{6,2},{1... | collective-permute-start | bytes 405512 | tf_op jit(solution)/shard_map/ppermute | solution.py:206
  19.7 2.6 %collective-permute-start.6 = (s16[528,128]{1,0:T(8,128)(2,1)S(1)}, s16[528,128]{1,0:T(8,128)(2,1)S(1)}, u32[]{:S(2)}, u32[]{:S(2)}) collective-permute-start(s16[528,128]{1,0:T(8,128)(2,1)S(1)} %get-tuple-element.25), channel_id=1, source_target_pairs={{0,8},{4,12},{8,0},{12,4},{1,9},{5,13},{9,1},{13,5},{2,10},{6,14},... | collective-permute-start | bytes 405512 | tf_op jit(solution)/shard_map/ppermute | solution.py:206
  22.3 0.2 collective-permute-start.7
  22.5 3.5 %collective-permute-done.5.z1_ref = s16[528,128]{1,0:T(8,128)(2,1)S(1)} collective-permute-done((s16[528,128]{1,0:T(8,128)(2,1)S(1)}, s16[528,128]{1,0:T(8,128)(2,1)S(1)}, u32[]{:S(2)}, u32[]{:S(2)}) %collective-permute-start.5) | collective-permute-done | bytes 135200 | tf_op jit(solution)/shard_map/ppermute | solution.py:206
  26.0 6.9 %collective-permute-done.6.z2_ref = s16[528,128]{1,0:T(8,128)(2,1)S(1)} collective-permute-done((s16[528,128]{1,0:T(8,128)(2,1)S(1)}, s16[528,128]{1,0:T(8,128)(2,1)S(1)}, u32[]{:S(2)}, u32[]{:S(2)}) %collective-permute-start.6) | collective-permute-done | bytes 135200 | tf_op jit(solution)/shard_map/ppermute | solution.py:206
  32.9 0.0 collective-permute-done.7.z3_ref
  32.9 0.2 shard_map.40
  33.1 0.6 %collective-permute-start.8 = (s16[272,128]{1,0:T(8,128)(2,1)S(1)}, s16[272,128]{1,0:T(8,128)(2,1)S(1)}, u32[]{:S(2)}, u32[]{:S(2)}) collective-permute-start(s16[272,128]{1,0:T(8,128)(2,1)S(1)} %get-tuple-element.28), channel_id=1, source_target_pairs={{0,2},{1,3},{2,0},{3,1},{4,6},{5,7},{6,4},{7,5},{8,10},{9,11},{10,... | collective-permute-start | bytes 208904 | tf_op jit(solution)/shard_map/ppermute | solution.py:206
  33.6 0.0 collective-permute-done.1.x_ref
  33.6 0.2 shard_map.39
  33.8 2.6 %collective-permute-start.2 = (s16[272,128]{1,0:T(8,128)(2,1)S(1)}, s16[272,128]{1,0:T(8,128)(2,1)S(1)}, u32[]{:S(2)}, u32[]{:S(2)}) collective-permute-start(s16[272,128]{1,0:T(8,128)(2,1)S(1)} %get-tuple-element.20), channel_id=1, source_target_pairs={{0,4},{4,0},{8,12},{12,8},{1,5},{5,1},{9,13},{13,9},{2,6},{6,2},{1... | collective-permute-start | bytes 208904 | tf_op jit(solution)/shard_map/ppermute | solution.py:206
  36.4 1.1 %collective-permute-start.3 = (s16[272,128]{1,0:T(8,128)(2,1)S(1)}, s16[272,128]{1,0:T(8,128)(2,1)S(1)}, u32[]{:S(2)}, u32[]{:S(2)}) collective-permute-start(s16[272,128]{1,0:T(8,128)(2,1)S(1)} %get-tuple-element.21), channel_id=1, source_target_pairs={{0,8},{4,12},{8,0},{12,4},{1,9},{5,13},{9,1},{13,5},{2,10},{6,14},... | collective-permute-start | bytes 208904 | tf_op jit(solution)/shard_map/ppermute | solution.py:206
  37.5 1.4 %collective-permute-start.4 = (s16[272,128]{1,0:T(8,128)(2,1)S(1)}, s16[272,128]{1,0:T(8,128)(2,1)S(1)}, u32[]{:S(2)}, u32[]{:S(2)}) collective-permute-start(s16[272,128]{1,0:T(8,128)(2,1)S(1)} %get-tuple-element.22), channel_id=1, source_target_pairs={{0,12},{4,8},{8,4},{12,0},{1,13},{5,9},{9,5},{13,1},{2,14},{6,10},... | collective-permute-start | bytes 208904 | tf_op jit(solution)/shard_map/ppermute | solution.py:206
  38.9 0.0 collective-permute-done.8.x_ref
  38.9 0.5 %collective-permute-done.2.z1_ref = s16[272,128]{1,0:T(8,128)(2,1)S(1)} collective-permute-done((s16[272,128]{1,0:T(8,128)(2,1)S(1)}, s16[272,128]{1,0:T(8,128)(2,1)S(1)}, u32[]{:S(2)}, u32[]{:S(2)}) %collective-permute-start.2) | collective-permute-done | bytes 69664 | tf_op jit(solution)/shard_map/ppermute | solution.py:206
  39.4 4.3 %collective-permute-done.3.z2_ref = s16[272,128]{1,0:T(8,128)(2,1)S(1)} collective-permute-done((s16[272,128]{1,0:T(8,128)(2,1)S(1)}, s16[272,128]{1,0:T(8,128)(2,1)S(1)}, u32[]{:S(2)}, u32[]{:S(2)}) %collective-permute-start.3) | collective-permute-done | bytes 69664 | tf_op jit(solution)/shard_map/ppermute | solution.py:206
  43.7 0.0 collective-permute-done.4.z3_ref
  43.7 0.8 %shard_map.41 = f32[1,512,128]{2,1,0:T(8,128)} custom-call(f32[2,128,128]{2,1,0:T(8,128)S(1)} %get-tuple-element.19.own_p, s16[272,128]{1,0:T(8,128)(2,1)S(1)} %collective-permute-done.2.z1_ref, s16[272,128]{1,0:T(8,128)(2,1)S(1)} %collective-permute-done.3.z2_ref, s16[272,128]{1,0:T(8,128)(2,1)S(1)} %collective-permute-done.4.z3_ref, ...), custom_call_target="tpu_custom_call" | custom-call | bytes 1048576 | tf_op jit(solution)/shard_map/pallas_call | solution.py:187
Async XLA Ops:
  0.0 5.7 %collective-permute-start = (bf16[16,4,128,128]{3,2,1,0:T(8,128)(2,1)}, bf16[16,4,128,128]{3,2,1,0:T(8,128)(2,1)S(1)}, u32[]{:S(2)}, u32[]{:S(2)}) collective-permute-start(bf16[16,4,128,128]{3,2,1,0:T(8,128)(2,1)} %own_ref.1), channel_id=1, source_target_pairs={{0,1},{1,0},{2,3},{3,2},{4,5},{5,4},{6,7},{7,6},{8,9},{9,8},{10,11... | collective-permute-start | bytes 6291464 | tf_op jit(solution)/shard_map/ppermute | solution.py:206
  5.7 1.6 %copy-start = (bf16[16,4,128,128]{3,2,1,0:T(8,128)(2,1)S(1)}, bf16[16,4,128,128]{3,2,1,0:T(8,128)(2,1)}, u32[]{:S(2)}) copy-start(bf16[16,4,128,128]{3,2,1,0:T(8,128)(2,1)} %own_ref.1) | copy-start | bytes 6291460
  7.3 0.7 %copy-start.1 = (s32[16,8]{1,0:T(8,128)S(1)}, s32[16,8]{1,0:T(8,128)}, u32[]{:S(2)}) copy-start(s32[16,8]{1,0:T(8,128)} %shard_map.37.plan_ref) | copy-start | bytes 1540
  15.6 18.0 %collective-permute-start.1 = (s16[1040,128]{1,0:T(8,128)(2,1)S(1)}, s16[1040,128]{1,0:T(8,128)(2,1)S(1)}, u32[]{:S(2)}, u32[]{:S(2)}) collective-permute-start(s16[1040,128]{1,0:T(8,128)(2,1)S(1)} %get-tuple-element.18), channel_id=1, source_target_pairs={{0,2},{1,3},{2,0},{3,1},{4,6},{5,7},{6,4},{7,5},{8,10},{9,11},{10,... | collective-permute-start | bytes 798728 | tf_op jit(solution)/shard_map/ppermute | solution.py:206
  18.2 7.9 %collective-permute-start.5 = (s16[528,128]{1,0:T(8,128)(2,1)S(1)}, s16[528,128]{1,0:T(8,128)(2,1)S(1)}, u32[]{:S(2)}, u32[]{:S(2)}) collective-permute-start(s16[528,128]{1,0:T(8,128)(2,1)S(1)} %get-tuple-element.24), channel_id=1, source_target_pairs={{0,4},{4,0},{8,12},{12,8},{1,5},{5,1},{9,13},{13,9},{2,6},{6,2},{1... | collective-permute-start | bytes 405512 | tf_op jit(solution)/shard_map/ppermute | solution.py:206
  19.7 13.2 %collective-permute-start.6 = (s16[528,128]{1,0:T(8,128)(2,1)S(1)}, s16[528,128]{1,0:T(8,128)(2,1)S(1)}, u32[]{:S(2)}, u32[]{:S(2)}) collective-permute-start(s16[528,128]{1,0:T(8,128)(2,1)S(1)} %get-tuple-element.25), channel_id=1, source_target_pairs={{0,8},{4,12},{8,0},{12,4},{1,9},{5,13},{9,1},{13,5},{2,10},{6,14},... | collective-permute-start | bytes 405512 | tf_op jit(solution)/shard_map/ppermute | solution.py:206
  22.3 10.6 %collective-permute-start.7 = (s16[528,128]{1,0:T(8,128)(2,1)S(1)}, s16[528,128]{1,0:T(8,128)(2,1)S(1)}, u32[]{:S(2)}, u32[]{:S(2)}) collective-permute-start(s16[528,128]{1,0:T(8,128)(2,1)S(1)} %get-tuple-element.26), channel_id=1, source_target_pairs={{0,12},{4,8},{8,4},{12,0},{1,13},{5,9},{9,5},{13,1},{2,14},{6,10},... | collective-permute-start | bytes 405512 | tf_op jit(solution)/shard_map/ppermute | solution.py:206
  33.1 5.8 %collective-permute-start.8 = (s16[272,128]{1,0:T(8,128)(2,1)S(1)}, s16[272,128]{1,0:T(8,128)(2,1)S(1)}, u32[]{:S(2)}, u32[]{:S(2)}) collective-permute-start(s16[272,128]{1,0:T(8,128)(2,1)S(1)} %get-tuple-element.28), channel_id=1, source_target_pairs={{0,2},{1,3},{2,0},{3,1},{4,6},{5,7},{6,4},{7,5},{8,10},{9,11},{10,... | collective-permute-start | bytes 208904 | tf_op jit(solution)/shard_map/ppermute | solution.py:206
  33.8 5.5 %collective-permute-start.2 = (s16[272,128]{1,0:T(8,128)(2,1)S(1)}, s16[272,128]{1,0:T(8,128)(2,1)S(1)}, u32[]{:S(2)}, u32[]{:S(2)}) collective-permute-start(s16[272,128]{1,0:T(8,128)(2,1)S(1)} %get-tuple-element.20), channel_id=1, source_target_pairs={{0,4},{4,0},{8,12},{12,8},{1,5},{5,1},{9,13},{13,9},{2,6},{6,2},{1... | collective-permute-start | bytes 208904 | tf_op jit(solution)/shard_map/ppermute | solution.py:206
  36.4 7.3 %collective-permute-start.3 = (s16[272,128]{1,0:T(8,128)(2,1)S(1)}, s16[272,128]{1,0:T(8,128)(2,1)S(1)}, u32[]{:S(2)}, u32[]{:S(2)}) collective-permute-start(s16[272,128]{1,0:T(8,128)(2,1)S(1)} %get-tuple-element.21), channel_id=1, source_target_pairs={{0,8},{4,12},{8,0},{12,4},{1,9},{5,13},{9,1},{13,5},{2,10},{6,14},... | collective-permute-start | bytes 208904 | tf_op jit(solution)/shard_map/ppermute | solution.py:206
  37.5 6.2 %collective-permute-start.4 = (s16[272,128]{1,0:T(8,128)(2,1)S(1)}, s16[272,128]{1,0:T(8,128)(2,1)S(1)}, u32[]{:S(2)}, u32[]{:S(2)}) collective-permute-start(s16[272,128]{1,0:T(8,128)(2,1)S(1)} %get-tuple-element.22), channel_id=1, source_target_pairs={{0,12},{4,8},{8,4},{12,0},{1,13},{5,9},{9,5},{13,1},{2,14},{6,10},... | collective-permute-start | bytes 208904 | tf_op jit(solution)/shard_map/ppermute | solution.py:206
where the time goes:
time: 44.8 us; the launch traced here: 44.5 us
  waiting for transfers between devices  15.2 us (34%)
  starting transfers between devices  13 us (29%)
  Pallas kernels  12.6 us (28%)
  local copies, waits for them, and re-layouts  3.67 us (8%)
    ppermute x9, waiting for transfers between devices, swap(): lax.ppermute(value, axis, [(i, i ^ apart) for i in range(lax.axis_size(ax...  15.2 us
    ppermute x9, starting transfers between devices, swap(): lax.ppermute(value, axis, [(i, i ^ apart) for i in range(lax.axis_size(ax...  13 us
    pallas_call x4, Pallas kernels, call(): pl.pallas_call(kernel, out_shape=outs, in_specs=specs, out_specs=jax.tree...  8.77 us
    pallas_call x1, Pallas kernels, on_device(): pl.pallas_call(functools.partial(plan_kernel, panels_here), out_shape=jax...  3.8 us
    unnamed x5, local copies, waits for them, and re-layouts  3.67 us
  transfers between devices with their start and end apart: 9, of which 4 were waited for; matrix products, arithmetic and copies ran while one was open for 3% of the time, Pallas kernels for 9%

commit v1 on v0

v1 whole, which is shorter than its diff:
```python
import jax
import jax.numpy as jnp
from jax import lax
from jax.experimental import pallas as pl
from jax.experimental.pallas import tpu as pltpu
from jax.sharding import PartitionSpec as P

NB = 512
SPAN = 8
STRIP = 2 * SPAN
EXTRA = 16

VMEM = pl.BlockSpec(memory_space=pltpu.VMEM)
SMEM = pl.BlockSpec(memory_space=pltpu.SMEM)
HBM = pl.BlockSpec(memory_space=pltpu.HBM)
PARAMS = pltpu.CompilerParams(vmem_limit_bytes=32 * 1024 * 1024)


def encode(block):
    top = jnp.max(jnp.abs(block), axis=0, keepdims=True)
    power = jnp.ceil(jnp.log2(jnp.maximum(top, 1e-30)))
    scaled = jnp.round(block * jnp.exp2(15.0 - power))
    codes = jnp.clip(scaled, -32767.0, 32767.0).astype(jnp.int32).astype(jnp.int16)
    return codes, power


def pack(blocks, message_ref, power_ref):
    size = blocks[0].shape[0]
    power_ref[...] = jnp.zeros_like(power_ref)
    for at, block in enumerate(blocks):
        codes, power = encode(block)
        message_ref[at * size : (at + 1) * size, :] = codes
        power_ref[at : at + 1, :] = power
    message_ref[len(blocks) * size :, :] = power_ref[...].astype(jnp.int32).astype(jnp.int16)


def powers_of(message_ref):
    rows = message_ref.shape[0]
    power = message_ref[rows - EXTRA :, :].astype(jnp.int32).astype(jnp.float32)
    return jnp.exp2(power - 15.0)


def unpack(message_ref, scales, at, size):
    codes = message_ref[at * size : (at + 1) * size, :].astype(jnp.int32).astype(jnp.float32)
    return codes * scales[at : at + 1, :]


def plan_of(cols_ref, low_ref, fields_ref, quota):
    here = lax.axis_index("tile")
    cols = cols_ref[...]
    count = cols.shape[1]
    folded = jnp.minimum(cols, NB - 1 - cols)
    near = (folded == low_ref[here]).astype(jnp.int32)
    far = (folded == low_ref[here ^ 2]).astype(jnp.int32)
    hit = near + far
    target = jnp.sum(hit * cols, axis=0, keepdims=True)
    slot = jnp.sum(hit * lax.broadcasted_iota(jnp.int32, cols.shape, 0), axis=0, keepdims=True)
    local = jnp.sum(near, axis=0, keepdims=True)
    wanted = jnp.sum(hit, axis=0, keepdims=True)
    place = cols - target + SPAN - 1
    good = (cols >= 0) & (place >= 0) & (place < SPAN)
    place = jnp.where(good, place + jnp.where(target >= NB // 2, SPAN, 0), STRIP)
    panel = lax.broadcasted_iota(jnp.int32, (1, count), 1)
    device = panel // (4 * quota)
    mate = (device == (here ^ 1)).astype(jnp.int32)
    wanted = (wanted > 0) & ((device == here) | (mate > 0))
    group = jnp.where(wanted, local * 2 + mate, -1)
    members = (lax.broadcasted_iota(jnp.int32, (8, count), 0) == group).astype(jnp.float32)
    before = (
        lax.broadcasted_iota(jnp.int32, (count, count), 0) < lax.broadcasted_iota(jnp.int32, (count, count), 1)
    ).astype(jnp.float32)
    ranks = jnp.dot(members, before, preferred_element_type=jnp.float32)
    rank = jnp.sum(members * ranks, axis=0, keepdims=True).astype(jnp.int32)
    entry = jnp.where(wanted, group * quota + rank, -1)
    chosen = (lax.broadcasted_iota(jnp.int32, (4 * quota, count), 0) == entry).astype(jnp.float32)
    fields_ref[...] = jnp.zeros_like(fields_ref)
    fields_ref[0:1, 0:count] = (panel % (4 * quota)).astype(jnp.float32)
    fields_ref[1:2, 0:count] = slot.astype(jnp.float32)
    fields_ref[2:6, 0:count] = place.astype(jnp.float32)
    table = lax.dot_general(
        chosen, fields_ref[:, 0:count], (((1,), (1,)), ((), ())), preferred_element_type=jnp.float32
    )
    return table.astype(jnp.int32)


def add_products(plan_ref, entry, panels_ref, sums_ref):
    panel = plan_ref[entry, 0]
    column = panels_ref[panel, plan_ref[entry, 1]].T
    size = column.shape[0]
    wide = jnp.concatenate([panels_ref[panel, slot] for slot in range(4)], axis=1)
    made = jnp.dot(column, wide, preferred_element_type=jnp.float32)
    for slot in range(4):
        sums_ref[plan_ref[entry, 2 + slot]] += made[:, slot * size : (slot + 1) * size]


def near_kernel(cols_hbm, low_hbm, blocks_ref, plan_ref, far_ref, own_ref, held, cols_ref, low_ref, fields, table, sems):
    quota = blocks_ref.shape[0] // 4
    cols_copy = pltpu.make_async_copy(cols_hbm, cols_ref, sems.at[0])
    low_copy = pltpu.make_async_copy(low_hbm, low_ref, sems.at[1])
    held_copy = pltpu.make_async_copy(blocks_ref, held, sems.at[2])
    cols_copy.start()
    low_copy.start()
    held_copy.start()
    far_ref[...] = jnp.zeros_like(far_ref)
    own_ref[...] = jnp.zeros_like(own_ref)
    low_copy.wait()
    cols_copy.wait()
    table[:, 0:8] = plan_of(cols_ref, low_ref, fields, quota)
    plan_copy = pltpu.make_async_copy(table, plan_ref, sems.at[3])
    plan_copy.start()
    plan_copy.wait()
    held_copy.wait()
    for at in range(quota):
        add_products(plan_ref, at, held, far_ref)
        add_products(plan_ref, 2 * quota + at, held, own_ref)


def add_mate(plan_ref, mate_ref, far_ref, own_ref):
    quota = mate_ref.shape[0] // 4
    for at in range(quota):
        add_products(plan_ref, quota + at, mate_ref, far_ref)
        add_products(plan_ref, 3 * quota + at, mate_ref, own_ref)


def split_kernel(plan_ref, mate_ref, far_in, own_in, z2_ref, z3_ref, z1_ref, x_ref, far_ref, own_ref, power):
    add_mate(plan_ref, mate_ref, far_ref, own_ref)
    here = lax.axis_index("row")
    for apart, z_ref in ((1, z1_ref), (2, z2_ref), (3, z3_ref)):
        first = 4 * (here ^ apart) + 2
        pack([far_ref[first], far_ref[first + 1], own_ref[first], own_ref[first + 1]], z_ref, power)
    pack([far_ref[4 * owner + i] for owner in range(4) for i in range(2)], x_ref, power)


def after_x_kernel(own_ref, x_ref, z2_ref, z3_ref, z1_ref, keep_ref, sums, power):
    here = lax.axis_index("row")
    size = own_ref.shape[1]
    scales = powers_of(x_ref)
    for owner in range(4):
        for i in range(2):
            at = 2 * owner + i
            sums[at] = own_ref[4 * owner + i] + unpack(x_ref, scales, at, size)
    for apart, z_ref in ((1, z1_ref), (2, z2_ref), (3, z3_ref)):
        first = 2 * (here ^ apart)
        pack([sums[first], sums[first + 1]], z_ref, power)
    for i in range(2):
        keep_ref[i] = sums[2 * here + i]


def after_z_kernel(after_ref, far_ref, own_ref, z2_ref, z3_ref, z1_ref, x_ref, keep_ref, power):
    here = lax.axis_index("row")
    size = own_ref.shape[1]
    scales = [powers_of(ref) for ref in (z1_ref, z2_ref, z3_ref)]
    totals = []
    for at in range(4):
        sums_ref = far_ref if at < 2 else own_ref
        total = sums_ref[4 * here + 2 + at % 2]
        for ref, scale in zip((z1_ref, z2_ref, z3_ref), scales):
            total = total + unpack(ref, scale, at, size)
        totals.append(total)
    pack(totals[:2], x_ref, power)
    keep_ref[0] = totals[2]
    keep_ref[1] = totals[3]


def last_kernel(own_p, z2_ref, z3_ref, z1_ref, own_q, x_ref, out_ref):
    size = own_p.shape[1]
    odd = lax.axis_index("row") % 2
    scales = [powers_of(ref) for ref in (z1_ref, z2_ref, z3_ref)]
    for at in range(2):
        total = own_p[at]
        for ref, scale in zip((z1_ref, z2_ref, z3_ref), scales):
            total = total + unpack(ref, scale, at, size)
        out_ref[0, at * size : (at + 1) * size, :] = total
    scale = powers_of(x_ref)
    for at in range(2):
        total = own_q[at] + unpack(x_ref, scale, at, size)
        if at == 1:
            rows = lax.broadcasted_iota(jnp.int32, total.shape, 0)
            columns = lax.broadcasted_iota(jnp.int32, total.shape, 1)
            total = total + jnp.where((rows == columns) & (odd == 1), 1.0, 0.0)
        out_ref[0, (2 + at) * size : (3 + at) * size, :] = total


def full_kernel(plan_ref, mate_ref, far_in, own_in, x_ref, far_ref, own_ref, power):
    add_mate(plan_ref, mate_ref, far_ref, own_ref)
    pack([far_ref[at] for at in range(STRIP)], x_ref, power)


def add_kernel(own_ref, x_ref, sum_ref):
    size = own_ref.shape[1]
    scales = powers_of(x_ref)
    for at in range(STRIP):
        sum_ref[at] = own_ref[at] + unpack(x_ref, scales, at, size)


def call(kernel, outs, operands, specs, out_specs=None, scratch=(), size=1 << 20, aliases=None):
    return pl.pallas_call(
        kernel,
        out_shape=outs,
        in_specs=specs,
        out_specs=jax.tree.map(lambda _: VMEM, outs) if out_specs is None else out_specs,
        scratch_shapes=list(scratch),
        input_output_aliases=aliases or {},
        compiler_params=PARAMS,
        cost_estimate=pl.CostEstimate(flops=0, bytes_accessed=size, transcendentals=0),
    )(*operands)


def on_device(blocks, block_cols, pair_low):
    panels_here, slots, size, _ = blocks.shape
    tiles_count = lax.axis_size("tile")
    rows_count = lax.axis_size("row")
    assert tiles_count == 4 and pair_low.shape[0] == 4 and slots == 4

    def swap(value, axis, apart):
        return lax.ppermute(value, axis, [(i, i ^ apart) for i in range(lax.axis_size(axis))])

    def message(count):
        return jax.ShapeDtypeStruct((count * size + EXTRA, size), jnp.int16)

    def full(count):
        return jax.ShapeDtypeStruct((count, size, size), jnp.float32)

    power = pltpu.VMEM((EXTRA, size), jnp.float32)
    mate = swap(blocks, "tile", 1)
    plan, far, own = call(
        near_kernel,
        [jax.ShapeDtypeStruct((panels_here, 128), jnp.int32), full(STRIP + 1), full(STRIP + 1)],
        tuple(pltpu.with_memory_space_constraint(value, pltpu.HBM) for value in (block_cols.T, pair_low, blocks)),
        [HBM, HBM, HBM],
        [SMEM, VMEM, VMEM],
        [
            pltpu.VMEM(blocks.shape, blocks.dtype),
            pltpu.VMEM(block_cols.shape[::-1], jnp.int32),
            pltpu.SMEM(pair_low.shape, jnp.int32),
            pltpu.VMEM((8, 128), jnp.float32),
            pltpu.VMEM((panels_here, 128), jnp.int32),
            pltpu.SemaphoreType.DMA((4,)),
        ],
        8 << 20,
    )
    operands = (plan, mate, far, own)
    specs = [SMEM, VMEM, VMEM, VMEM]

    if rows_count != 4:
        across, far, own = call(
            full_kernel, [message(STRIP), far, own], operands, specs, scratch=[power], aliases={2: 1, 3: 2}
        )
        strip = call(add_kernel, full(STRIP), (own, swap(across, "tile", 2)), [VMEM, VMEM])
        share = lax.psum_scatter(strip.reshape(1, STRIP * size, size), "row", scatter_dimension=1, tiled=True)
        rows = lax.axis_index("row") * share.shape[1] + jnp.arange(share.shape[1], dtype=jnp.int32)
        unit = (rows // size % SPAN == SPAN - 1)[:, None] & ((rows % size)[:, None] == jnp.arange(size)[None, :])
        return share + unit.astype(jnp.float32)[None]

    q2, q3, q1, x_p, far, own = call(
        split_kernel,
        [message(4), message(4), message(4), message(8), full(STRIP + 1), full(STRIP + 1)],
        operands, specs, scratch=[power], aliases={2: 4, 3: 5},
    )
    q2 = swap(q2, "row", 2)
    q3 = swap(q3, "row", 3)
    q1 = swap(q1, "row", 1)
    x_p = swap(x_p, "tile", 2)
    p2, p3, p1, own_p = call(
        after_x_kernel, [message(2)] * 3 + [full(2)], (own, x_p), [VMEM] * 2, scratch=[pltpu.VMEM((8, size, size), jnp.float32), power]
    )
    p2 = swap(p2, "row", 2)
    p3 = swap(p3, "row", 3)
    p1 = swap(p1, "row", 1)
    x_q, own_q = call(after_z_kernel, [message(2), full(2)], (own_p, far, own, q2, q3, q1), [pl.BlockSpec(memory_space=pl.ANY)] + [VMEM] * 5, scratch=[power])
    x_q = swap(x_q, "tile", 2)
    return call(
        last_kernel, jax.ShapeDtypeStruct((1, 4 * size, size), jnp.float32), (own_p, p2, p3, p1, own_q, x_q), [VMEM] * 6
    )


def solution(mesh):
    return jax.shard_map(
        on_device,
        mesh=mesh,
        in_specs=(
            P(("groups", "row", "tile"), None, None, None),
            P(("groups", "row"), None),
            P("groups"),
        ),
        out_specs=P(("groups", "tile"), "row", None),
        check_vma=False,
    )
```

time: 44.8 us -> 30.9 us (0.69)
  the two profiles are of different devices: /device:TPU:0 before, /device:TPU:16 now
where the time goes in v1:
time: 30.9 us; the launch traced here: 30.8 us
  starting transfers between devices  13.9 us (45%)
  waiting for transfers between devices  11.4 us (37%)
  Pallas kernels  5.37 us (17%)
    ppermute x9, starting transfers between devices, swap(): lax.ppermute(value, axis, [(i, i ^ apart) for i in range(lax.axis_size(ax...  13.9 us
    ppermute x9, waiting for transfers between devices, swap(): lax.ppermute(value, axis, [(i, i ^ apart) for i in range(lax.axis_size(ax...  11.4 us
    pallas_call x5, Pallas kernels, call(): pl.pallas_call(kernel, out_shape=outs, in_specs=specs, out_specs=jax.tree...  5.37 us
  transfers between devices with their start and end apart: 9, of which 6 were waited for; matrix products, arithmetic and copies ran while one was open for 0% of the time, Pallas kernels for 10%

profile of v1, /device:TPU:16, one launch (start us, length us, event | category | flops | bytes accessed | tf_op | source)
XLA Modules:
  0.0 30.8 jit_solution(12279677110993492130)
XLA Ops:
  0.0 0.0 collective-permute-start
  0.0 2.8 %shard_map.37 = (s32[16,128]{1,0:T(8,128)S(1)}, f32[17,128,128]{2,1,0:T(8,128)S(1)}, f32[17,128,128]{2,1,0:T(8,128)S(1)}) custom-call(s32[4,64]{1,0:T(4,128)} %bitcast.1, s32[4]{0:T(128)} %low_hbm.1, bf16[16,4,128,128]{3,2,1,0:T(8,128)(2,1)} %blocks_ref.1), custom_call_target="tpu_custom_call" | custom-call | bytes 8388608 | tf_op jit(solution)/shard_map/pallas_call | solution.py:197
  2.8 1.5 %collective-permute-done.mate_ref = bf16[16,4,128,128]{3,2,1,0:T(8,128)(2,1)S(1)} collective-permute-done((bf16[16,4,128,128]{3,2,1,0:T(8,128)(2,1)}, bf16[16,4,128,128]{3,2,1,0:T(8,128)(2,1)S(1)}, u32[]{:S(2)}, u32[]{:S(2)}) %collective-permute-start) | collective-permute-done | bytes 2097184 | tf_op jit(solution)/shard_map/ppermute | solution.py:216
  4.4 1.4 %shard_map.38 = (s16[528,128]{1,0:T(8,128)(2,1)S(1)}, s16[528,128]{1,0:T(8,128)(2,1)S(1)}, s16[528,128]{1,0:T(8,128)(2,1)S(1)}, s16[1040,128]{1,0:T(8,128)(2,1)S...) custom-call(s32[16,128]{1,0:T(8,128)S(1)} %get-tuple-element.20.plan_, ...), custom_call_target="tpu_custom_call", output_to_operand_aliasing={{4}: (2, {}), {5}: (3, {})} | custom-call | bytes 1048576 | tf_op jit(solution)/shard_map/pallas_call | solution.py:197
  5.8 1.5 %collective-permute-start.1 = (s16[1040,128]{1,0:T(8,128)(2,1)S(1)}, s16[1040,128]{1,0:T(8,128)(2,1)S(1)}, u32[]{:S(2)}, u32[]{:S(2)}) collective-permute-start(s16[1040,128]{1,0:T(8,128)(2,1)S(1)} %get-tuple-element.24), channel_id=1, source_target_pairs={{0,2},{1,3},{2,0},{3,1},{4,6},{5,7},{6,4},{7,5},{8,10},{9,11},{10,... | collective-permute-start | bytes 798728 | tf_op jit(solution)/shard_map/ppermute | solution.py:216
  7.3 0.3 %collective-permute-start.5 = (s16[528,128]{1,0:T(8,128)(2,1)S(1)}, s16[528,128]{1,0:T(8,128)(2,1)S(1)}, u32[]{:S(2)}, u32[]{:S(2)}) collective-permute-start(s16[528,128]{1,0:T(8,128)(2,1)S(1)} %get-tuple-element.30), channel_id=1, source_target_pairs={{0,8},{4,12},{8,0},{12,4},{1,9},{5,13},{9,1},{13,5},{2,10},{6,14},... | collective-permute-start | bytes 405512 | tf_op jit(solution)/shard_map/ppermute | solution.py:216
  7.7 2.7 %collective-permute-start.6 = (s16[528,128]{1,0:T(8,128)(2,1)S(1)}, s16[528,128]{1,0:T(8,128)(2,1)S(1)}, u32[]{:S(2)}, u32[]{:S(2)}) collective-permute-start(s16[528,128]{1,0:T(8,128)(2,1)S(1)} %get-tuple-element.31), channel_id=1, source_target_pairs={{0,12},{4,8},{8,4},{12,0},{1,13},{5,9},{9,5},{13,1},{2,14},{6,10},... | collective-permute-start | bytes 405512 | tf_op jit(solution)/shard_map/ppermute | solution.py:216
  10.4 1.4 %collective-permute-start.7 = (s16[528,128]{1,0:T(8,128)(2,1)S(1)}, s16[528,128]{1,0:T(8,128)(2,1)S(1)}, u32[]{:S(2)}, u32[]{:S(2)}) collective-permute-start(s16[528,128]{1,0:T(8,128)(2,1)S(1)} %get-tuple-element.32), channel_id=1, source_target_pairs={{0,4},{4,0},{8,12},{12,8},{1,5},{5,1},{9,13},{13,9},{2,6},{6,2},{1... | collective-permute-start | bytes 405512 | tf_op jit(solution)/shard_map/ppermute | solution.py:216
  11.7 2.6 %collective-permute-done.1.x_ref = s16[1040,128]{1,0:T(8,128)(2,1)S(1)} collective-permute-done((s16[1040,128]{1,0:T(8,128)(2,1)S(1)}, s16[1040,128]{1,0:T(8,128)(2,1)S(1)}, u32[]{:S(2)}, u32[]{:S(2)}) %collective-permute-start.1) | collective-permute-done | bytes 266272 | tf_op jit(solution)/shard_map/ppermute | solution.py:216
  14.3 0.2 shard_map.39
  14.5 0.2 collective-permute-start.2
  14.6 3.0 %collective-permute-start.3 = (s16[272,128]{1,0:T(8,128)(2,1)S(1)}, s16[272,128]{1,0:T(8,128)(2,1)S(1)}, u32[]{:S(2)}, u32[]{:S(2)}) collective-permute-start(s16[272,128]{1,0:T(8,128)(2,1)S(1)} %get-tuple-element.27), channel_id=1, source_target_pairs={{0,12},{4,8},{8,4},{12,0},{1,13},{5,9},{9,5},{13,1},{2,14},{6,10},... | collective-permute-start | bytes 208904 | tf_op jit(solution)/shard_map/ppermute | solution.py:216
  17.6 0.2 collective-permute-done.5.z2_ref
  17.8 4.3 %collective-permute-start.4 = (s16[272,128]{1,0:T(8,128)(2,1)S(1)}, s16[272,128]{1,0:T(8,128)(2,1)S(1)}, u32[]{:S(2)}, u32[]{:S(2)}) collective-permute-start(s16[272,128]{1,0:T(8,128)(2,1)S(1)} %get-tuple-element.28), channel_id=1, source_target_pairs={{0,4},{4,0},{8,12},{12,8},{1,5},{5,1},{9,13},{13,9},{2,6},{6,2},{1... | collective-permute-start | bytes 208904 | tf_op jit(solution)/shard_map/ppermute | solution.py:216
  22.1 3.3 %collective-permute-done.6.z3_ref = s16[528,128]{1,0:T(8,128)(2,1)S(1)} collective-permute-done((s16[528,128]{1,0:T(8,128)(2,1)S(1)}, s16[528,128]{1,0:T(8,128)(2,1)S(1)}, u32[]{:S(2)}, u32[]{:S(2)}) %collective-permute-start.6) | collective-permute-done | bytes 135200 | tf_op jit(solution)/shard_map/ppermute | solution.py:216
  25.4 0.0 collective-permute-done.7.z1_ref
  25.4 0.2 shard_map.40
  25.6 0.6 %collective-permute-start.8 = (s16[272,128]{1,0:T(8,128)(2,1)S(1)}, s16[272,128]{1,0:T(8,128)(2,1)S(1)}, u32[]{:S(2)}, u32[]{:S(2)}) collective-permute-start(s16[272,128]{1,0:T(8,128)(2,1)S(1)} %get-tuple-element.34), channel_id=1, source_target_pairs={{0,2},{1,3},{2,0},{3,1},{4,6},{5,7},{6,4},{7,5},{8,10},{9,11},{10,... | collective-permute-start | bytes 208904 | tf_op jit(solution)/shard_map/ppermute | solution.py:216
  26.2 0.0 collective-permute-done.2.z2_ref
  26.2 2.1 %collective-permute-done.3.z3_ref = s16[272,128]{1,0:T(8,128)(2,1)S(1)} collective-permute-done((s16[272,128]{1,0:T(8,128)(2,1)S(1)}, s16[272,128]{1,0:T(8,128)(2,1)S(1)}, u32[]{:S(2)}, u32[]{:S(2)}) %collective-permute-start.3) | collective-permute-done | bytes 69664 | tf_op jit(solution)/shard_map/ppermute | solution.py:216
  28.3 0.0 collective-permute-done.4.z1_ref
  28.3 1.6 %collective-permute-done.8.x_ref = s16[272,128]{1,0:T(8,128)(2,1)S(1)} collective-permute-done((s16[272,128]{1,0:T(8,128)(2,1)S(1)}, s16[272,128]{1,0:T(8,128)(2,1)S(1)}, u32[]{:S(2)}, u32[]{:S(2)}) %collective-permute-start.8) | collective-permute-done | bytes 69664 | tf_op jit(solution)/shard_map/ppermute | solution.py:216
  30.0 0.8 %shard_map.41 = f32[1,512,128]{2,1,0:T(8,128)} custom-call(f32[2,128,128]{2,1,0:T(8,128)S(1)} %get-tuple-element.25.after_ref.own_p, s16[272,128]{1,0:T(8,128)(2,1)S(1)} %collective-permute-done.2.z2_ref, s16[272,128]{1,0:T(8,128)(2,1)S(1)} %collective-permute-done.3.z3_ref, s16[272,128]{1,0:T(8,128)(2,1)S(1)} %collective-permute-done.4.z1_ref, ...), custom_call_target="tpu_custom_call" | custom-call | bytes 1048576 | tf_op jit(solution)/shard_map/pallas_call | solution.py:197
Async XLA Ops:
  0.0 4.4 %collective-permute-start = (bf16[16,4,128,128]{3,2,1,0:T(8,128)(2,1)}, bf16[16,4,128,128]{3,2,1,0:T(8,128)(2,1)S(1)}, u32[]{:S(2)}, u32[]{:S(2)}) collective-permute-start(bf16[16,4,128,128]{3,2,1,0:T(8,128)(2,1)} %blocks_ref.1), channel_id=1, source_target_pairs={{0,1},{1,0},{2,3},{3,2},{4,5},{5,4},{6,7},{7,6},{8,9},{9,8},{10,11... | collective-permute-start | bytes 6291464 | tf_op jit(solution)/shard_map/ppermute | solution.py:216
  5.8 8.5 %collective-permute-start.1 = (s16[1040,128]{1,0:T(8,128)(2,1)S(1)}, s16[1040,128]{1,0:T(8,128)(2,1)S(1)}, u32[]{:S(2)}, u32[]{:S(2)}) collective-permute-start(s16[1040,128]{1,0:T(8,128)(2,1)S(1)} %get-tuple-element.24), channel_id=1, source_target_pairs={{0,2},{1,3},{2,0},{3,1},{4,6},{5,7},{6,4},{7,5},{8,10},{9,11},{10,... | collective-permute-start | bytes 798728 | tf_op jit(solution)/shard_map/ppermute | solution.py:216
  7.3 10.5 %collective-permute-start.5 = (s16[528,128]{1,0:T(8,128)(2,1)S(1)}, s16[528,128]{1,0:T(8,128)(2,1)S(1)}, u32[]{:S(2)}, u32[]{:S(2)}) collective-permute-start(s16[528,128]{1,0:T(8,128)(2,1)S(1)} %get-tuple-element.30), channel_id=1, source_target_pairs={{0,8},{4,12},{8,0},{12,4},{1,9},{5,13},{9,1},{13,5},{2,10},{6,14},... | collective-permute-start | bytes 405512 | tf_op jit(solution)/shard_map/ppermute | solution.py:216
  7.7 17.7 %collective-permute-start.6 = (s16[528,128]{1,0:T(8,128)(2,1)S(1)}, s16[528,128]{1,0:T(8,128)(2,1)S(1)}, u32[]{:S(2)}, u32[]{:S(2)}) collective-permute-start(s16[528,128]{1,0:T(8,128)(2,1)S(1)} %get-tuple-element.31), channel_id=1, source_target_pairs={{0,12},{4,8},{8,4},{12,0},{1,13},{5,9},{9,5},{13,1},{2,14},{6,10},... | collective-permute-start | bytes 405512 | tf_op jit(solution)/shard_map/ppermute | solution.py:216
  10.4 15.0 %collective-permute-start.7 = (s16[528,128]{1,0:T(8,128)(2,1)S(1)}, s16[528,128]{1,0:T(8,128)(2,1)S(1)}, u32[]{:S(2)}, u32[]{:S(2)}) collective-permute-start(s16[528,128]{1,0:T(8,128)(2,1)S(1)} %get-tuple-element.32), channel_id=1, source_target_pairs={{0,4},{4,0},{8,12},{12,8},{1,5},{5,1},{9,13},{13,9},{2,6},{6,2},{1... | collective-permute-start | bytes 405512 | tf_op jit(solution)/shard_map/ppermute | solution.py:216
  14.5 11.7 %collective-permute-start.2 = (s16[272,128]{1,0:T(8,128)(2,1)S(1)}, s16[272,128]{1,0:T(8,128)(2,1)S(1)}, u32[]{:S(2)}, u32[]{:S(2)}) collective-permute-start(s16[272,128]{1,0:T(8,128)(2,1)S(1)} %get-tuple-element.26), channel_id=1, source_target_pairs={{0,8},{4,12},{8,0},{12,4},{1,9},{5,13},{9,1},{13,5},{2,10},{6,14},... | collective-permute-start | bytes 208904 | tf_op jit(solution)/shard_map/ppermute | solution.py:216
  14.6 13.7 %collective-permute-start.3 = (s16[272,128]{1,0:T(8,128)(2,1)S(1)}, s16[272,128]{1,0:T(8,128)(2,1)S(1)}, u32[]{:S(2)}, u32[]{:S(2)}) collective-permute-start(s16[272,128]{1,0:T(8,128)(2,1)S(1)} %get-tuple-element.27), channel_id=1, source_target_pairs={{0,12},{4,8},{8,4},{12,0},{1,13},{5,9},{9,5},{13,1},{2,14},{6,10},... | collective-permute-start | bytes 208904 | tf_op jit(solution)/shard_map/ppermute | solution.py:216
  17.8 10.5 %collective-permute-start.4 = (s16[272,128]{1,0:T(8,128)(2,1)S(1)}, s16[272,128]{1,0:T(8,128)(2,1)S(1)}, u32[]{:S(2)}, u32[]{:S(2)}) collective-permute-start(s16[272,128]{1,0:T(8,128)(2,1)S(1)} %get-tuple-element.28), channel_id=1, source_target_pairs={{0,4},{4,0},{8,12},{12,8},{1,5},{5,1},{9,13},{13,9},{2,6},{6,2},{1... | collective-permute-start | bytes 208904 | tf_op jit(solution)/shard_map/ppermute | solution.py:216
  25.6 4.4 %collective-permute-start.8 = (s16[272,128]{1,0:T(8,128)(2,1)S(1)}, s16[272,128]{1,0:T(8,128)(2,1)S(1)}, u32[]{:S(2)}, u32[]{:S(2)}) collective-permute-start(s16[272,128]{1,0:T(8,128)(2,1)S(1)} %get-tuple-element.34), channel_id=1, source_target_pairs={{0,2},{1,3},{2,0},{3,1},{4,6},{5,7},{6,4},{7,5},{8,10},{9,11},{10,... | collective-permute-start | bytes 208904 | tf_op jit(solution)/shard_map/ppermute | solution.py:216

commit v2 on v1

--- a/solution.py
+++ b/solution.py
@@ -1,3 +1,5 @@
+import functools
+
 import jax
 import jax.numpy as jnp
 from jax import lax
@@ -8,41 +10,55 @@
 NB = 512
 SPAN = 8
 STRIP = 2 * SPAN
-EXTRA = 16
+UNIT = 64
+X_FIRST = ((0, 1, 2, 3, 4),)
+Z_FIRST = ((5, 6, 7),)
+
+ORDER = (("x", 0), ("z", 0))
 
 VMEM = pl.BlockSpec(memory_space=pltpu.VMEM)
 SMEM = pl.BlockSpec(memory_space=pltpu.SMEM)
 HBM = pl.BlockSpec(memory_space=pltpu.HBM)
+ANY = pl.BlockSpec(memory_space=pl.ANY)
 PARAMS = pltpu.CompilerParams(vmem_limit_bytes=32 * 1024 * 1024)
 
 
-def encode(block):
-    top = jnp.max(jnp.abs(block), axis=0, keepdims=True)
+def encode(values):
+    top = jnp.max(jnp.abs(values), axis=0, keepdims=True)
     power = jnp.ceil(jnp.log2(jnp.maximum(top, 1e-30)))
-    scaled = jnp.round(block * jnp.exp2(15.0 - power))
+    scaled = jnp.round(values * jnp.exp2(15.0 - power))
     codes = jnp.clip(scaled, -32767.0, 32767.0).astype(jnp.int32).astype(jnp.int16)
     return codes, power
 
 
-def pack(blocks, message_ref, power_ref):
-    size = blocks[0].shape[0]
+def extra_of(count):
+    return -(-count // 16) * 16
+
+
+def pack(units, message_ref, power_ref):
+    extra = extra_of(len(units))
     power_ref[...] = jnp.zeros_like(power_ref)
-    for at, block in enumerate(blocks):
-        codes, power = encode(block)
-        message_ref[at * size : (at + 1) * size, :] = codes
+    for at, values in enumerate(units):
+        codes, power = encode(values)
+        message_ref[at * UNIT : (at + 1) * UNIT, :] = codes
         power_ref[at : at + 1, :] = power
-    message_ref[len(blocks) * size :, :] = power_ref[...].astype(jnp.int32).astype(jnp.int16)
-
-
-def powers_of(message_ref):
-    rows = message_ref.shape[0]
-    power = message_ref[rows - EXTRA :, :].astype(jnp.int32).astype(jnp.float32)
-    return jnp.exp2(power - 15.0)
-
-
-def unpack(message_ref, scales, at, size):
-    codes = message_ref[at * size : (at + 1) * size, :].astype(jnp.int32).astype(jnp.float32)
-    return codes * scales[at : at + 1, :]
+    message_ref[len(units) * UNIT :, :] = power_ref[0:extra, :].astype(jnp.int32).astype(jnp.int16)
+
+
+def unpacker(message_ref):
+    extra = message_ref.shape[0] % UNIT
+    first = message_ref.shape[0] - extra
+    scales = jnp.exp2(message_ref[first:, :].astype(jnp.int32).astype(jnp.float32) - 15.0)
+
+    def unit(at):
+        codes = message_ref[at * UNIT : (at + 1) * UNIT, :].astype(jnp.int32).astype(jnp.float32)
+        return codes * scales[at : at + 1, :]
+
+    return unit
+
+
+def unit_of(sums_ref, owner, unit):
+    return sums_ref[4 * owner + unit // 2, unit % 2 * UNIT : (unit % 2 + 1) * UNIT, :]
 
 
 def plan_of(cols_ref, low_ref, fields_ref, quota):
@@ -122,75 +138,79 @@
         add_products(plan_ref, 3 * quota + at, mate_ref, own_ref)
 
 
-def split_kernel(plan_ref, mate_ref, far_in, own_in, z2_ref, z3_ref, z1_ref, x_ref, far_ref, own_ref, power):
+def split_kernel(plan_ref, mate_ref, far_in, own_in, *refs):
+    refs, (far_ref, own_ref, power) = list(refs[:-3]), refs[-3:]
     add_mate(plan_ref, mate_ref, far_ref, own_ref)
     here = lax.axis_index("row")
-    for apart, z_ref in ((1, z1_ref), (2, z2_ref), (3, z3_ref)):
-        first = 4 * (here ^ apart) + 2
-        pack([far_ref[first], far_ref[first + 1], own_ref[first], own_ref[first + 1]], z_ref, power)
-    pack([far_ref[4 * owner + i] for owner in range(4) for i in range(2)], x_ref, power)
-
-
-def after_x_kernel(own_ref, x_ref, z2_ref, z3_ref, z1_ref, keep_ref, sums, power):
+    for units in X_FIRST:
+        pack([unit_of(far_ref, owner, unit) for owner in range(4) for unit in units], refs.pop(0), power)
+    for units in Z_FIRST:
+        for apart in (2, 3, 1):
+            owner = here ^ apart
+            pack([unit_of(ref, owner, unit) for ref in (far_ref, own_ref) for unit in units], refs.pop(0), power)
+
+
+def after_x_kernel(units, after_ref, x_ref, own_ref, z2_ref, z3_ref, z1_ref, keep_ref, sums, power):
     here = lax.axis_index("row")
-    size = own_ref.shape[1]
-    scales = powers_of(x_ref)
+    received = unpacker(x_ref)
+    count = len(units)
     for owner in range(4):
-        for i in range(2):
-            at = 2 * owner + i
-            sums[at] = own_ref[4 * owner + i] + unpack(x_ref, scales, at, size)
-    for apart, z_ref in ((1, z1_ref), (2, z2_ref), (3, z3_ref)):
-        first = 2 * (here ^ apart)
-        pack([sums[first], sums[first + 1]], z_ref, power)
-    for i in range(2):
-        keep_ref[i] = sums[2 * here + i]
-
-
-def after_z_kernel(after_ref, far_ref, own_ref, z2_ref, z3_ref, z1_ref, x_ref, keep_ref, power):
+        for at, unit in enumerate(units):
+            sums[owner * count + at] = unit_of(own_ref, owner, unit) + received(owner * count + at)
+    for apart, z_ref in ((2, z2_ref), (3, z3_ref), (1, z1_ref)):
+        first = (here ^ apart) * count
+        pack([sums[first + at] for at in range(count)], z_ref, power)
+    for at in range(count):
+        keep_ref[at] = sums[here * count + at]
+
+
+def after_z_kernel(units, after_ref, z2_ref, z3_ref, z1_ref, far_ref, own_ref, x_ref, keep_ref, power):
     here = lax.axis_index("row")
-    size = own_ref.shape[1]
-    scales = [powers_of(ref) for ref in (z1_ref, z2_ref, z3_ref)]
+    received = [unpacker(ref) for ref in (z2_ref, z3_ref, z1_ref)]
+    count = len(units)
     totals = []
-    for at in range(4):
-        sums_ref = far_ref if at < 2 else own_ref
-        total = sums_ref[4 * here + 2 + at % 2]
-        for ref, scale in zip((z1_ref, z2_ref, z3_ref), scales):
-            total = total + unpack(ref, scale, at, size)
-        totals.append(total)
-    pack(totals[:2], x_ref, power)
-    keep_ref[0] = totals[2]
-    keep_ref[1] = totals[3]
-
-
-def last_kernel(own_p, z2_ref, z3_ref, z1_ref, own_q, x_ref, out_ref):
-    size = own_p.shape[1]
+    for side, sums_ref in enumerate((far_ref, own_ref)):
+        for at, unit in enumerate(units):
+            total = unit_of(sums_ref, here, unit)
+            for part in received:
+                total = total + part(side * count + at)
+            totals.append(total)
+    pack(totals[:count], x_ref, power)
+    for at in range(count):
+        keep_ref[at] = totals[count + at]
+
+
+def last_kernel(*refs):
+    refs, out_ref = list(refs[:-1]), refs[-1]
     odd = lax.axis_index("row") % 2
-    scales = [powers_of(ref) for ref in (z1_ref, z2_ref, z3_ref)]
-    for at in range(2):
-        total = own_p[at]
-        for ref, scale in zip((z1_ref, z2_ref, z3_ref), scales):
-            total = total + unpack(ref, scale, at, size)
-        out_ref[0, at * size : (at + 1) * size, :] = total
-    scale = powers_of(x_ref)
-    for at in range(2):
-        total = own_q[at] + unpack(x_ref, scale, at, size)
-        if at == 1:
-            rows = lax.broadcasted_iota(jnp.int32, total.shape, 0)
-            columns = lax.broadcasted_iota(jnp.int32, total.shape, 1)
-            total = total + jnp.where((rows == columns) & (odd == 1), 1.0, 0.0)
-        out_ref[0, (2 + at) * size : (3 + at) * size, :] = total
+
+    def put(units, keep_ref, parts):
+        received = [unpacker(ref) for ref in parts]
+        for at, unit in enumerate(units):
+            total = keep_ref[at]
+            for part in received:
+                total = total + part(at)
+            if unit >= 6:
+                rows = lax.broadcasted_iota(jnp.int32, total.shape, 0) + unit % 2 * UNIT
+                columns = lax.broadcasted_iota(jnp.int32, total.shape, 1)
+                total = total + jnp.where((rows == columns) & (odd == 1), 1.0, 0.0)
+            out_ref[0, unit * UNIT : (unit + 1) * UNIT, :] = total
+
+    for units in Z_FIRST:
+        put(units, refs.pop(0), [refs.pop(0)])
+    for units in X_FIRST:
+        put(units, refs.pop(0), [refs.pop(0) for _ in range(3)])
 
 
 def full_kernel(plan_ref, mate_ref, far_in, own_in, x_ref, far_ref, own_ref, power):
     add_mate(plan_ref, mate_ref, far_ref, own_ref)
-    pack([far_ref[at] for at in range(STRIP)], x_ref, power)
+    pack([unit_of(far_ref, owner, unit) for owner in range(4) for unit in range(8)], x_ref, power)
 
 
 def add_kernel(own_ref, x_ref, sum_ref):
-    size = own_ref.shape[1]
-    scales = powers_of(x_ref)
-    for at in range(STRIP):
-        sum_ref[at] = own_ref[at] + unpack(x_ref, scales, at, size)
+    received = unpacker(x_ref)
+    for at in range(4 * 8):
+        sum_ref[at * UNIT : (at + 1) * UNIT, :] = unit_of(own_ref, at // 8, at % 8) + received(at)
 
 
 def call(kernel, outs, operands, specs, out_specs=None, scratch=(), size=1 << 20, aliases=None):
@@ -216,12 +236,12 @@
         return lax.ppermute(value, axis, [(i, i ^ apart) for i in range(lax.axis_size(axis))])
 
     def message(count):
-        return jax.ShapeDtypeStruct((count * size + EXTRA, size), jnp.int16)
-
-    def full(count):
-        return jax.ShapeDtypeStruct((count, size, size), jnp.float32)
-
-    power = pltpu.VMEM((EXTRA, size), jnp.float32)
+        return jax.ShapeDtypeStruct((count * UNIT + extra_of(count), size), jnp.int16)
+
+    def full(count, rows=size):
+        return jax.ShapeDtypeStruct((count, rows, size), jnp.float32)
+
+    power = pltpu.VMEM((32, size), jnp.float32)
     mate = swap(blocks, "tile", 1)
     plan, far, own = call(
         near_kernel,
@@ -244,34 +264,56 @@
 
     if rows_count != 4:
         across, far, own = call(
-            full_kernel, [message(STRIP), far, own], operands, specs, scratch=[power], aliases={2: 1, 3: 2}
+            full_kernel, [message(4 * 8), far, own], operands, specs, scratch=[power], aliases={2: 1, 3: 2}
         )
-        strip = call(add_kernel, full(STRIP), (own, swap(across, "tile", 2)), [VMEM, VMEM])
-        share = lax.psum_scatter(strip.reshape(1, STRIP * size, size), "row", scatter_dimension=1, tiled=True)
+        sums = jax.ShapeDtypeStruct((STRIP * size, size), jnp.float32)
+        strip = call(add_kernel, sums, (own, swap(across, "tile", 2)), [VMEM, VMEM])
+        share = lax.psum_scatter(strip[None], "row", scatter_dimension=1, tiled=True)
         rows = lax.axis_index("row") * share.shape[1] + jnp.arange(share.shape[1], dtype=jnp.int32)
         unit = (rows // size % SPAN == SPAN - 1)[:, None] & ((rows % size)[:, None] == jnp.arange(size)[None, :])
         return share + unit.astype(jnp.float32)[None]
 
-    q2, q3, q1, x_p, far, own = call(
-        split_kernel,
-        [message(4), message(4), message(4), message(8), full(STRIP + 1), full(STRIP + 1)],
-        operands, specs, scratch=[power], aliases={2: 4, 3: 5},
+    def over_z(messages):
+        return [swap(value, "row", apart) for value, apart in zip(messages, (2, 3, 1))]
+
+    sent = [message(4 * len(units)) for units in X_FIRST]
+    for units in Z_FIRST:
+        sent += [message(2 * len(units))] * 3
+    *made, far, own = call(
+        split_kernel, [*sent, full(STRIP + 1), full(STRIP + 1)], operands, specs, scratch=[power],
+        aliases={2: len(sent), 3: len(sent) + 1},
     )
-    q2 = swap(q2, "row", 2)
-    q3 = swap(q3, "row", 3)
-    q1 = swap(q1, "row", 1)
-    x_p = swap(x_p, "tile", 2)
-    p2, p3, p1, own_p = call(
-        after_x_kernel, [message(2)] * 3 + [full(2)], (own, x_p), [VMEM] * 2, scratch=[pltpu.VMEM((8, size, size), jnp.float32), power]
-    )
-    p2 = swap(p2, "row", 2)
-    p3 = swap(p3, "row", 3)
-    p1 = swap(p1, "row", 1)
-    x_q, own_q = call(after_z_kernel, [message(2), full(2)], (own_p, far, own, q2, q3, q1), [pl.BlockSpec(memory_space=pl.ANY)] + [VMEM] * 5, scratch=[power])
-    x_q = swap(x_q, "tile", 2)
-    return call(
-        last_kernel, jax.ShapeDtypeStruct((1, 4 * size, size), jnp.float32), (own_p, p2, p3, p1, own_q, x_q), [VMEM] * 6
-    )
+    over_x = [swap(made.pop(0), "tile", 2) for units in X_FIRST]
+    first_z = [over_z([made.pop(0) for _ in range(3)]) for units in Z_FIRST]
+    last = {}
+    after = plan
+
+    def run_x(at):
+        units = X_FIRST[at]
+        count = len(units)
+        *onward, keep = call(
+            functools.partial(after_x_kernel, units), [message(count)] * 3 + [full(count, UNIT)],
+            (after, over_x[at], own), [ANY, VMEM, VMEM],
+            scratch=[pltpu.VMEM((4 * count, UNIT, size), jnp.float32), power],
+        )
+        last["x", at] = [keep, *over_z(onward)]
+        return keep
+
+    def run_z(at):
+        units = Z_FIRST[at]
+        count = len(units)
+        onward, keep = call(
+            functools.partial(after_z_kernel, units), [message(count), full(count, UNIT)],
+            (after, *first_z[at], far, own), [ANY] + [VMEM] * 5, scratch=[power],
+        )
+        last["z", at] = [keep, swap(onward, "tile", 2)]
+        return keep
+
+    for kind, at in ORDER:
+        after = (run_x if kind == "x" else run_z)(at)
+    parts = [part for at in range(len(Z_FIRST)) for part in last["z", at]]
+    parts += [part for at in range(len(X_FIRST)) for part in last["x", at]]
+    return call(last_kernel, jax.ShapeDtypeStruct((1, 4 * size, size), jnp.float32), parts, [VMEM] * len(parts))
 
 
 def solution(mesh):

time: 30.9 us -> 28.4 us (0.919)
  the two profiles are of different devices: /device:TPU:16 before, /device:TPU:0 now
where the time goes in v2:
time: 28.4 us; the launch traced here: 28.2 us
  starting transfers between devices  13.6 us (48%)
  waiting for transfers between devices  9.19 us (32%)
  Pallas kernels  5.42 us (19%)
    ppermute x9, starting transfers between devices, swap(): lax.ppermute(value, axis, [(i, i ^ apart) for i in range(lax.axis_size(ax...  13.6 us
    ppermute x9, waiting for transfers between devices, swap(): lax.ppermute(value, axis, [(i, i ^ apart) for i in range(lax.axis_size(ax...  9.19 us
    pallas_call x5, Pallas kernels, call(): pl.pallas_call(kernel, out_shape=outs, in_specs=specs, out_specs=jax.tree...  5.42 us
  transfers between devices with their start and end apart: 9, of which 5 were waited for; matrix products, arithmetic and copies ran while one was open for 0% of the time, Pallas kernels for 11%

profile of v2, /device:TPU:0, one launch (start us, length us, event | category | flops | bytes accessed | tf_op | source)
XLA Modules:
  0.0 28.2 jit_solution(8642601926309796177)
XLA Ops:
  0.0 0.5 %collective-permute-start = (bf16[16,4,128,128]{3,2,1,0:T(8,128)(2,1)}, bf16[16,4,128,128]{3,2,1,0:T(8,128)(2,1)S(1)}, u32[]{:S(2)}, u32[]{:S(2)}) collective-permute-start(bf16[16,4,128,128]{3,2,1,0:T(8,128)(2,1)} %blocks_ref.1), channel_id=1, source_target_pairs={{0,1},{1,0},{2,3},{3,2},{4,5},{5,4},{6,7},{7,6},{8,9},{9,8},{10,11... | collective-permute-start | bytes 6291464 | tf_op jit(solution)/shard_map/ppermute | solution.py:236
  0.5 2.8 %shard_map.37 = (s32[16,128]{1,0:T(8,128)S(1)}, f32[17,128,128]{2,1,0:T(8,128)S(1)}, f32[17,128,128]{2,1,0:T(8,128)S(1)}) custom-call(s32[4,64]{1,0:T(4,128)} %bitcast.1, s32[4]{0:T(128)} %low_hbm.1, bf16[16,4,128,128]{3,2,1,0:T(8,128)(2,1)} %blocks_ref.1), custom_call_target="tpu_custom_call" | custom-call | bytes 8388608 | tf_op jit(solution)/shard_map/pallas_call | solution.py:217
  3.3 1.2 %collective-permute-done.mate_ref = bf16[16,4,128,128]{3,2,1,0:T(8,128)(2,1)S(1)} collective-permute-done((bf16[16,4,128,128]{3,2,1,0:T(8,128)(2,1)}, bf16[16,4,128,128]{3,2,1,0:T(8,128)(2,1)S(1)}, u32[]{:S(2)}, u32[]{:S(2)}) %collective-permute-start) | collective-permute-done | bytes 2097184 | tf_op jit(solution)/shard_map/ppermute | solution.py:236
  4.5 1.4 %shard_map.38 = (s16[1312,128]{1,0:T(8,128)(2,1)S(1)}, s16[400,128]{1,0:T(8,128)(2,1)S(1)}, s16[400,128]{1,0:T(8,128)(2,1)S(1)}, s16[400,128]{1,0:T(8,128)(2,1)S...) custom-call(s32[16,128]{1,0:T(8,128)S(1)} %get-tuple-element.20.plan_, ...), custom_call_target="tpu_custom_call", output_to_operand_aliasing={{4}: (2, {}), {5}: (3, {})} | custom-call | bytes 1048576 | tf_op jit(solution)/shard_map/pallas_call | solution.py:217
  5.9 2.9 %collective-permute-start.1 = (s16[1312,128]{1,0:T(8,128)(2,1)S(1)}, s16[1312,128]{1,0:T(8,128)(2,1)S(1)}, u32[]{:S(2)}, u32[]{:S(2)}) collective-permute-start(s16[1312,128]{1,0:T(8,128)(2,1)S(1)} %get-tuple-element.23), channel_id=1, source_target_pairs={{0,2},{1,3},{2,0},{3,1},{4,6},{5,7},{6,4},{7,5},{8,10},{9,11},{10,... | collective-permute-start | bytes 1007624 | tf_op jit(solution)/shard_map/ppermute | solution.py:236
  8.8 2.6 %collective-permute-start.2 = (s16[400,128]{1,0:T(8,128)(2,1)S(1)}, s16[400,128]{1,0:T(8,128)(2,1)S(1)}, u32[]{:S(2)}, u32[]{:S(2)}) collective-permute-start(s16[400,128]{1,0:T(8,128)(2,1)S(1)} %get-tuple-element.26), channel_id=1, source_target_pairs={{0,8},{4,12},{8,0},{12,4},{1,9},{5,13},{9,1},{13,5},{2,10},{6,14},... | collective-permute-start | bytes 307208 | tf_op jit(solution)/shard_map/ppermute | solution.py:236
  11.4 1.3 %collective-permute-start.3 = (s16[400,128]{1,0:T(8,128)(2,1)S(1)}, s16[400,128]{1,0:T(8,128)(2,1)S(1)}, u32[]{:S(2)}, u32[]{:S(2)}) collective-permute-start(s16[400,128]{1,0:T(8,128)(2,1)S(1)} %get-tuple-element.27), channel_id=1, source_target_pairs={{0,12},{4,8},{8,4},{12,0},{1,13},{5,9},{9,5},{13,1},{2,14},{6,10},... | collective-permute-start | bytes 307208 | tf_op jit(solution)/shard_map/ppermute | solution.py:236
  12.8 0.2 collective-permute-start.4
  13.0 4.0 %collective-permute-done.1.x_ref = s16[1312,128]{1,0:T(8,128)(2,1)S(1)} collective-permute-done((s16[1312,128]{1,0:T(8,128)(2,1)S(1)}, s16[1312,128]{1,0:T(8,128)(2,1)S(1)}, u32[]{:S(2)}, u32[]{:S(2)}) %collective-permute-start.1) | collective-permute-done | bytes 335904 | tf_op jit(solution)/shard_map/ppermute | solution.py:236
  17.0 0.2 shard_map.39
  17.2 2.9 %collective-permute-start.6 = (s16[336,128]{1,0:T(8,128)(2,1)S(1)}, s16[336,128]{1,0:T(8,128)(2,1)S(1)}, u32[]{:S(2)}, u32[]{:S(2)}) collective-permute-start(s16[336,128]{1,0:T(8,128)(2,1)S(1)} %get-tuple-element.32), channel_id=1, source_target_pairs={{0,8},{4,12},{8,0},{12,4},{1,9},{5,13},{9,1},{13,5},{2,10},{6,14},... | collective-permute-start | bytes 258056 | tf_op jit(solution)/shard_map/ppermute | solution.py:236
  20.1 1.4 %collective-permute-start.7 = (s16[336,128]{1,0:T(8,128)(2,1)S(1)}, s16[336,128]{1,0:T(8,128)(2,1)S(1)}, u32[]{:S(2)}, u32[]{:S(2)}) collective-permute-start(s16[336,128]{1,0:T(8,128)(2,1)S(1)} %get-tuple-element.33), channel_id=1, source_target_pairs={{0,12},{4,8},{8,4},{12,0},{1,13},{5,9},{9,5},{13,1},{2,14},{6,10},... | collective-permute-start | bytes 258056 | tf_op jit(solution)/shard_map/ppermute | solution.py:236
  21.5 0.0 collective-permute-done.2.z2_ref
  21.5 0.2 collective-permute-start.8
  21.7 0.0 collective-permute-done.3.z3_ref
  21.7 0.0 collective-permute-done.4.z1_ref
  21.7 0.1 shard_map.40
  21.9 1.6 %collective-permute-start.5 = (s16[208,128]{1,0:T(8,128)(2,1)S(1)}, s16[208,128]{1,0:T(8,128)(2,1)S(1)}, u32[]{:S(2)}, u32[]{:S(2)}) collective-permute-start(s16[208,128]{1,0:T(8,128)(2,1)S(1)} %get-tuple-element.31), channel_id=1, source_target_pairs={{0,2},{1,3},{2,0},{3,1},{4,6},{5,7},{6,4},{7,5},{8,10},{9,11},{10,... | collective-permute-start | bytes 159752 | tf_op jit(solution)/shard_map/ppermute | solution.py:236
  23.4 2.6 %collective-permute-done.5.refs_1_ = s16[208,128]{1,0:T(8,128)(2,1)S(1)} collective-permute-done((s16[208,128]{1,0:T(8,128)(2,1)S(1)}, s16[208,128]{1,0:T(8,128)(2,1)S(1)}, u32[]{:S(2)}, u32[]{:S(2)}) %collective-permute-start.5) | collective-permute-done | bytes 53280 | tf_op jit(solution)/shard_map/ppermute | solution.py:236
  26.1 1.0 %collective-permute-done.6.refs_3_ = s16[336,128]{1,0:T(8,128)(2,1)S(1)} collective-permute-done((s16[336,128]{1,0:T(8,128)(2,1)S(1)}, s16[336,128]{1,0:T(8,128)(2,1)S(1)}, u32[]{:S(2)}, u32[]{:S(2)}) %collective-permute-start.6) | collective-permute-done | bytes 86048 | tf_op jit(solution)/shard_map/ppermute | solution.py:236
  27.1 0.0 collective-permute-done.7.refs_4_
  27.1 0.4 %collective-permute-done.8.refs_5_ = s16[336,128]{1,0:T(8,128)(2,1)S(1)} collective-permute-done((s16[336,128]{1,0:T(8,128)(2,1)S(1)}, s16[336,128]{1,0:T(8,128)(2,1)S(1)}, u32[]{:S(2)}, u32[]{:S(2)}) %collective-permute-start.8) | collective-permute-done | bytes 86048 | tf_op jit(solution)/shard_map/ppermute | solution.py:236
  27.4 0.8 %shard_map.41 = f32[1,512,128]{2,1,0:T(8,128)} custom-call(f32[3,64,128]{2,1,0:T(8,128)S(1)} %get-tuple-element.30.refs_0_, s16[208,128]{1,0:T(8,128)(2,1)S(1)} %collective-permute-done.5.refs_1_, f32[5,64,128]{2,1,0:T(8,128)S(1)} %get-tuple-element.25.after_ref.refs_2_, s16[336,128]{1,0:T(8,128)(2,1)S(1)} %collective-permute-done.6.refs_3_, ...), custom_call_target="tpu_custom_call" | custom-call | bytes 1048576 | tf_op jit(solution)/shard_map/pallas_call | solution.py:217
Async XLA Ops:
  0.0 4.5 %collective-permute-start = (bf16[16,4,128,128]{3,2,1,0:T(8,128)(2,1)}, bf16[16,4,128,128]{3,2,1,0:T(8,128)(2,1)S(1)}, u32[]{:S(2)}, u32[]{:S(2)}) collective-permute-start(bf16[16,4,128,128]{3,2,1,0:T(8,128)(2,1)} %blocks_ref.1), channel_id=1, source_target_pairs={{0,1},{1,0},{2,3},{3,2},{4,5},{5,4},{6,7},{7,6},{8,9},{9,8},{10,11... | collective-permute-start | bytes 6291464 | tf_op jit(solution)/shard_map/ppermute | solution.py:236
  5.9 11.1 %collective-permute-start.1 = (s16[1312,128]{1,0:T(8,128)(2,1)S(1)}, s16[1312,128]{1,0:T(8,128)(2,1)S(1)}, u32[]{:S(2)}, u32[]{:S(2)}) collective-permute-start(s16[1312,128]{1,0:T(8,128)(2,1)S(1)} %get-tuple-element.23), channel_id=1, source_target_pairs={{0,2},{1,3},{2,0},{3,1},{4,6},{5,7},{6,4},{7,5},{8,10},{9,11},{10,... | collective-permute-start | bytes 1007624 | tf_op jit(solution)/shard_map/ppermute | solution.py:236
  8.8 12.7 %collective-permute-start.2 = (s16[400,128]{1,0:T(8,128)(2,1)S(1)}, s16[400,128]{1,0:T(8,128)(2,1)S(1)}, u32[]{:S(2)}, u32[]{:S(2)}) collective-permute-start(s16[400,128]{1,0:T(8,128)(2,1)S(1)} %get-tuple-element.26), channel_id=1, source_target_pairs={{0,8},{4,12},{8,0},{12,4},{1,9},{5,13},{9,1},{13,5},{2,10},{6,14},... | collective-permute-start | bytes 307208 | tf_op jit(solution)/shard_map/ppermute | solution.py:236
  11.4 10.3 %collective-permute-start.3 = (s16[400,128]{1,0:T(8,128)(2,1)S(1)}, s16[400,128]{1,0:T(8,128)(2,1)S(1)}, u32[]{:S(2)}, u32[]{:S(2)}) collective-permute-start(s16[400,128]{1,0:T(8,128)(2,1)S(1)} %get-tuple-element.27), channel_id=1, source_target_pairs={{0,12},{4,8},{8,4},{12,0},{1,13},{5,9},{9,5},{13,1},{2,14},{6,10},... | collective-permute-start | bytes 307208 | tf_op jit(solution)/shard_map/ppermute | solution.py:236
  12.8 9.0 %collective-permute-start.4 = (s16[400,128]{1,0:T(8,128)(2,1)S(1)}, s16[400,128]{1,0:T(8,128)(2,1)S(1)}, u32[]{:S(2)}, u32[]{:S(2)}) collective-permute-start(s16[400,128]{1,0:T(8,128)(2,1)S(1)} %get-tuple-element.28), channel_id=1, source_target_pairs={{0,4},{4,0},{8,12},{12,8},{1,5},{5,1},{9,13},{13,9},{2,6},{6,2},{1... | collective-permute-start | bytes 307208 | tf_op jit(solution)/shard_map/ppermute | solution.py:236
  17.2 9.8 %collective-permute-start.6 = (s16[336,128]{1,0:T(8,128)(2,1)S(1)}, s16[336,128]{1,0:T(8,128)(2,1)S(1)}, u32[]{:S(2)}, u32[]{:S(2)}) collective-permute-start(s16[336,128]{1,0:T(8,128)(2,1)S(1)} %get-tuple-element.32), channel_id=1, source_target_pairs={{0,8},{4,12},{8,0},{12,4},{1,9},{5,13},{9,1},{13,5},{2,10},{6,14},... | collective-permute-start | bytes 258056 | tf_op jit(solution)/shard_map/ppermute | solution.py:236
  20.1 6.9 %collective-permute-start.7 = (s16[336,128]{1,0:T(8,128)(2,1)S(1)}, s16[336,128]{1,0:T(8,128)(2,1)S(1)}, u32[]{:S(2)}, u32[]{:S(2)}) collective-permute-start(s16[336,128]{1,0:T(8,128)(2,1)S(1)} %get-tuple-element.33), channel_id=1, source_target_pairs={{0,12},{4,8},{8,4},{12,0},{1,13},{5,9},{9,5},{13,1},{2,14},{6,10},... | collective-permute-start | bytes 258056 | tf_op jit(solution)/shard_map/ppermute | solution.py:236
  21.5 5.9 %collective-permute-start.8 = (s16[336,128]{1,0:T(8,128)(2,1)S(1)}, s16[336,128]{1,0:T(8,128)(2,1)S(1)}, u32[]{:S(2)}, u32[]{:S(2)}) collective-permute-start(s16[336,128]{1,0:T(8,128)(2,1)S(1)} %get-tuple-element.34), channel_id=1, source_target_pairs={{0,4},{4,0},{8,12},{12,8},{1,5},{5,1},{9,13},{13,9},{2,6},{6,2},{1... | collective-permute-start | bytes 258056 | tf_op jit(solution)/shard_map/ppermute | solution.py:236
  21.9 4.2 %collective-permute-start.5 = (s16[208,128]{1,0:T(8,128)(2,1)S(1)}, s16[208,128]{1,0:T(8,128)(2,1)S(1)}, u32[]{:S(2)}, u32[]{:S(2)}) collective-permute-start(s16[208,128]{1,0:T(8,128)(2,1)S(1)} %get-tuple-element.31), channel_id=1, source_target_pairs={{0,2},{1,3},{2,0},{3,1},{4,6},{5,7},{6,4},{7,5},{8,10},{9,11},{10,... | collective-permute-start | bytes 159752 | tf_op jit(solution)/shard_map/ppermute | solution.py:236

commit v3 on v1

v3 whole, which is shorter than its diff:
```python
import functools

import jax
import jax.numpy as jnp
from jax import lax
from jax.experimental import pallas as pl
from jax.experimental.pallas import tpu as pltpu
from jax.sharding import PartitionSpec as P

NB = 512
SPAN = 8
STRIP = 2 * SPAN

X_FIRST = (80, 80, 80, 80)
Z_FIRST = (96, 96)
TILE = 16
X_ROWS = sum(X_FIRST)
Z_ROWS = sum(Z_FIRST)
LENT = len(X_FIRST)
PLAIN = 64

HBM = pl.BlockSpec(memory_space=pltpu.HBM)
ANY = pl.BlockSpec(memory_space=pl.ANY)
VMEM = pl.BlockSpec(memory_space=pltpu.VMEM)
SMEM = pl.BlockSpec(memory_space=pltpu.SMEM)
PARAMS = pltpu.CompilerParams(vmem_limit_bytes=32 * 1024 * 1024)


def spans(groups, first=0):
    return [(first + sum(groups[:at]), rows) for at, rows in enumerate(groups)]


def power_of(*values):
    top = functools.reduce(jnp.maximum, [jnp.max(jnp.abs(v), axis=0, keepdims=True) for v in values])
    return jnp.ceil(jnp.log2(jnp.maximum(top, 1e-30)))


def codes_of(values, power):
    return jnp.clip(jnp.round(values * jnp.exp2(15.0 - power)), -32767.0, 32767.0)


def narrow(codes):
    return codes.astype(jnp.int32).astype(jnp.int16)


def widen(codes):
    return codes.astype(jnp.int32).astype(jnp.float32)


def last_row(rows, size, last, others):
    return jnp.where(lax.broadcasted_iota(jnp.int32, (rows, size), 0) == rows - 1, last, others)


def encode_lent(values):
    power = power_of(values)
    return narrow(last_row(*values.shape, power, codes_of(values, power)))


def decode_lent(codes):
    codes = widen(codes)
    return codes * jnp.exp2(codes[-1:, :] - 15.0)


def part_rows(owner, first, rows, part):
    return pl.ds(pl.multiple_of(owner * part + first, 16), rows)


def lent_row(ref, owner, first, rows, part):
    return ref[pl.ds(pl.multiple_of(owner * part + first + rows - 8, 8), 8), :][7:8, :]


def pack_sides(sides, message_ref, tile_ref):
    count = len(Z_FIRST)
    tile_ref[...] = jnp.zeros_like(tile_ref)
    for side, (groups, lent) in enumerate(sides):
        for at, (values, (first, rows)) in enumerate(zip(groups, spans(Z_FIRST, side * Z_ROWS))):
            power = power_of(values, *lent) if at == 0 else power_of(values)
            message_ref[first : first + rows, :] = narrow(codes_of(values, power))
            row = side * count + at
            tile_ref[row : row + 1, :] = power
            if at == 0:
                for index, value in enumerate(lent):
                    row = len(sides) * count + side * LENT + index
                    tile_ref[row : row + 1, :] = codes_of(value, power)
    message_ref[len(sides) * Z_ROWS :, :] = narrow(tile_ref[...])


def unpack_sides(message_ref, sides):
    count = len(Z_FIRST)
    tile = widen(message_ref[sides * Z_ROWS :, :])
    made = []
    for side in range(sides):
        scales = [jnp.exp2(tile[row : row + 1, :] - 15.0) for row in range(side * count, (side + 1) * count)]
        groups = [
            widen(message_ref[first : first + rows, :]) * scale
            for (first, rows), scale in zip(spans(Z_FIRST, side * Z_ROWS), scales)
        ]
        start = sides * count + side * LENT
        made.append((groups, [tile[row : row + 1, :] * scales[0] for row in range(start, start + LENT)]))
    return made


def plan_of(cols_ref, low_ref, fields_ref, quota):
    here = lax.axis_index("tile")
    cols = cols_ref[...]
    count = cols.shape[1]
    folded = jnp.minimum(cols, NB - 1 - cols)
    near = (folded == low_ref[here]).astype(jnp.int32)
    far = (folded == low_ref[here ^ 2]).astype(jnp.int32)
    hit = near + far
    target = jnp.sum(hit * cols, axis=0, keepdims=True)
    slot = jnp.sum(hit * lax.broadcasted_iota(jnp.int32, cols.shape, 0), axis=0, keepdims=True)
    local = jnp.sum(near, axis=0, keepdims=True)
    wanted = jnp.sum(hit, axis=0, keepdims=True)
    place = cols - target + SPAN - 1
    good = (cols >= 0) & (place >= 0) & (place < SPAN)
    place = jnp.where(good, place + jnp.where(target >= NB // 2, SPAN, 0), STRIP)
    panel = lax.broadcasted_iota(jnp.int32, (1, count), 1)
    device = panel // (4 * quota)
    mate = (device == (here ^ 1)).astype(jnp.int32)
    wanted = (wanted > 0) & ((device == here) | (mate > 0))
    group = jnp.where(wanted, local * 2 + mate, -1)
    members = (lax.broadcasted_iota(jnp.int32, (8, count), 0) == group).astype(jnp.float32)
    before = (
        lax.broadcasted_iota(jnp.int32, (count, count), 0) < lax.broadcasted_iota(jnp.int32, (count, count), 1)
    ).astype(jnp.float32)
    ranks = jnp.dot(members, before, preferred_element_type=jnp.float32)
    rank = jnp.sum(members * ranks, axis=0, keepdims=True).astype(jnp.int32)
    entry = jnp.where(wanted, group * quota + rank, -1)
    chosen = (lax.broadcasted_iota(jnp.int32, (4 * quota, count), 0) == entry).astype(jnp.float32)
    fields_ref[...] = jnp.zeros_like(fields_ref)
    fields_ref[0:1, 0:count] = (panel % (4 * quota)).astype(jnp.float32)
    fields_ref[1:2, 0:count] = slot.astype(jnp.float32)
    fields_ref[2:6, 0:count] = place.astype(jnp.float32)
    table = lax.dot_general(
        chosen, fields_ref[:, 0:count], (((1,), (1,)), ((), ())), preferred_element_type=jnp.float32
    )
    return table.astype(jnp.int32)


def add_products(plan_ref, entry, panels_ref, sums_ref):
    panel = plan_ref[entry, 0]
    column = panels_ref[panel, plan_ref[entry, 1]].T
    size = column.shape[0]
    wide = jnp.concatenate([panels_ref[panel, slot] for slot in range(4)], axis=1)
    made = jnp.dot(column, wide, preferred_element_type=jnp.float32)
    for slot in range(4):
        place = pl.multiple_of(plan_ref[entry, 2 + slot] * size, size)
        sums_ref[pl.ds(place, size), :] += made[:, slot * size : (slot + 1) * size]


def near_kernel(cols_hbm, low_hbm, blocks_ref, plan_ref, far_ref, own_ref, held, cols_ref, low_ref, fields, table, sems):
    quota = blocks_ref.shape[0] // 4
    cols_copy = pltpu.make_async_copy(cols_hbm, cols_ref, sems.at[0])
    low_copy = pltpu.make_async_copy(low_hbm, low_ref, sems.at[1])
    held_copy = pltpu.make_async_copy(blocks_ref, held, sems.at[2])
    cols_copy.start()
    low_copy.start()
    held_copy.start()
    far_ref[...] = jnp.zeros_like(far_ref)
    own_ref[...] = jnp.zeros_like(own_ref)
    low_copy.wait()
    cols_copy.wait()
    table[:, 0:8] = plan_of(cols_ref, low_ref, fields, quota)
    plan_copy = pltpu.make_async_copy(table, plan_ref, sems.at[3])
    plan_copy.start()
    plan_copy.wait()
    held_copy.wait()
    for at in range(quota):
        add_products(plan_ref, at, held, far_ref)
        add_products(plan_ref, 2 * quota + at, held, own_ref)


def add_mate(plan_ref, mate_ref, sums_ref, group):
    quota = mate_ref.shape[0] // 4
    for at in range(quota):
        add_products(plan_ref, group * quota + at, mate_ref, sums_ref)


def sides_of(refs, owner, part):
    return [
        (
            [ref[part_rows(owner, first, rows, part), :] for first, rows in spans(Z_FIRST, X_ROWS)],
            [lent_row(ref, owner, first, rows, part) for first, rows in spans(X_FIRST)],
        )
        for ref in refs
    ]


def pack_z(far_ref, own_ref, z_refs, tile):
    here = lax.axis_index("row")
    part = STRIP * far_ref.shape[1] // 4
    for apart, z_ref in zip((2, 3, 1), z_refs):
        pack_sides(sides_of((far_ref, own_ref), here ^ apart, part), z_ref, tile)


def pack_x(far_ref, x_ref):
    part = STRIP * far_ref.shape[1] // 4
    for owner in range(4):
        for first, rows in spans(X_FIRST):
            start = owner * part + first
            x_ref[owner * X_ROWS + first : owner * X_ROWS + first + rows, :] = encode_lent(far_ref[start : start + rows, :])


def split_kernel(plan_ref, mate_ref, far_in, own_in, x_ref, z2_ref, z3_ref, z1_ref, far_ref, own_ref, tile):
    add_mate(plan_ref, mate_ref, far_ref, 1)
    add_mate(plan_ref, mate_ref, own_ref, 3)
    pack_x(far_ref, x_ref)
    pack_z(far_ref, own_ref, (z2_ref, z3_ref, z1_ref), tile)


def after_x_kernel(x_ref, own_ref, z2_ref, z3_ref, z1_ref, keep_ref):
    here = lax.axis_index("row")
    part = STRIP * own_ref.shape[1] // 4

    def total(owner, first, rows):
        received = decode_lent(x_ref[part_rows(owner, first, rows, X_ROWS), :])
        return own_ref[part_rows(owner, first, rows, part), :] + received

    for apart, z_ref in ((2, z2_ref), (3, z3_ref), (1, z1_ref)):
        for first, rows in spans(X_FIRST):
            z_ref[first : first + rows, :] = encode_lent(total(here ^ apart, first, rows))
    for first, rows in spans(X_FIRST):
        keep_ref[first : first + rows, :] = total(here, first, rows)


def after_z_kernel(after_ref, z2_ref, z3_ref, z1_ref, far_ref, own_ref, x_ref, keep_ref, tile):
    here = lax.axis_index("row")
    part = STRIP * own_ref.shape[1] // 4
    mine = sides_of((far_ref, own_ref), here, part)
    received = [unpack_sides(ref, 2) for ref in (z2_ref, z3_ref, z1_ref)]

    def total(side):
        sides = [mine[side], *[sender[side] for sender in received]]
        return [[sum(values[1:], values[0]) for values in zip(*lists)] for lists in zip(*sides)]

    pack_sides([total(0)], x_ref, tile)
    groups, lent = total(1)
    for values, (first, rows) in zip(groups, spans(Z_FIRST)):
        keep_ref[first : first + rows, :] = values
    for index, value in enumerate(lent):
        keep_ref[Z_ROWS + index : Z_ROWS + index + 1, :] = value


def last_kernel(keep_q, x_ref, keep_p, z2_ref, z3_ref, z1_ref, out_ref):
    odd = lax.axis_index("row") % 2 == 1
    part, size = out_ref.shape[1:]

    def put(values, first, rows):
        if first + rows > part - size:
            row = lax.broadcasted_iota(jnp.int32, (rows, size), 0) + first
            column = lax.broadcasted_iota(jnp.int32, (rows, size), 1) + (part - size)
            values = values + jnp.where((row == column) & odd, 1.0, 0.0)
        out_ref[0, first : first + rows, :] = values

    ((groups, lent),) = unpack_sides(x_ref, 1)
    for values, (first, rows) in zip(groups, spans(Z_FIRST)):
        put(keep_q[first : first + rows, :] + values, X_ROWS + first, rows)
    for index, (first, rows) in enumerate(spans(X_FIRST)):
        values = keep_p[first : first + rows, :]
        for ref in (z2_ref, z3_ref, z1_ref):
            values = values + decode_lent(ref[first : first + rows, :])
        row = Z_ROWS + index
        put(last_row(rows, size, keep_q[row : row + 1, :] + lent[index], values), first, rows)


def all_kernel(plan_ref, mate_ref, far_in, own_in, x_ref, far_ref, own_ref, tile):
    add_mate(plan_ref, mate_ref, far_ref, 1)
    add_mate(plan_ref, mate_ref, own_ref, 3)
    count = tile.shape[0]
    for at in range(count):
        values = far_ref[at * PLAIN : (at + 1) * PLAIN, :]
        power = power_of(values)
        x_ref[at * PLAIN : (at + 1) * PLAIN, :] = narrow(codes_of(values, power))
        tile[at : at + 1, :] = power
    x_ref[count * PLAIN :, :] = narrow(tile[...])


def add_kernel(own_ref, x_ref, sum_ref):
    count = sum_ref.shape[0] // PLAIN
    scales = jnp.exp2(widen(x_ref[count * PLAIN :, :]) - 15.0)
    for at in range(count):
        rows = slice(at * PLAIN, (at + 1) * PLAIN)
        sum_ref[rows, :] = own_ref[rows, :] + widen(x_ref[rows, :]) * scales[at : at + 1, :]


def call(kernel, outs, operands, specs, out_specs=None, scratch=(), size=1 << 20, aliases=None):
    return pl.pallas_call(
        kernel,
        out_shape=outs,
        in_specs=specs,
        out_specs=jax.tree.map(lambda _: VMEM, outs) if out_specs is None else out_specs,
        scratch_shapes=list(scratch),
        input_output_aliases=aliases or {},
        compiler_params=PARAMS,
        cost_estimate=pl.CostEstimate(flops=0, bytes_accessed=size, transcendentals=0),
    )(*operands)


def on_device(blocks, block_cols, pair_low):
    panels_here, slots, size, _ = blocks.shape
    tiles_count = lax.axis_size("tile")
    rows_count = lax.axis_size("row")
    assert tiles_count == 4 and pair_low.shape[0] == 4 and slots == 4
    strip_rows = STRIP * size
    share = strip_rows // 4
    assert X_ROWS + Z_ROWS == share and 2 * (LENT + len(Z_FIRST)) <= TILE

    def swap(value, axis, apart):
        return lax.ppermute(value, axis, [(i, i ^ apart) for i in range(lax.axis_size(axis))])

    def message(rows):
        return jax.ShapeDtypeStruct((rows, size), jnp.int16)

    def full(rows):
        return jax.ShapeDtypeStruct((rows, size), jnp.float32)

    mate = swap(blocks, "tile", 1)
    strip = full(strip_rows + size)
    plan, far, own = call(
        near_kernel,
        [pltpu.SMEM((panels_here, 128), jnp.int32), strip, strip],
        tuple(pltpu.with_memory_space_constraint(value, pltpu.HBM) for value in (block_cols.T, pair_low, blocks)),
        [HBM, HBM, HBM],
        [SMEM, VMEM, VMEM],
        [
            pltpu.VMEM(blocks.shape, blocks.dtype),
            pltpu.VMEM(block_cols.shape[::-1], jnp.int32),
            pltpu.SMEM(pair_low.shape, jnp.int32),
            pltpu.VMEM((8, 128), jnp.float32),
            pltpu.VMEM((panels_here, 128), jnp.int32),
            pltpu.SemaphoreType.DMA((4,)),
        ],
        8 << 20,
    )

    if rows_count != 4:
        groups = strip_rows // PLAIN
        across, far, own = call(
            all_kernel, [message(strip_rows + groups), strip, strip], (plan, mate, far, own), [SMEM] + [VMEM] * 3,
            scratch=[pltpu.VMEM((groups, size), jnp.float32)], aliases={2: 1, 3: 2},
        )
        sums = call(add_kernel, full(strip_rows), (own, swap(across, "tile", 2)), [VMEM, VMEM])
        part = lax.psum_scatter(sums[None], "row", scatter_dimension=1, tiled=True)
        rows = lax.axis_index("row") * part.shape[1] + jnp.arange(part.shape[1], dtype=jnp.int32)
        unit = (rows // size % SPAN == SPAN - 1)[:, None] & ((rows % size)[:, None] == jnp.arange(size)[None, :])
        return part + unit.astype(jnp.float32)[None]

    def over_z(messages):
        return [swap(value, "row", apart) for value, apart in zip(messages, (2, 3, 1))]

    tile = pltpu.VMEM((TILE, size), jnp.float32)
    z_sent = [message(2 * Z_ROWS + TILE)] * 3
    p_x, *q_z, far, own = call(
        split_kernel, [message(4 * X_ROWS), *z_sent, strip, strip], (plan, mate, far, own), [SMEM] + [VMEM] * 3,
        scratch=[tile], aliases={2: 4, 3: 5},
    )
    p_x = swap(p_x, "tile", 2)
    q_z = over_z(q_z)
    *p_z, p_keep = call(after_x_kernel, [message(X_ROWS)] * 3 + [full(X_ROWS)], (p_x, own), [VMEM, VMEM])
    p_z = over_z(p_z)
    q_x, q_keep = call(
        after_z_kernel, [message(Z_ROWS + TILE), full(Z_ROWS + 8)],
        (p_keep, *q_z, far, own), [ANY] + [VMEM] * 5, scratch=[tile],
    )
    q_x = swap(q_x, "tile", 2)
    out = jax.ShapeDtypeStruct((1, share, size), jnp.float32)
    return call(last_kernel, out, (q_keep, q_x, p_keep, *p_z), [VMEM] * 6)


def solution(mesh):
    return jax.shard_map(
        on_device,
        mesh=mesh,
        in_specs=(
            P(("groups", "row", "tile"), None, None, None),
            P(("groups", "row"), None),
            P("groups"),
        ),
        out_specs=P(("groups", "tile"), "row", None),
        check_vma=False,
    )
```

time: 30.9 us -> 27.5 us (0.89)
  the two profiles are of different devices: /device:TPU:16 before, /device:TPU:0 now
where the time goes in v3:
time: 27.5 us; the launch traced here: 27.4 us
  starting transfers between devices  13.6 us (49%)
  waiting for transfers between devices  9.56 us (35%)
  Pallas kernels  4.2 us (15%)
    ppermute x9, starting transfers between devices, swap(): lax.ppermute(value, axis, [(i, i ^ apart) for i in range(lax.axis_size(ax...  13.6 us
    ppermute x9, waiting for transfers between devices, swap(): lax.ppermute(value, axis, [(i, i ^ apart) for i in range(lax.axis_size(ax...  9.56 us
    pallas_call x5, Pallas kernels, call(): pl.pallas_call(kernel, out_shape=outs, in_specs=specs, out_specs=jax.tree...  4.2 us
  transfers between devices with their start and end apart: 9, of which 5 were waited for; matrix products, arithmetic and copies ran while one was open for 0% of the time, Pallas kernels for 10%

profile of v3, /device:TPU:0, one launch (start us, length us, event | category | flops | bytes accessed | tf_op | source)
XLA Modules:
  0.0 27.4 jit_solution(7653908349096276310)
XLA Ops:
  0.0 0.5 %collective-permute-start = (bf16[16,4,128,128]{3,2,1,0:T(8,128)(2,1)}, bf16[16,4,128,128]{3,2,1,0:T(8,128)(2,1)S(1)}, u32[]{:S(2)}, u32[]{:S(2)}) collective-permute-start(bf16[16,4,128,128]{3,2,1,0:T(8,128)(2,1)} %blocks_ref.1), channel_id=1, source_target_pairs={{0,1},{1,0},{2,3},{3,2},{4,5},{5,4},{6,7},{7,6},{8,9},{9,8},{10,11... | collective-permute-start | bytes 6291464 | tf_op jit(solution)/shard_map/ppermute | solution.py:310
  0.5 2.3 %shard_map.37 = (s32[16,128]{1,0:T(8,128)S(4)}, f32[2176,128]{1,0:T(8,128)S(1)}, f32[2176,128]{1,0:T(8,128)S(1)}) custom-call(s32[4,64]{1,0:T(4,128)} %bitcast.1, s32[4]{0:T(128)} %low_hbm.1, bf16[16,4,128,128]{3,2,1,0:T(8,128)(2,1)} %blocks_ref.1), custom_call_target="tpu_custom_call" | custom-call | bytes 8388608 | tf_op jit(solution)/shard_map/pallas_call | solution.py:288
  2.7 1.7 %collective-permute-done.mate_ref = bf16[16,4,128,128]{3,2,1,0:T(8,128)(2,1)S(1)} collective-permute-done((bf16[16,4,128,128]{3,2,1,0:T(8,128)(2,1)}, bf16[16,4,128,128]{3,2,1,0:T(8,128)(2,1)S(1)}, u32[]{:S(2)}, u32[]{:S(2)}) %collective-permute-start) | collective-permute-done | bytes 2097184 | tf_op jit(solution)/shard_map/ppermute | solution.py:310
  4.5 0.8 %shard_map.38 = (s16[1280,128]{1,0:T(8,128)(2,1)S(1)}, s16[400,128]{1,0:T(8,128)(2,1)S(1)}, s16[400,128]{1,0:T(8,128)(2,1)S(1)}, s16[400,128]{1,0:T(8,128)(2,1)S...) custom-call(s32[16,128]{1,0:T(8,128)S(4)} %get-tuple-element.20.plan_ref, ...), custom_call_target="tpu_custom_call", output_to_operand_aliasing={{4}: (2, {}), {5}: (3, {})} | custom-call | bytes 1048576 | tf_op jit(solution)/shard_map/pallas_call | solution.py:288
  5.2 2.9 %collective-permute-start.1 = (s16[1280,128]{1,0:T(8,128)(2,1)S(1)}, s16[1280,128]{1,0:T(8,128)(2,1)S(1)}, u32[]{:S(2)}, u32[]{:S(2)}) collective-permute-start(s16[1280,128]{1,0:T(8,128)(2,1)S(1)} %get-tuple-element.23), channel_id=1, source_target_pairs={{0,2},{1,3},{2,0},{3,1},{4,6},{5,7},{6,4},{7,5},{8,10},{9,11},{10,... | collective-permute-start | bytes 983048 | tf_op jit(solution)/shard_map/ppermute | solution.py:310
  8.2 2.6 %collective-permute-start.2 = (s16[400,128]{1,0:T(8,128)(2,1)S(1)}, s16[400,128]{1,0:T(8,128)(2,1)S(1)}, u32[]{:S(2)}, u32[]{:S(2)}) collective-permute-start(s16[400,128]{1,0:T(8,128)(2,1)S(1)} %get-tuple-element.26), channel_id=1, source_target_pairs={{0,8},{4,12},{8,0},{12,4},{1,9},{5,13},{9,1},{13,5},{2,10},{6,14},... | collective-permute-start | bytes 307208 | tf_op jit(solution)/shard_map/ppermute | solution.py:310
  10.8 1.3 %collective-permute-start.3 = (s16[400,128]{1,0:T(8,128)(2,1)S(1)}, s16[400,128]{1,0:T(8,128)(2,1)S(1)}, u32[]{:S(2)}, u32[]{:S(2)}) collective-permute-start(s16[400,128]{1,0:T(8,128)(2,1)S(1)} %get-tuple-element.27), channel_id=1, source_target_pairs={{0,12},{4,8},{8,4},{12,0},{1,13},{5,9},{9,5},{13,1},{2,14},{6,10},... | collective-permute-start | bytes 307208 | tf_op jit(solution)/shard_map/ppermute | solution.py:310
  12.1 0.2 collective-permute-start.4
  12.3 3.9 %collective-permute-done.1.x_ref = s16[1280,128]{1,0:T(8,128)(2,1)S(1)} collective-permute-done((s16[1280,128]{1,0:T(8,128)(2,1)S(1)}, s16[1280,128]{1,0:T(8,128)(2,1)S(1)}, u32[]{:S(2)}, u32[]{:S(2)}) %collective-permute-start.1) | collective-permute-done | bytes 327712 | tf_op jit(solution)/shard_map/ppermute | solution.py:310
  16.2 0.2 shard_map.39
  16.4 2.9 %collective-permute-start.6 = (s16[320,128]{1,0:T(8,128)(2,1)S(1)}, s16[320,128]{1,0:T(8,128)(2,1)S(1)}, u32[]{:S(2)}, u32[]{:S(2)}) collective-permute-start(s16[320,128]{1,0:T(8,128)(2,1)S(1)} %get-tuple-element.32), channel_id=1, source_target_pairs={{0,8},{4,12},{8,0},{12,4},{1,9},{5,13},{9,1},{13,5},{2,10},{6,14},... | collective-permute-start | bytes 245768 | tf_op jit(solution)/shard_map/ppermute | solution.py:310
  19.3 1.4 %collective-permute-start.7 = (s16[320,128]{1,0:T(8,128)(2,1)S(1)}, s16[320,128]{1,0:T(8,128)(2,1)S(1)}, u32[]{:S(2)}, u32[]{:S(2)}) collective-permute-start(s16[320,128]{1,0:T(8,128)(2,1)S(1)} %get-tuple-element.33), channel_id=1, source_target_pairs={{0,12},{4,8},{8,4},{12,0},{1,13},{5,9},{9,5},{13,1},{2,14},{6,10},... | collective-permute-start | bytes 245768 | tf_op jit(solution)/shard_map/ppermute | solution.py:310
  20.6 0.0 collective-permute-done.2.z2_ref
  20.6 0.2 collective-permute-start.8
  20.9 0.0 collective-permute-done.3.z3_ref
  20.9 0.0 collective-permute-done.4.z1_ref
  20.9 0.1 shard_map.40
  21.0 1.6 %collective-permute-start.5 = (s16[208,128]{1,0:T(8,128)(2,1)S(1)}, s16[208,128]{1,0:T(8,128)(2,1)S(1)}, u32[]{:S(2)}, u32[]{:S(2)}) collective-permute-start(s16[208,128]{1,0:T(8,128)(2,1)S(1)} %get-tuple-element.31), channel_id=1, source_target_pairs={{0,2},{1,3},{2,0},{3,1},{4,6},{5,7},{6,4},{7,5},{8,10},{9,11},{10,... | collective-permute-start | bytes 159752 | tf_op jit(solution)/shard_map/ppermute | solution.py:310
  22.6 2.6 %collective-permute-done.5.x_ref = s16[208,128]{1,0:T(8,128)(2,1)S(1)} collective-permute-done((s16[208,128]{1,0:T(8,128)(2,1)S(1)}, s16[208,128]{1,0:T(8,128)(2,1)S(1)}, u32[]{:S(2)}, u32[]{:S(2)}) %collective-permute-start.5) | collective-permute-done | bytes 53280 | tf_op jit(solution)/shard_map/ppermute | solution.py:310
  25.2 1.1 %collective-permute-done.6.z2_ref = s16[320,128]{1,0:T(8,128)(2,1)S(1)} collective-permute-done((s16[320,128]{1,0:T(8,128)(2,1)S(1)}, s16[320,128]{1,0:T(8,128)(2,1)S(1)}, u32[]{:S(2)}, u32[]{:S(2)}) %collective-permute-start.6) | collective-permute-done | bytes 81952 | tf_op jit(solution)/shard_map/ppermute | solution.py:310
  26.3 0.0 collective-permute-done.7.z3_ref
  26.3 0.3 %collective-permute-done.8.z1_ref = s16[320,128]{1,0:T(8,128)(2,1)S(1)} collective-permute-done((s16[320,128]{1,0:T(8,128)(2,1)S(1)}, s16[320,128]{1,0:T(8,128)(2,1)S(1)}, u32[]{:S(2)}, u32[]{:S(2)}) %collective-permute-start.8) | collective-permute-done | bytes 81952 | tf_op jit(solution)/shard_map/ppermute | solution.py:310
  26.6 0.8 %shard_map.41 = f32[1,512,128]{2,1,0:T(8,128)} custom-call(f32[200,128]{1,0:T(8,128)S(1)} %get-tuple-element.30.keep_q, s16[208,128]{1,0:T(8,128)(2,1)S(1)} %collective-permute-done.5.x_ref, f32[320,128]{1,0:T(8,128)S(1)} %get-tuple-element.25.after_ref.keep_p, s16[320,128]{1,0:T(8,128)(2,1)S(1)} %collective-permute-done.6.z2_ref, ...), custom_call_target="tpu_custom_call" | custom-call | bytes 1048576 | tf_op jit(solution)/shard_map/pallas_call | solution.py:288
Async XLA Ops:
  0.0 4.5 %collective-permute-start = (bf16[16,4,128,128]{3,2,1,0:T(8,128)(2,1)}, bf16[16,4,128,128]{3,2,1,0:T(8,128)(2,1)S(1)}, u32[]{:S(2)}, u32[]{:S(2)}) collective-permute-start(bf16[16,4,128,128]{3,2,1,0:T(8,128)(2,1)} %blocks_ref.1), channel_id=1, source_target_pairs={{0,1},{1,0},{2,3},{3,2},{4,5},{5,4},{6,7},{7,6},{8,9},{9,8},{10,11... | collective-permute-start | bytes 6291464 | tf_op jit(solution)/shard_map/ppermute | solution.py:310
  5.2 11.0 %collective-permute-start.1 = (s16[1280,128]{1,0:T(8,128)(2,1)S(1)}, s16[1280,128]{1,0:T(8,128)(2,1)S(1)}, u32[]{:S(2)}, u32[]{:S(2)}) collective-permute-start(s16[1280,128]{1,0:T(8,128)(2,1)S(1)} %get-tuple-element.23), channel_id=1, source_target_pairs={{0,2},{1,3},{2,0},{3,1},{4,6},{5,7},{6,4},{7,5},{8,10},{9,11},{10,... | collective-permute-start | bytes 983048 | tf_op jit(solution)/shard_map/ppermute | solution.py:310
  8.2 12.5 %collective-permute-start.2 = (s16[400,128]{1,0:T(8,128)(2,1)S(1)}, s16[400,128]{1,0:T(8,128)(2,1)S(1)}, u32[]{:S(2)}, u32[]{:S(2)}) collective-permute-start(s16[400,128]{1,0:T(8,128)(2,1)S(1)} %get-tuple-element.26), channel_id=1, source_target_pairs={{0,8},{4,12},{8,0},{12,4},{1,9},{5,13},{9,1},{13,5},{2,10},{6,14},... | collective-permute-start | bytes 307208 | tf_op jit(solution)/shard_map/ppermute | solution.py:310
  10.8 10.1 %collective-permute-start.3 = (s16[400,128]{1,0:T(8,128)(2,1)S(1)}, s16[400,128]{1,0:T(8,128)(2,1)S(1)}, u32[]{:S(2)}, u32[]{:S(2)}) collective-permute-start(s16[400,128]{1,0:T(8,128)(2,1)S(1)} %get-tuple-element.27), channel_id=1, source_target_pairs={{0,12},{4,8},{8,4},{12,0},{1,13},{5,9},{9,5},{13,1},{2,14},{6,10},... | collective-permute-start | bytes 307208 | tf_op jit(solution)/shard_map/ppermute | solution.py:310
  12.1 8.8 %collective-permute-start.4 = (s16[400,128]{1,0:T(8,128)(2,1)S(1)}, s16[400,128]{1,0:T(8,128)(2,1)S(1)}, u32[]{:S(2)}, u32[]{:S(2)}) collective-permute-start(s16[400,128]{1,0:T(8,128)(2,1)S(1)} %get-tuple-element.28), channel_id=1, source_target_pairs={{0,4},{4,0},{8,12},{12,8},{1,5},{5,1},{9,13},{13,9},{2,6},{6,2},{1... | collective-permute-start | bytes 307208 | tf_op jit(solution)/shard_map/ppermute | solution.py:310
  16.4 9.9 %collective-permute-start.6 = (s16[320,128]{1,0:T(8,128)(2,1)S(1)}, s16[320,128]{1,0:T(8,128)(2,1)S(1)}, u32[]{:S(2)}, u32[]{:S(2)}) collective-permute-start(s16[320,128]{1,0:T(8,128)(2,1)S(1)} %get-tuple-element.32), channel_id=1, source_target_pairs={{0,8},{4,12},{8,0},{12,4},{1,9},{5,13},{9,1},{13,5},{2,10},{6,14},... | collective-permute-start | bytes 245768 | tf_op jit(solution)/shard_map/ppermute | solution.py:310
  19.3 7.0 %collective-permute-start.7 = (s16[320,128]{1,0:T(8,128)(2,1)S(1)}, s16[320,128]{1,0:T(8,128)(2,1)S(1)}, u32[]{:S(2)}, u32[]{:S(2)}) collective-permute-start(s16[320,128]{1,0:T(8,128)(2,1)S(1)} %get-tuple-element.33), channel_id=1, source_target_pairs={{0,12},{4,8},{8,4},{12,0},{1,13},{5,9},{9,5},{13,1},{2,14},{6,10},... | collective-permute-start | bytes 245768 | tf_op jit(solution)/shard_map/ppermute | solution.py:310
  20.6 5.9 %collective-permute-start.8 = (s16[320,128]{1,0:T(8,128)(2,1)S(1)}, s16[320,128]{1,0:T(8,128)(2,1)S(1)}, u32[]{:S(2)}, u32[]{:S(2)}) collective-permute-start(s16[320,128]{1,0:T(8,128)(2,1)S(1)} %get-tuple-element.34), channel_id=1, source_target_pairs={{0,4},{4,0},{8,12},{12,8},{1,5},{5,1},{9,13},{13,9},{2,6},{6,2},{1... | collective-permute-start | bytes 245768 | tf_op jit(solution)/shard_map/ppermute | solution.py:310
  21.0 4.2 %collective-permute-start.5 = (s16[208,128]{1,0:T(8,128)(2,1)S(1)}, s16[208,128]{1,0:T(8,128)(2,1)S(1)}, u32[]{:S(2)}, u32[]{:S(2)}) collective-permute-start(s16[208,128]{1,0:T(8,128)(2,1)S(1)} %get-tuple-element.31), channel_id=1, source_target_pairs={{0,2},{1,3},{2,0},{3,1},{4,6},{5,7},{6,4},{7,5},{8,10},{9,11},{10,... | collective-permute-start | bytes 159752 | tf_op jit(solution)/shard_map/ppermute | solution.py:310

commit v4 on v1

v4 whole, which is shorter than its diff:
```python
import functools

import jax
import jax.numpy as jnp
from jax import lax
from jax.experimental import pallas as pl
from jax.experimental.pallas import tpu as pltpu
from jax.sharding import PartitionSpec as P

NB = 512
SPAN = 8
STRIP = 2 * SPAN

SPLIT = (240, 240, 512, 240)
BLOCK = 128
ORDER = (2, 3, 1)
X_FIRST = ((2,), (0, 3, 1))
TAIL_CUT = 2

HBM = pl.BlockSpec(memory_space=pltpu.HBM)
ANY = pl.BlockSpec(memory_space=pl.ANY)
VMEM = pl.BlockSpec(memory_space=pltpu.VMEM)
SMEM = pl.BlockSpec(memory_space=pltpu.SMEM)
PARAMS = pltpu.CompilerParams(vmem_limit_bytes=32 * 1024 * 1024)


def cut(first, last, count):
    edges = [first + (last - first) * at // count // 16 * 16 for at in range(count)] + [last]
    return list(zip(edges, edges[1:]))


def groups_of(first, last):
    return [(low, high - low) for low, high in cut(first, last, -(-(last - first) // BLOCK))]


def early(part):
    made = [[(apart, groups_of(0, SPLIT[apart])) for apart in held if SPLIT[apart] > 0] for held in X_FIRST]
    return [message for message in made if message]


def z_first(part):
    made = []
    for apart in ORDER:
        if SPLIT[apart] < part:
            made.append((apart, groups_of(SPLIT[apart], part)))
    return made


def tail(part):
    return [groups_of(*rows) for rows in cut(SPLIT[0], part, TAIL_CUT)]


def message_rows(groups):
    return sum(rows for _, rows in groups) + -(-len(groups) // 16) * 16


def power_of(values):
    top = jnp.max(jnp.abs(values), axis=0, keepdims=True)
    return jnp.ceil(jnp.log2(jnp.maximum(top, 1e-30)))


def widen(codes):
    return codes.astype(jnp.int32).astype(jnp.float32)


def pack(groups, message_ref, tile_ref):
    first = 0
    tile_ref[...] = jnp.zeros_like(tile_ref)
    for at, values in enumerate(groups):
        power = power_of(values)
        codes = jnp.clip(jnp.round(values * jnp.exp2(15.0 - power)), -32767.0, 32767.0)
        message_ref[first : first + values.shape[0], :] = codes.astype(jnp.int32).astype(jnp.int16)
        tile_ref[at : at + 1, :] = power
        first += values.shape[0]
    extra = message_ref.shape[0] - first
    message_ref[first:, :] = tile_ref[0:extra, :].astype(jnp.int32).astype(jnp.int16)


def unpack(message_ref, groups):
    total = sum(rows for _, rows in groups)
    scales = jnp.exp2(widen(message_ref[total:, :]) - 15.0)
    made = []
    first = 0
    for at, (_, rows) in enumerate(groups):
        made.append(widen(message_ref[first : first + rows, :]) * scales[at : at + 1, :])
        first += rows
    return made


def part_rows(owner, first, rows, part):
    return pl.ds(pl.multiple_of(owner * part + first, 16), rows)


def plan_of(cols_ref, low_ref, fields_ref, quota):
    here = lax.axis_index("tile")
    cols = cols_ref[...]
    count = cols.shape[1]
    folded = jnp.minimum(cols, NB - 1 - cols)
    near = (folded == low_ref[here]).astype(jnp.int32)
    far = (folded == low_ref[here ^ 2]).astype(jnp.int32)
    hit = near + far
    target = jnp.sum(hit * cols, axis=0, keepdims=True)
    slot = jnp.sum(hit * lax.broadcasted_iota(jnp.int32, cols.shape, 0), axis=0, keepdims=True)
    local = jnp.sum(near, axis=0, keepdims=True)
    wanted = jnp.sum(hit, axis=0, keepdims=True)
    place = cols - target + SPAN - 1
    good = (cols >= 0) & (place >= 0) & (place < SPAN)
    place = jnp.where(good, place + jnp.where(target >= NB // 2, SPAN, 0), STRIP)
    panel = lax.broadcasted_iota(jnp.int32, (1, count), 1)
    device = panel // (4 * quota)
    mate = (device == (here ^ 1)).astype(jnp.int32)
    wanted = (wanted > 0) & ((device == here) | (mate > 0))
    group = jnp.where(wanted, local * 2 + mate, -1)
    members = (lax.broadcasted_iota(jnp.int32, (8, count), 0) == group).astype(jnp.float32)
    before = (
        lax.broadcasted_iota(jnp.int32, (count, count), 0) < lax.broadcasted_iota(jnp.int32, (count, count), 1)
    ).astype(jnp.float32)
    ranks = jnp.dot(members, before, preferred_element_type=jnp.float32)
    rank = jnp.sum(members * ranks, axis=0, keepdims=True).astype(jnp.int32)
    entry = jnp.where(wanted, group * quota + rank, -1)
    chosen = (lax.broadcasted_iota(jnp.int32, (4 * quota, count), 0) == entry).astype(jnp.float32)
    fields_ref[...] = jnp.zeros_like(fields_ref)
    fields_ref[0:1, 0:count] = (panel % (4 * quota)).astype(jnp.float32)
    fields_ref[1:2, 0:count] = slot.astype(jnp.float32)
    fields_ref[2:6, 0:count] = place.astype(jnp.float32)
    table = lax.dot_general(
        chosen, fields_ref[:, 0:count], (((1,), (1,)), ((), ())), preferred_element_type=jnp.float32
    )
    return table.astype(jnp.int32)


def add_products(plan_ref, entry, panels_ref, sums_ref):
    panel = plan_ref[entry, 0]
    column = panels_ref[panel, plan_ref[entry, 1]].T
    size = column.shape[0]
    wide = jnp.concatenate([panels_ref[panel, slot] for slot in range(4)], axis=1)
    made = jnp.dot(column, wide, preferred_element_type=jnp.float32)
    for slot in range(4):
        place = pl.multiple_of(plan_ref[entry, 2 + slot] * size, size)
        sums_ref[pl.ds(place, size), :] += made[:, slot * size : (slot + 1) * size]


def near_kernel(cols_hbm, low_hbm, blocks_ref, plan_ref, far_ref, own_ref, held, cols_ref, low_ref, fields, table, sems):
    quota = blocks_ref.shape[0] // 4
    cols_copy = pltpu.make_async_copy(cols_hbm, cols_ref, sems.at[0])
    low_copy = pltpu.make_async_copy(low_hbm, low_ref, sems.at[1])
    held_copy = pltpu.make_async_copy(blocks_ref, held, sems.at[2])
    cols_copy.start()
    low_copy.start()
    held_copy.start()
    far_ref[...] = jnp.zeros_like(far_ref)
    own_ref[...] = jnp.zeros_like(own_ref)
    low_copy.wait()
    cols_copy.wait()
    table[:, 0:8] = plan_of(cols_ref, low_ref, fields, quota)
    plan_copy = pltpu.make_async_copy(table, plan_ref, sems.at[3])
    plan_copy.start()
    plan_copy.wait()
    held_copy.wait()
    for at in range(quota):
        add_products(plan_ref, at, held, far_ref)
        add_products(plan_ref, 2 * quota + at, held, own_ref)


def add_mate(plan_ref, mate_ref, sums_ref, group):
    quota = mate_ref.shape[0] // 4
    for at in range(quota):
        add_products(plan_ref, group * quota + at, mate_ref, sums_ref)


def split_kernel(plan_ref, mate_ref, far_in, own_in, *refs):
    *refs, far_ref, own_ref, tile = refs
    add_mate(plan_ref, mate_ref, far_ref, 1)
    add_mate(plan_ref, mate_ref, own_ref, 3)
    here = lax.axis_index("row")
    part = STRIP * far_ref.shape[1] // 4
    for held in early(part):
        groups = [far_ref[part_rows(here ^ apart, *group, part), :] for apart, groups in held for group in groups]
        pack(groups, refs.pop(0), tile)
    for apart, groups in z_first(part):
        groups = [ref[part_rows(here ^ apart, *group, part), :] for ref in (far_ref, own_ref) for group in groups]
        pack(groups, refs.pop(0), tile)


def after_x_kernel(held, after_ref, x_ref, own_ref, *refs):
    *refs, tile = refs
    here = lax.axis_index("row")
    part = STRIP * own_ref.shape[1] // 4
    received = unpack(x_ref, [group for _, groups in held for group in groups])
    for apart, groups in held:
        totals = [own_ref[part_rows(here ^ apart, *group, part), :] + received.pop(0) for group in groups]
        if apart == 0:
            refs[0][...] = jnp.concatenate(totals)
        else:
            pack(totals, refs[0], tile)
        refs = refs[1:]


def after_z_kernel(after_ref, far_ref, own_ref, *refs):
    z_refs, x_refs = refs[: len(refs) - TAIL_CUT - 3], refs[len(refs) - TAIL_CUT - 3 : -3]
    keep_ref, far_sum, tile = refs[-3:]
    here = lax.axis_index("row")
    part = STRIP * own_ref.shape[1] // 4
    first = SPLIT[0]
    for sums_ref, total_ref in ((far_ref, far_sum), (own_ref, keep_ref)):
        total_ref[...] = sums_ref[part_rows(here, first, part - first, part), :]
    for (apart, groups), z_ref in zip(z_first(part), z_refs):
        received = unpack(z_ref, 2 * groups)
        for total_ref in (far_sum, keep_ref):
            for low, rows in groups:
                total_ref[low - first : low - first + rows, :] += received.pop(0)
    for groups, x_ref in zip(tail(part), x_refs):
        pack([far_sum[low - first : low - first + rows, :] for low, rows in groups], x_ref, tile)


def last_kernel(keep_q, keep_p, *refs):
    x_refs, z_refs, out_ref = refs[:TAIL_CUT], refs[TAIL_CUT:-1], refs[-1]
    part, size = out_ref.shape[1:]
    first = SPLIT[0]
    if first > 0:
        out_ref[0, 0:first, :] = keep_p[...]
    for groups, x_ref in zip(tail(part), x_refs):
        for (low, rows), values in zip(groups, unpack(x_ref, groups)):
            out_ref[0, low : low + rows, :] = keep_q[low - first : low - first + rows, :] + values
    came = dict(pair for held in early(part) for pair in held)
    for apart, z_ref in zip([apart for apart in ORDER if apart in came], z_refs):
        for (low, rows), values in zip(came[apart], unpack(z_ref, came[apart])):
            out_ref[0, low : low + rows, :] += values
    row = lax.broadcasted_iota(jnp.int32, (size, size), 0)
    column = lax.broadcasted_iota(jnp.int32, (size, size), 1)
    odd = lax.axis_index("row") % 2 == 1
    out_ref[0, part - size :, :] += jnp.where((row == column) & odd, 1.0, 0.0)


def all_kernel(plan_ref, mate_ref, far_in, own_in, x_ref, far_ref, own_ref, tile):
    add_mate(plan_ref, mate_ref, far_ref, 1)
    add_mate(plan_ref, mate_ref, own_ref, 3)
    size = far_ref.shape[1]
    pack([far_ref[low : low + rows, :] for low, rows in groups_of(0, STRIP * size)], x_ref, tile)


def add_kernel(own_ref, x_ref, sum_ref):
    groups = groups_of(0, sum_ref.shape[0])
    for (low, rows), values in zip(groups, unpack(x_ref, groups)):
        sum_ref[low : low + rows, :] = own_ref[low : low + rows, :] + values


def call(kernel, outs, operands, specs, out_specs=None, scratch=(), size=1 << 20, aliases=None):
    return pl.pallas_call(
        kernel,
        out_shape=outs,
        in_specs=specs,
        out_specs=jax.tree.map(lambda _: VMEM, outs) if out_specs is None else out_specs,
        scratch_shapes=list(scratch),
        input_output_aliases=aliases or {},
        compiler_params=PARAMS,
        cost_estimate=pl.CostEstimate(flops=0, bytes_accessed=size, transcendentals=0),
    )(*operands)


def on_device(blocks, block_cols, pair_low):
    panels_here, slots, size, _ = blocks.shape
    tiles_count = lax.axis_size("tile")
    rows_count = lax.axis_size("row")
    assert tiles_count == 4 and pair_low.shape[0] == 4 and slots == 4
    strip_rows = STRIP * size
    share = strip_rows // 4
    assert SPLIT[0] == SPLIT[1] <= min(SPLIT[2:]) and max(SPLIT) <= share

    def swap(value, axis, apart):
        return lax.ppermute(value, axis, [(i, i ^ apart) for i in range(lax.axis_size(axis))])

    def message(groups):
        return jax.ShapeDtypeStruct((message_rows(groups), size), jnp.int16)

    def full(rows):
        return jax.ShapeDtypeStruct((rows, size), jnp.float32)

    mate = swap(blocks, "tile", 1)
    strip = full(strip_rows + size)
    plan, far, own = call(
        near_kernel,
        [pltpu.SMEM((panels_here, 128), jnp.int32), strip, strip],
        tuple(pltpu.with_memory_space_constraint(value, pltpu.HBM) for value in (block_cols.T, pair_low, blocks)),
        [HBM, HBM, HBM],
        [SMEM, VMEM, VMEM],
        [
            pltpu.VMEM(blocks.shape, blocks.dtype),
            pltpu.VMEM(block_cols.shape[::-1], jnp.int32),
            pltpu.SMEM(pair_low.shape, jnp.int32),
            pltpu.VMEM((8, 128), jnp.float32),
            pltpu.VMEM((panels_here, 128), jnp.int32),
            pltpu.SemaphoreType.DMA((4,)),
        ],
        8 << 20,
    )

    tile = pltpu.VMEM((32, size), jnp.float32)

    if rows_count != 4:
        across, far, own = call(
            all_kernel, [message(groups_of(0, strip_rows)), strip, strip], (plan, mate, far, own), [SMEM] + [VMEM] * 3,
            scratch=[tile], aliases={2: 1, 3: 2},
        )
        sums = call(add_kernel, full(strip_rows), (own, swap(across, "tile", 2)), [VMEM, VMEM])
        part = lax.psum_scatter(sums[None], "row", scatter_dimension=1, tiled=True)
        rows = lax.axis_index("row") * part.shape[1] + jnp.arange(part.shape[1], dtype=jnp.int32)
        unit = (rows // size % SPAN == SPAN - 1)[:, None] & ((rows % size)[:, None] == jnp.arange(size)[None, :])
        return part + unit.astype(jnp.float32)[None]

    x_sent, z_sent = early(share), z_first(share)
    x_groups = [[group for _, groups in held for group in groups] for held in x_sent]
    *made, far, own = call(
        split_kernel,
        [*[message(groups) for groups in x_groups], *[message(2 * groups) for _, groups in z_sent], strip, strip],
        (plan, mate, far, own), [SMEM] + [VMEM] * 3, scratch=[tile],
        aliases={2: len(x_sent) + len(z_sent), 3: len(x_sent) + len(z_sent) + 1},
    )
    over_x = [swap(made.pop(0), "tile", 2) for _ in x_sent]
    q_z = [swap(made.pop(0), "row", apart) for apart, _ in z_sent]
    after, second = plan, {}
    for held, value in zip(x_sent, over_x):
        results = [full(SPLIT[0]) if apart == 0 else message(groups) for apart, groups in held]
        results = call(
            functools.partial(after_x_kernel, held), results, (after, value, own), [ANY, VMEM, VMEM], scratch=[tile]
        )
        after = results[0]
        for (apart, _), value in zip(held, results):
            second[apart] = value if apart == 0 else swap(value, "row", apart)
    p_keep = second.get(0, plan)
    p_z = [second[apart] for apart in ORDER if apart in second]
    rest = share - SPLIT[0]
    *q_x, q_keep = call(
        after_z_kernel, [*[message(groups) for groups in tail(share)], full(rest)], (after, far, own, *q_z),
        [ANY] + [VMEM] * (2 + len(q_z)), scratch=[pltpu.VMEM((rest, size), jnp.float32), tile],
    )
    q_x = [swap(value, "tile", 2) for value in q_x]
    out = jax.ShapeDtypeStruct((1, share, size), jnp.float32)
    return call(last_kernel, out, (q_keep, p_keep, *q_x, *p_z), [VMEM, VMEM if 0 in second else ANY] + [VMEM] * (len(q_x) + len(p_z)))


def solution(mesh):
    return jax.shard_map(
        on_device,
        mesh=mesh,
        in_specs=(
            P(("groups", "row", "tile"), None, None, None),
            P(("groups", "row"), None),
            P("groups"),
        ),
        out_specs=P(("groups", "tile"), "row", None),
        check_vma=False,
    )
```

time: 30.9 us -> 26.9 us (0.87)
  the two profiles are of different devices: /device:TPU:16 before, /device:TPU:0 now
where the time goes in v4:
time: 26.9 us; the launch traced here: 26.8 us
  starting transfers between devices  16.7 us (62%)
  waiting for transfers between devices  5.87 us (22%)
  Pallas kernels  4.21 us (16%)
    ppermute x10, starting transfers between devices, swap(): lax.ppermute(value, axis, [(i, i ^ apart) for i in range(lax.axis_size(ax...  16.7 us
    ppermute x10, waiting for transfers between devices, swap(): lax.ppermute(value, axis, [(i, i ^ apart) for i in range(lax.axis_size(ax...  5.87 us
    pallas_call x6, Pallas kernels, call(): pl.pallas_call(kernel, out_shape=outs, in_specs=specs, out_specs=jax.tree...  4.21 us
  transfers between devices with their start and end apart: 10, of which 5 were waited for; matrix products, arithmetic and copies ran while one was open for 0% of the time, Pallas kernels for 10%

profile of v4, /device:TPU:0, one launch (start us, length us, event | category | flops | bytes accessed | tf_op | source)
XLA Modules:
  0.0 26.8 jit_solution(1932021623711239967)
XLA Ops:
  0.0 0.5 %collective-permute-start = (bf16[16,4,128,128]{3,2,1,0:T(8,128)(2,1)}, bf16[16,4,128,128]{3,2,1,0:T(8,128)(2,1)S(1)}, u32[]{:S(2)}, u32[]{:S(2)}) collective-permute-start(bf16[16,4,128,128]{3,2,1,0:T(8,128)(2,1)} %blocks_ref.1), channel_id=1, source_target_pairs={{0,1},{1,0},{2,3},{3,2},{4,5},{5,4},{6,7},{7,6},{8,9},{9,8},{10,11... | collective-permute-start | bytes 6291464 | tf_op jit(solution)/shard_map/ppermute | solution.py:271
  0.5 2.3 %shard_map.37 = (s32[16,128]{1,0:T(8,128)S(4)}, f32[2176,128]{1,0:T(8,128)S(1)}, f32[2176,128]{1,0:T(8,128)S(1)}) custom-call(s32[4,64]{1,0:T(4,128)} %bitcast.1, s32[4]{0:T(128)} %low_hbm.1, bf16[16,4,128,128]{3,2,1,0:T(8,128)(2,1)} %blocks_ref.1), custom_call_target="tpu_custom_call" | custom-call | bytes 8388608 | tf_op jit(solution)/shard_map/pallas_call | solution.py:249
  2.7 1.7 %collective-permute-done.mate_ref = bf16[16,4,128,128]{3,2,1,0:T(8,128)(2,1)S(1)} collective-permute-done((bf16[16,4,128,128]{3,2,1,0:T(8,128)(2,1)}, bf16[16,4,128,128]{3,2,1,0:T(8,128)(2,1)S(1)}, u32[]{:S(2)}, u32[]{:S(2)}) %collective-permute-start) | collective-permute-done | bytes 2097184 | tf_op jit(solution)/shard_map/ppermute | solution.py:271
  4.5 0.8 %shard_map.38 = (s16[528,128]{1,0:T(8,128)(2,1)S(1)}, s16[736,128]{1,0:T(8,128)(2,1)S(1)}, s16[560,128]{1,0:T(8,128)(2,1)S(1)}, s16[560,128]{1,0:T(8,128)(2,1)S(...) custom-call(s32[16,128]{1,0:T(8,128)S(4)} %get-tuple-element.20.plan_ref.after, ...), custom_call_target="tpu_custom_call", output_to_operand_aliasing={{4}: (2, {}), {5}: (3, {})} | custom-call | bytes 1048576 | tf_op jit(solution)/shard_map/pallas_call | solution.py:249
  5.2 2.9 %collective-permute-start.1 = (s16[528,128]{1,0:T(8,128)(2,1)S(1)}, s16[528,128]{1,0:T(8,128)(2,1)S(1)}, u32[]{:S(2)}, u32[]{:S(2)}) collective-permute-start(s16[528,128]{1,0:T(8,128)(2,1)S(1)} %get-tuple-element.23), channel_id=1, source_target_pairs={{0,2},{1,3},{2,0},{3,1},{4,6},{5,7},{6,4},{7,5},{8,10},{9,11},{10,... | collective-permute-start | bytes 405512 | tf_op jit(solution)/shard_map/ppermute | solution.py:271
  8.1 0.1 collective-permute-start.2
  8.2 4.1 %collective-permute-start.3 = (s16[560,128]{1,0:T(8,128)(2,1)S(1)}, s16[560,128]{1,0:T(8,128)(2,1)S(1)}, u32[]{:S(2)}, u32[]{:S(2)}) collective-permute-start(s16[560,128]{1,0:T(8,128)(2,1)S(1)} %get-tuple-element.28), channel_id=1, source_target_pairs={{0,12},{4,8},{8,4},{12,0},{1,13},{5,9},{9,5},{13,1},{2,14},{6,10},... | collective-permute-start | bytes 430088 | tf_op jit(solution)/shard_map/ppermute | solution.py:271
  12.3 0.0 collective-permute-start.4
  12.3 0.2 collective-permute-done.1.x_ref
  12.5 0.1 shard_map.39.after_ref
  12.6 3.2 %collective-permute-start.7 = (s16[528,128]{1,0:T(8,128)(2,1)S(1)}, s16[528,128]{1,0:T(8,128)(2,1)S(1)}, u32[]{:S(2)}, u32[]{:S(2)}) collective-permute-start(s16[528,128]{1,0:T(8,128)(2,1)S(1)} %shard_map.39.after_ref), channel_id=1, source_target_pairs={{0,8},{4,12},{8,0},{12,4},{1,9},{5,13},{9,1},{13,5},{2,10},{6,14},... | collective-permute-start | bytes 405512 | tf_op jit(solution)/shard_map/ppermute | solution.py:271
  15.8 0.3 collective-permute-done.2.x_ref
  16.1 0.1 shard_map.40
  16.2 3.9 %collective-permute-start.8 = (s16[256,128]{1,0:T(8,128)(2,1)S(1)}, s16[256,128]{1,0:T(8,128)(2,1)S(1)}, u32[]{:S(2)}, u32[]{:S(2)}) collective-permute-start(s16[256,128]{1,0:T(8,128)(2,1)S(1)} %get-tuple-element.33), channel_id=1, source_target_pairs={{0,12},{4,8},{8,4},{12,0},{1,13},{5,9},{9,5},{13,1},{2,14},{6,10},... | collective-permute-start | bytes 196616 | tf_op jit(solution)/shard_map/ppermute | solution.py:271
  20.1 0.0 collective-permute-start.9
  20.1 0.0 collective-permute-done.3.refs_0_
  20.1 0.0 collective-permute-done.4.refs_1_
  20.1 0.1 shard_map.41
  20.2 1.5 %collective-permute-start.6 = (s16[160,128]{1,0:T(8,128)(2,1)S(1)}, s16[160,128]{1,0:T(8,128)(2,1)S(1)}, u32[]{:S(2)}, u32[]{:S(2)}) collective-permute-start(s16[160,128]{1,0:T(8,128)(2,1)S(1)} %get-tuple-element.32), channel_id=1, source_target_pairs={{0,2},{1,3},{2,0},{3,1},{4,6},{5,7},{6,4},{7,5},{8,10},{9,11},{10,... | collective-permute-start | bytes 122888 | tf_op jit(solution)/shard_map/ppermute | solution.py:271
  21.8 0.5 %collective-permute-start.5 = (s16[144,128]{1,0:T(8,128)(2,1)S(1)}, s16[144,128]{1,0:T(8,128)(2,1)S(1)}, u32[]{:S(2)}, u32[]{:S(2)}) collective-permute-start(s16[144,128]{1,0:T(8,128)(2,1)S(1)} %get-tuple-element.31), channel_id=1, source_target_pairs={{0,2},{1,3},{2,0},{3,1},{4,6},{5,7},{6,4},{7,5},{8,10},{9,11},{10,... | collective-permute-start | bytes 110600 | tf_op jit(solution)/shard_map/ppermute | solution.py:271
  22.3 3.4 %collective-permute-done.5.refs_0_ = s16[144,128]{1,0:T(8,128)(2,1)S(1)} collective-permute-done((s16[144,128]{1,0:T(8,128)(2,1)S(1)}, s16[144,128]{1,0:T(8,128)(2,1)S(1)}, u32[]{:S(2)}, u32[]{:S(2)}) %collective-permute-start.5) | collective-permute-done | bytes 36896 | tf_op jit(solution)/shard_map/ppermute | solution.py:271
  25.8 0.0 collective-permute-done.6.refs_1_
  25.8 0.0 collective-permute-done.8.refs_3_
  25.8 0.3 collective-permute-done.9.refs_4_
  26.0 0.0 collective-permute-done.7.refs_2_
  26.0 0.8 %shard_map.42 = f32[1,512,128]{2,1,0:T(8,128)} custom-call(f32[272,128]{1,0:T(8,128)S(1)} %get-tuple-element.30.keep_q, f32[240,128]{1,0:T(8,128)S(1)} %get-tuple-element.26.after_ref.keep_p, s16[144,128]{1,0:T(8,128)(2,1)S(1)} %collective-permute-done.5.refs_0_, s16[160,128]{1,0:T(8,128)(2,1)S(1)} %collective-permute-done.6.refs_1_, ...), custom_call_target="tpu_custom_call" | custom-call | bytes 1048576 | tf_op jit(solution)/shard_map/pallas_call | solution.py:249
Async XLA Ops:
  0.0 4.5 %collective-permute-start = (bf16[16,4,128,128]{3,2,1,0:T(8,128)(2,1)}, bf16[16,4,128,128]{3,2,1,0:T(8,128)(2,1)S(1)}, u32[]{:S(2)}, u32[]{:S(2)}) collective-permute-start(bf16[16,4,128,128]{3,2,1,0:T(8,128)(2,1)} %blocks_ref.1), channel_id=1, source_target_pairs={{0,1},{1,0},{2,3},{3,2},{4,5},{5,4},{6,7},{7,6},{8,9},{9,8},{10,11... | collective-permute-start | bytes 6291464 | tf_op jit(solution)/shard_map/ppermute | solution.py:271
  5.2 7.3 %collective-permute-start.1 = (s16[528,128]{1,0:T(8,128)(2,1)S(1)}, s16[528,128]{1,0:T(8,128)(2,1)S(1)}, u32[]{:S(2)}, u32[]{:S(2)}) collective-permute-start(s16[528,128]{1,0:T(8,128)(2,1)S(1)} %get-tuple-element.23), channel_id=1, source_target_pairs={{0,2},{1,3},{2,0},{3,1},{4,6},{5,7},{6,4},{7,5},{8,10},{9,11},{10,... | collective-permute-start | bytes 405512 | tf_op jit(solution)/shard_map/ppermute | solution.py:271
  8.1 7.9 %collective-permute-start.2 = (s16[736,128]{1,0:T(8,128)(2,1)S(1)}, s16[736,128]{1,0:T(8,128)(2,1)S(1)}, u32[]{:S(2)}, u32[]{:S(2)}) collective-permute-start(s16[736,128]{1,0:T(8,128)(2,1)S(1)} %get-tuple-element.25), channel_id=1, source_target_pairs={{0,2},{1,3},{2,0},{3,1},{4,6},{5,7},{6,4},{7,5},{8,10},{9,11},{10,... | collective-permute-start | bytes 565256 | tf_op jit(solution)/shard_map/ppermute | solution.py:271
  8.2 11.9 %collective-permute-start.3 = (s16[560,128]{1,0:T(8,128)(2,1)S(1)}, s16[560,128]{1,0:T(8,128)(2,1)S(1)}, u32[]{:S(2)}, u32[]{:S(2)}) collective-permute-start(s16[560,128]{1,0:T(8,128)(2,1)S(1)} %get-tuple-element.28), channel_id=1, source_target_pairs={{0,12},{4,8},{8,4},{12,0},{1,13},{5,9},{9,5},{13,1},{2,14},{6,10},... | collective-permute-start | bytes 430088 | tf_op jit(solution)/shard_map/ppermute | solution.py:271
  12.3 7.8 %collective-permute-start.4 = (s16[560,128]{1,0:T(8,128)(2,1)S(1)}, s16[560,128]{1,0:T(8,128)(2,1)S(1)}, u32[]{:S(2)}, u32[]{:S(2)}) collective-permute-start(s16[560,128]{1,0:T(8,128)(2,1)S(1)} %get-tuple-element.29), channel_id=1, source_target_pairs={{0,4},{4,0},{8,12},{12,8},{1,5},{5,1},{9,13},{13,9},{2,6},{6,2},{1... | collective-permute-start | bytes 430088 | tf_op jit(solution)/shard_map/ppermute | solution.py:271
  12.6 13.4 %collective-permute-start.7 = (s16[528,128]{1,0:T(8,128)(2,1)S(1)}, s16[528,128]{1,0:T(8,128)(2,1)S(1)}, u32[]{:S(2)}, u32[]{:S(2)}) collective-permute-start(s16[528,128]{1,0:T(8,128)(2,1)S(1)} %shard_map.39.after_ref), channel_id=1, source_target_pairs={{0,8},{4,12},{8,0},{12,4},{1,9},{5,13},{9,1},{13,5},{2,10},{6,14},... | collective-permute-start | bytes 405512 | tf_op jit(solution)/shard_map/ppermute | solution.py:271
  16.2 9.6 %collective-permute-start.8 = (s16[256,128]{1,0:T(8,128)(2,1)S(1)}, s16[256,128]{1,0:T(8,128)(2,1)S(1)}, u32[]{:S(2)}, u32[]{:S(2)}) collective-permute-start(s16[256,128]{1,0:T(8,128)(2,1)S(1)} %get-tuple-element.33), channel_id=1, source_target_pairs={{0,12},{4,8},{8,4},{12,0},{1,13},{5,9},{9,5},{13,1},{2,14},{6,10},... | collective-permute-start | bytes 196616 | tf_op jit(solution)/shard_map/ppermute | solution.py:271
  20.1 5.9 %collective-permute-start.9 = (s16[256,128]{1,0:T(8,128)(2,1)S(1)}, s16[256,128]{1,0:T(8,128)(2,1)S(1)}, u32[]{:S(2)}, u32[]{:S(2)}) collective-permute-start(s16[256,128]{1,0:T(8,128)(2,1)S(1)} %get-tuple-element.34), channel_id=1, source_target_pairs={{0,4},{4,0},{8,12},{12,8},{1,5},{5,1},{9,13},{13,9},{2,6},{6,2},{1... | collective-permute-start | bytes 196616 | tf_op jit(solution)/shard_map/ppermute | solution.py:271
  20.2 5.5 %collective-permute-start.6 = (s16[160,128]{1,0:T(8,128)(2,1)S(1)}, s16[160,128]{1,0:T(8,128)(2,1)S(1)}, u32[]{:S(2)}, u32[]{:S(2)}) collective-permute-start(s16[160,128]{1,0:T(8,128)(2,1)S(1)} %get-tuple-element.32), channel_id=1, source_target_pairs={{0,2},{1,3},{2,0},{3,1},{4,6},{5,7},{6,4},{7,5},{8,10},{9,11},{10,... | collective-permute-start | bytes 122888 | tf_op jit(solution)/shard_map/ppermute | solution.py:271
  21.8 4.0 %collective-permute-start.5 = (s16[144,128]{1,0:T(8,128)(2,1)S(1)}, s16[144,128]{1,0:T(8,128)(2,1)S(1)}, u32[]{:S(2)}, u32[]{:S(2)}) collective-permute-start(s16[144,128]{1,0:T(8,128)(2,1)S(1)} %get-tuple-element.31), channel_id=1, source_target_pairs={{0,2},{1,3},{2,0},{3,1},{4,6},{5,7},{6,4},{7,5},{8,10},{9,11},{10,... | collective-permute-start | bytes 110600 | tf_op jit(solution)/shard_map/ppermute | solution.py:271

commit v5 on v4

--- a/solution.py
+++ b/solution.py
@@ -14,8 +14,9 @@
 SPLIT = (240, 240, 512, 240)
 BLOCK = 128
 ORDER = (2, 3, 1)
-X_FIRST = ((2,), (0, 3, 1))
+X_FIRST = ((2, 0), (1, 3))
 TAIL_CUT = 2
+TAIL_ROWS = 208
 
 HBM = pl.BlockSpec(memory_space=pltpu.HBM)
 ANY = pl.BlockSpec(memory_space=pl.ANY)
@@ -47,7 +48,8 @@
 
 
 def tail(part):
-    return [groups_of(*rows) for rows in cut(SPLIT[0], part, TAIL_CUT)]
+    middle = SPLIT[0] + TAIL_ROWS
+    return [groups_of(SPLIT[0], middle), groups_of(middle, part)]
 
 
 def message_rows(groups):

time: 26.9 us -> 26.8 us (level)
  starting transfers between devices: 16.7 us -> 16.1 us
  waiting for transfers between devices: 5.87 us -> 6.28 us
    ppermute x10, starting transfers between devices: 16.7 us -> 16.1 us  [swap(): lax.ppermute(value, axis, [(i, i ^ apart) for i in range(lax.axis_size(ax...]
    ppermute x10, waiting for transfers between devices: 5.87 us -> 6.28 us  [swap(): lax.ppermute(value, axis, [(i, i ^ apart) for i in range(lax.axis_size(ax...]
  transfers between devices with their start and end apart: 10 -> 10, of which waited for: 5 -> 4; matrix products, arithmetic and copies ran while one was open for 0% -> 0% of each run, Pallas kernels for 10% -> 10%
where the time goes in v5:
time: 26.8 us; the launch traced here: 26.6 us
  starting transfers between devices  16.1 us (60%)
  waiting for transfers between devices  6.28 us (23%)
  Pallas kernels  4.2 us (16%)
    ppermute x10, starting transfers between devices, swap(): lax.ppermute(value, axis, [(i, i ^ apart) for i in range(lax.axis_size(ax...  16.1 us
    ppermute x10, waiting for transfers between devices, swap(): lax.ppermute(value, axis, [(i, i ^ apart) for i in range(lax.axis_size(ax...  6.28 us
    pallas_call x6, Pallas kernels, call(): pl.pallas_call(kernel, out_shape=outs, in_specs=specs, out_specs=jax.tree...  4.2 us
  transfers between devices with their start and end apart: 10, of which 4 were waited for; matrix products, arithmetic and copies ran while one was open for 0% of the time, Pallas kernels for 10%

profile of v5, /device:TPU:0, one launch (start us, length us, event | category | flops | bytes accessed | tf_op | source)
XLA Modules:
  0.0 26.6 jit_solution(10862405478489282191)
XLA Ops:
  0.0 0.5 %collective-permute-start = (bf16[16,4,128,128]{3,2,1,0:T(8,128)(2,1)}, bf16[16,4,128,128]{3,2,1,0:T(8,128)(2,1)S(1)}, u32[]{:S(2)}, u32[]{:S(2)}) collective-permute-start(bf16[16,4,128,128]{3,2,1,0:T(8,128)(2,1)} %blocks_ref.1), channel_id=1, source_target_pairs={{0,1},{1,0},{2,3},{3,2},{4,5},{5,4},{6,7},{7,6},{8,9},{9,8},{10,11... | collective-permute-start | bytes 6291464 | tf_op jit(solution)/shard_map/ppermute | solution.py:273
  0.5 2.3 %shard_map.37 = (s32[16,128]{1,0:T(8,128)S(4)}, f32[2176,128]{1,0:T(8,128)S(1)}, f32[2176,128]{1,0:T(8,128)S(1)}) custom-call(s32[4,64]{1,0:T(4,128)} %bitcast.1, s32[4]{0:T(128)} %low_hbm.1, bf16[16,4,128,128]{3,2,1,0:T(8,128)(2,1)} %blocks_ref.1), custom_call_target="tpu_custom_call" | custom-call | bytes 8388608 | tf_op jit(solution)/shard_map/pallas_call | solution.py:251
  2.7 1.7 %collective-permute-done.mate_ref = bf16[16,4,128,128]{3,2,1,0:T(8,128)(2,1)S(1)} collective-permute-done((bf16[16,4,128,128]{3,2,1,0:T(8,128)(2,1)}, bf16[16,4,128,128]{3,2,1,0:T(8,128)(2,1)S(1)}, u32[]{:S(2)}, u32[]{:S(2)}) %collective-permute-start) | collective-permute-done | bytes 2097184 | tf_op jit(solution)/shard_map/ppermute | solution.py:273
  4.5 0.7 %shard_map.38 = (s16[768,128]{1,0:T(8,128)(2,1)S(1)}, s16[496,128]{1,0:T(8,128)(2,1)S(1)}, s16[560,128]{1,0:T(8,128)(2,1)S(1)}, s16[560,128]{1,0:T(8,128)(2,1)S(...) custom-call(s32[16,128]{1,0:T(8,128)S(4)} %get-tuple-element.21.plan_ref.after, ...), custom_call_target="tpu_custom_call", output_to_operand_aliasing={{4}: (2, {}), {5}: (3, {})} | custom-call | bytes 1048576 | tf_op jit(solution)/shard_map/pallas_call | solution.py:251
  5.2 2.9 %collective-permute-start.1 = (s16[768,128]{1,0:T(8,128)(2,1)S(1)}, s16[768,128]{1,0:T(8,128)(2,1)S(1)}, u32[]{:S(2)}, u32[]{:S(2)}) collective-permute-start(s16[768,128]{1,0:T(8,128)(2,1)S(1)} %get-tuple-element.24), channel_id=1, source_target_pairs={{0,2},{1,3},{2,0},{3,1},{4,6},{5,7},{6,4},{7,5},{8,10},{9,11},{10,... | collective-permute-start | bytes 589832 | tf_op jit(solution)/shard_map/ppermute | solution.py:273
  8.1 3.6 %collective-permute-start.3 = (s16[560,128]{1,0:T(8,128)(2,1)S(1)}, s16[560,128]{1,0:T(8,128)(2,1)S(1)}, u32[]{:S(2)}, u32[]{:S(2)}) collective-permute-start(s16[560,128]{1,0:T(8,128)(2,1)S(1)} %get-tuple-element.30), channel_id=1, source_target_pairs={{0,12},{4,8},{8,4},{12,0},{1,13},{5,9},{9,5},{13,1},{2,14},{6,10},... | collective-permute-start | bytes 430088 | tf_op jit(solution)/shard_map/ppermute | solution.py:273
  11.8 0.0 collective-permute-start.4
  11.8 0.5 %collective-permute-start.2 = (s16[496,128]{1,0:T(8,128)(2,1)S(1)}, s16[496,128]{1,0:T(8,128)(2,1)S(1)}, u32[]{:S(2)}, u32[]{:S(2)}) collective-permute-start(s16[496,128]{1,0:T(8,128)(2,1)S(1)} %get-tuple-element.27), channel_id=1, source_target_pairs={{0,2},{1,3},{2,0},{3,1},{4,6},{5,7},{6,4},{7,5},{8,10},{9,11},{10,... | collective-permute-start | bytes 380936 | tf_op jit(solution)/shard_map/ppermute | solution.py:273
  12.3 1.1 %collective-permute-done.1.x_ref = s16[768,128]{1,0:T(8,128)(2,1)S(1)} collective-permute-done((s16[768,128]{1,0:T(8,128)(2,1)S(1)}, s16[768,128]{1,0:T(8,128)(2,1)S(1)}, u32[]{:S(2)}, u32[]{:S(2)}) %collective-permute-start.1) | collective-permute-done | bytes 196640 | tf_op jit(solution)/shard_map/ppermute | solution.py:273
  13.4 0.1 shard_map.39
  13.5 3.7 %collective-permute-start.7 = (s16[528,128]{1,0:T(8,128)(2,1)S(1)}, s16[528,128]{1,0:T(8,128)(2,1)S(1)}, u32[]{:S(2)}, u32[]{:S(2)}) collective-permute-start(s16[528,128]{1,0:T(8,128)(2,1)S(1)} %get-tuple-element.26.after_ref), channel_id=1, source_target_pairs={{0,8},{4,12},{8,0},{12,4},{1,9},{5,13},{9,1},{13,5},{2,10},{6,14},... | collective-permute-start | bytes 405512 | tf_op jit(solution)/shard_map/ppermute | solution.py:273
  17.1 0.0 collective-permute-done.2.x_ref
  17.2 0.1 shard_map.40
  17.3 2.8 %collective-permute-start.8 = (s16[256,128]{1,0:T(8,128)(2,1)S(1)}, s16[256,128]{1,0:T(8,128)(2,1)S(1)}, u32[]{:S(2)}, u32[]{:S(2)}) collective-permute-start(s16[256,128]{1,0:T(8,128)(2,1)S(1)} %get-tuple-element.36), channel_id=1, source_target_pairs={{0,12},{4,8},{8,4},{12,0},{1,13},{5,9},{9,5},{13,1},{2,14},{6,10},... | collective-permute-start | bytes 196616 | tf_op jit(solution)/shard_map/ppermute | solution.py:273
  20.1 0.0 collective-permute-start.9
  20.1 0.0 collective-permute-done.3.refs_0_
  20.1 0.0 collective-permute-done.4.refs_1_
  20.1 0.1 shard_map.41
  20.2 1.6 %collective-permute-start.5 = (s16[224,128]{1,0:T(8,128)(2,1)S(1)}, s16[224,128]{1,0:T(8,128)(2,1)S(1)}, u32[]{:S(2)}, u32[]{:S(2)}) collective-permute-start(s16[224,128]{1,0:T(8,128)(2,1)S(1)} %get-tuple-element.34), channel_id=1, source_target_pairs={{0,2},{1,3},{2,0},{3,1},{4,6},{5,7},{6,4},{7,5},{8,10},{9,11},{10,... | collective-permute-start | bytes 172040 | tf_op jit(solution)/shard_map/ppermute | solution.py:273
  21.8 0.5 %collective-permute-start.6 = (s16[80,128]{1,0:T(8,128)(2,1)S(1)}, s16[80,128]{1,0:T(8,128)(2,1)S(1)}, u32[]{:S(2)}, u32[]{:S(2)}) collective-permute-start(s16[80,128]{1,0:T(8,128)(2,1)S(1)} %get-tuple-element.35), channel_id=1, source_target_pairs={{0,2},{1,3},{2,0},{3,1},{4,6},{5,7},{6,4},{7,5},{8,10},{9,11},{10,... | collective-permute-start | bytes 61448 | tf_op jit(solution)/shard_map/ppermute | solution.py:273
  22.3 3.2 %collective-permute-done.6.refs_1_ = s16[80,128]{1,0:T(8,128)(2,1)S(1)} collective-permute-done((s16[80,128]{1,0:T(8,128)(2,1)S(1)}, s16[80,128]{1,0:T(8,128)(2,1)S(1)}, u32[]{:S(2)}, u32[]{:S(2)}) %collective-permute-start.6) | collective-permute-done | bytes 20512 | tf_op jit(solution)/shard_map/ppermute | solution.py:273
  25.6 0.0 collective-permute-done.5.refs_0_
  25.6 0.0 collective-permute-done.8.refs_3_
  25.6 0.2 collective-permute-done.9.refs_4_
  25.8 0.0 collective-permute-done.7.refs_2_
  25.8 0.8 %shard_map.42 = f32[1,512,128]{2,1,0:T(8,128)} custom-call(f32[272,128]{1,0:T(8,128)S(1)} %get-tuple-element.32.keep_q, f32[240,128]{1,0:T(8,128)S(1)} %get-tuple-element.33.keep_p, s16[224,128]{1,0:T(8,128)(2,1)S(1)} %collective-permute-done.5.refs_0_, s16[80,128]{1,0:T(8,128)(2,1)S(1)} %collective-permute-done.6.refs_1_, ...), custom_call_target="tpu_custom_call" | custom-call | bytes 1048576 | tf_op jit(solution)/shard_map/pallas_call | solution.py:251
Async XLA Ops:
  0.0 4.5 %collective-permute-start = (bf16[16,4,128,128]{3,2,1,0:T(8,128)(2,1)}, bf16[16,4,128,128]{3,2,1,0:T(8,128)(2,1)S(1)}, u32[]{:S(2)}, u32[]{:S(2)}) collective-permute-start(bf16[16,4,128,128]{3,2,1,0:T(8,128)(2,1)} %blocks_ref.1), channel_id=1, source_target_pairs={{0,1},{1,0},{2,3},{3,2},{4,5},{5,4},{6,7},{7,6},{8,9},{9,8},{10,11... | collective-permute-start | bytes 6291464 | tf_op jit(solution)/shard_map/ppermute | solution.py:273
  5.2 8.2 %collective-permute-start.1 = (s16[768,128]{1,0:T(8,128)(2,1)S(1)}, s16[768,128]{1,0:T(8,128)(2,1)S(1)}, u32[]{:S(2)}, u32[]{:S(2)}) collective-permute-start(s16[768,128]{1,0:T(8,128)(2,1)S(1)} %get-tuple-element.24), channel_id=1, source_target_pairs={{0,2},{1,3},{2,0},{3,1},{4,6},{5,7},{6,4},{7,5},{8,10},{9,11},{10,... | collective-permute-start | bytes 589832 | tf_op jit(solution)/shard_map/ppermute | solution.py:273
  8.1 11.9 %collective-permute-start.3 = (s16[560,128]{1,0:T(8,128)(2,1)S(1)}, s16[560,128]{1,0:T(8,128)(2,1)S(1)}, u32[]{:S(2)}, u32[]{:S(2)}) collective-permute-start(s16[560,128]{1,0:T(8,128)(2,1)S(1)} %get-tuple-element.30), channel_id=1, source_target_pairs={{0,12},{4,8},{8,4},{12,0},{1,13},{5,9},{9,5},{13,1},{2,14},{6,10},... | collective-permute-start | bytes 430088 | tf_op jit(solution)/shard_map/ppermute | solution.py:273
  11.8 8.3 %collective-permute-start.4 = (s16[560,128]{1,0:T(8,128)(2,1)S(1)}, s16[560,128]{1,0:T(8,128)(2,1)S(1)}, u32[]{:S(2)}, u32[]{:S(2)}) collective-permute-start(s16[560,128]{1,0:T(8,128)(2,1)S(1)} %get-tuple-element.31), channel_id=1, source_target_pairs={{0,4},{4,0},{8,12},{12,8},{1,5},{5,1},{9,13},{13,9},{2,6},{6,2},{1... | collective-permute-start | bytes 430088 | tf_op jit(solution)/shard_map/ppermute | solution.py:273
  11.8 5.4 %collective-permute-start.2 = (s16[496,128]{1,0:T(8,128)(2,1)S(1)}, s16[496,128]{1,0:T(8,128)(2,1)S(1)}, u32[]{:S(2)}, u32[]{:S(2)}) collective-permute-start(s16[496,128]{1,0:T(8,128)(2,1)S(1)} %get-tuple-element.27), channel_id=1, source_target_pairs={{0,2},{1,3},{2,0},{3,1},{4,6},{5,7},{6,4},{7,5},{8,10},{9,11},{10,... | collective-permute-start | bytes 380936 | tf_op jit(solution)/shard_map/ppermute | solution.py:273
  13.5 12.3 %collective-permute-start.7 = (s16[528,128]{1,0:T(8,128)(2,1)S(1)}, s16[528,128]{1,0:T(8,128)(2,1)S(1)}, u32[]{:S(2)}, u32[]{:S(2)}) collective-permute-start(s16[528,128]{1,0:T(8,128)(2,1)S(1)} %get-tuple-element.26.after_ref), channel_id=1, source_target_pairs={{0,8},{4,12},{8,0},{12,4},{1,9},{5,13},{9,1},{13,5},{2,10},{6,14},... | collective-permute-start | bytes 405512 | tf_op jit(solution)/shard_map/ppermute | solution.py:273
  17.3 8.3 %collective-permute-start.8 = (s16[256,128]{1,0:T(8,128)(2,1)S(1)}, s16[256,128]{1,0:T(8,128)(2,1)S(1)}, u32[]{:S(2)}, u32[]{:S(2)}) collective-permute-start(s16[256,128]{1,0:T(8,128)(2,1)S(1)} %get-tuple-element.36), channel_id=1, source_target_pairs={{0,12},{4,8},{8,4},{12,0},{1,13},{5,9},{9,5},{13,1},{2,14},{6,10},... | collective-permute-start | bytes 196616 | tf_op jit(solution)/shard_map/ppermute | solution.py:273
  20.1 5.7 %collective-permute-start.9 = (s16[256,128]{1,0:T(8,128)(2,1)S(1)}, s16[256,128]{1,0:T(8,128)(2,1)S(1)}, u32[]{:S(2)}, u32[]{:S(2)}) collective-permute-start(s16[256,128]{1,0:T(8,128)(2,1)S(1)} %get-tuple-element.28.after_ref), channel_id=1, source_target_pairs={{0,4},{4,0},{8,12},{12,8},{1,5},{5,1},{9,13},{13,9},{2,6},{6,2},{1... | collective-permute-start | bytes 196616 | tf_op jit(solution)/shard_map/ppermute | solution.py:273
  20.2 5.3 %collective-permute-start.5 = (s16[224,128]{1,0:T(8,128)(2,1)S(1)}, s16[224,128]{1,0:T(8,128)(2,1)S(1)}, u32[]{:S(2)}, u32[]{:S(2)}) collective-permute-start(s16[224,128]{1,0:T(8,128)(2,1)S(1)} %get-tuple-element.34), channel_id=1, source_target_pairs={{0,2},{1,3},{2,0},{3,1},{4,6},{5,7},{6,4},{7,5},{8,10},{9,11},{10,... | collective-permute-start | bytes 172040 | tf_op jit(solution)/shard_map/ppermute | solution.py:273
  21.8 3.8 %collective-permute-start.6 = (s16[80,128]{1,0:T(8,128)(2,1)S(1)}, s16[80,128]{1,0:T(8,128)(2,1)S(1)}, u32[]{:S(2)}, u32[]{:S(2)}) collective-permute-start(s16[80,128]{1,0:T(8,128)(2,1)S(1)} %get-tuple-element.35), channel_id=1, source_target_pairs={{0,2},{1,3},{2,0},{3,1},{4,6},{5,7},{6,4},{7,5},{8,10},{9,11},{10,... | collective-permute-start | bytes 61448 | tf_op jit(solution)/shard_map/ppermute | solution.py:273

commit v6 on v5

--- a/solution.py
+++ b/solution.py
@@ -170,15 +170,24 @@
         add_products(plan_ref, group * quota + at, mate_ref, sums_ref)
 
 
-def split_kernel(plan_ref, mate_ref, far_in, own_in, *refs):
-    *refs, far_ref, own_ref, tile = refs
+def pack_x(held, here, part, far_ref, x_ref, tile):
+    groups = [far_ref[part_rows(here ^ apart, *group, part), :] for apart, groups in held for group in groups]
+    pack(groups, x_ref, tile)
+
+
+def sums_kernel(plan_ref, mate_ref, far_in, x_ref, far_ref, tile):
     add_mate(plan_ref, mate_ref, far_ref, 1)
+    part = STRIP * far_ref.shape[1] // 4
+    pack_x(early(part)[0], lax.axis_index("row"), part, far_ref, x_ref, tile)
+
+
+def split_kernel(plan_ref, mate_ref, far_ref, own_in, *refs):
+    *refs, own_ref, tile = refs
     add_mate(plan_ref, mate_ref, own_ref, 3)
     here = lax.axis_index("row")
     part = STRIP * far_ref.shape[1] // 4
-    for held in early(part):
-        groups = [far_ref[part_rows(here ^ apart, *group, part), :] for apart, groups in held for group in groups]
-        pack(groups, refs.pop(0), tile)
+    for held in early(part)[1:]:
+        pack_x(held, here, part, far_ref, refs.pop(0), tile)
     for apart, groups in z_first(part):
         groups = [ref[part_rows(here ^ apart, *group, part), :] for ref in (far_ref, own_ref) for group in groups]
         pack(groups, refs.pop(0), tile)
@@ -312,12 +321,15 @@
 
     x_sent, z_sent = early(share), z_first(share)
     x_groups = [[group for _, groups in held for group in groups] for held in x_sent]
-    *made, far, own = call(
-        split_kernel,
-        [*[message(groups) for groups in x_groups], *[message(2 * groups) for _, groups in z_sent], strip, strip],
-        (plan, mate, far, own), [SMEM] + [VMEM] * 3, scratch=[tile],
-        aliases={2: len(x_sent) + len(z_sent), 3: len(x_sent) + len(z_sent) + 1},
-    )
+    first, far = call(
+        sums_kernel, [message(x_groups[0]), strip], (plan, mate, far), [SMEM] + [VMEM] * 2, scratch=[tile], aliases={2: 1}
+    )
+    rest_sent = [*[message(groups) for groups in x_groups[1:]], *[message(2 * groups) for _, groups in z_sent]]
+    *made, own = call(
+        split_kernel, [*rest_sent, strip], (plan, mate, far, own), [SMEM] + [VMEM] * 3, scratch=[tile],
+        aliases={3: len(rest_sent)},
+    )
+    made = [first, *made]
     over_x = [swap(made.pop(0), "tile", 2) for _ in x_sent]
     q_z = [swap(made.pop(0), "row", apart) for apart, _ in z_sent]
     after, second = plan, {}

time: 26.8 us -> 26.9 us (level)
    pallas_call x6 -> x7, Pallas kernels: 4.2 us -> 4.38 us  [call(): pl.pallas_call(kernel, out_shape=outs, in_specs=specs, out_specs=jax.tree...]
  transfers between devices with their start and end apart: 10 -> 10, of which waited for: 4 -> 7; matrix products, arithmetic and copies ran while one was open for 0% -> 0% of each run, Pallas kernels for 10% -> 12%
where the time goes in v6:
time: 26.9 us; the launch traced here: 26.7 us
  starting transfers between devices  16.1 us (60%)
  waiting for transfers between devices  6.14 us (23%)
  Pallas kernels  4.38 us (16%)
    ppermute x10, starting transfers between devices, swap(): lax.ppermute(value, axis, [(i, i ^ apart) for i in range(lax.axis_size(ax...  16.1 us
    ppermute x10, waiting for transfers between devices, swap(): lax.ppermute(value, axis, [(i, i ^ apart) for i in range(lax.axis_size(ax...  6.14 us
    pallas_call x7, Pallas kernels, call(): pl.pallas_call(kernel, out_shape=outs, in_specs=specs, out_specs=jax.tree...  4.38 us
  transfers between devices with their start and end apart: 10, of which 7 were waited for; matrix products, arithmetic and copies ran while one was open for 0% of the time, Pallas kernels for 12%

profile of v6, /device:TPU:0, one launch (start us, length us, event | category | flops | bytes accessed | tf_op | source)
XLA Modules:
  0.0 26.7 jit_solution(8853633166659613272)
XLA Ops:
  0.0 0.5 %collective-permute-start = (bf16[16,4,128,128]{3,2,1,0:T(8,128)(2,1)}, bf16[16,4,128,128]{3,2,1,0:T(8,128)(2,1)S(1)}, u32[]{:S(2)}, u32[]{:S(2)}) collective-permute-start(bf16[16,4,128,128]{3,2,1,0:T(8,128)(2,1)} %blocks_ref.1), channel_id=1, source_target_pairs={{0,1},{1,0},{2,3},{3,2},{4,5},{5,4},{6,7},{7,6},{8,9},{9,8},{10,11... | collective-permute-start | bytes 6291464 | tf_op jit(solution)/shard_map/ppermute | solution.py:282
  0.5 2.3 %shard_map.37 = (s32[16,128]{1,0:T(8,128)S(4)}, f32[2176,128]{1,0:T(8,128)S(1)}, f32[2176,128]{1,0:T(8,128)S(1)}) custom-call(s32[4,64]{1,0:T(4,128)} %bitcast.1, s32[4]{0:T(128)} %low_hbm.1, bf16[16,4,128,128]{3,2,1,0:T(8,128)(2,1)} %blocks_ref.1), custom_call_target="tpu_custom_call" | custom-call | bytes 8388608 | tf_op jit(solution)/shard_map/pallas_call | solution.py:260
  2.7 1.7 %collective-permute-done.mate_ref = bf16[16,4,128,128]{3,2,1,0:T(8,128)(2,1)S(1)} collective-permute-done((bf16[16,4,128,128]{3,2,1,0:T(8,128)(2,1)}, bf16[16,4,128,128]{3,2,1,0:T(8,128)(2,1)S(1)}, u32[]{:S(2)}, u32[]{:S(2)}) %collective-permute-start) | collective-permute-done | bytes 2097184 | tf_op jit(solution)/shard_map/ppermute | solution.py:282
  4.5 0.4 %shard_map.38 = (s16[768,128]{1,0:T(8,128)(2,1)S(1)}, f32[2176,128]{1,0:T(8,128)S(1)}) custom-call(s32[16,128]{1,0:T(8,128)S(4)} %get-tuple-element.21.plan_ref.after_ref, bf16[16,4,128,128]{3,2,1,0:T(8,128)(2,1)S(1)} %collective-permute-done.mate_ref, f32[2176,128]{1,0:T(8,128)S(1)} %get-tuple-element.22.far_in), custom_call_target="tpu_custom_call", output_to_operand_aliasing={{1}: (2, {})} | custom-call | bytes 1048576 | tf_op jit(solution)/shard_map/pallas_call | solution.py:260
  4.9 2.9 %collective-permute-start.1 = (s16[768,128]{1,0:T(8,128)(2,1)S(1)}, s16[768,128]{1,0:T(8,128)(2,1)S(1)}, u32[]{:S(2)}, u32[]{:S(2)}) collective-permute-start(s16[768,128]{1,0:T(8,128)(2,1)S(1)} %get-tuple-element.23), channel_id=1, source_target_pairs={{0,2},{1,3},{2,0},{3,1},{4,6},{5,7},{6,4},{7,5},{8,10},{9,11},{10,... | collective-permute-start | bytes 589832 | tf_op jit(solution)/shard_map/ppermute | solution.py:282
  7.8 0.5 %shard_map.39 = (s16[496,128]{1,0:T(8,128)(2,1)S(1)}, s16[560,128]{1,0:T(8,128)(2,1)S(1)}, s16[560,128]{1,0:T(8,128)(2,1)S(1)}, f32[2176,128]{1,0:T(8,128)S(1)}) custom-call(s32[16,128]{1,0:T(8,128)S(4)} %get-tuple-element.21.plan_ref.after_ref, bf16[16,4,128,128]{3,2,1,0:T(8,128)(2,1)S(1)} %collective-permute-done.mate_ref, ...), custom_call_target="tpu_custom_call", output_to_operand_aliasing={{3}: (3, {})} | custom-call | bytes 1048576 | tf_op jit(solution)/shard_map/pallas_call | solution.py:260
  8.3 3.7 %collective-permute-start.3 = (s16[560,128]{1,0:T(8,128)(2,1)S(1)}, s16[560,128]{1,0:T(8,128)(2,1)S(1)}, u32[]{:S(2)}, u32[]{:S(2)}) collective-permute-start(s16[560,128]{1,0:T(8,128)(2,1)S(1)} %get-tuple-element.30), channel_id=1, source_target_pairs={{0,12},{4,8},{8,4},{12,0},{1,13},{5,9},{9,5},{13,1},{2,14},{6,10},... | collective-permute-start | bytes 430088 | tf_op jit(solution)/shard_map/ppermute | solution.py:282
  12.0 0.0 collective-permute-start.4
  12.0 0.5 %collective-permute-start.2 = (s16[496,128]{1,0:T(8,128)(2,1)S(1)}, s16[496,128]{1,0:T(8,128)(2,1)S(1)}, u32[]{:S(2)}, u32[]{:S(2)}) collective-permute-start(s16[496,128]{1,0:T(8,128)(2,1)S(1)} %get-tuple-element.28), channel_id=1, source_target_pairs={{0,2},{1,3},{2,0},{3,1},{4,6},{5,7},{6,4},{7,5},{8,10},{9,11},{10,... | collective-permute-start | bytes 380936 | tf_op jit(solution)/shard_map/ppermute | solution.py:282
  12.5 0.5 %collective-permute-done.1.x_ref = s16[768,128]{1,0:T(8,128)(2,1)S(1)} collective-permute-done((s16[768,128]{1,0:T(8,128)(2,1)S(1)}, s16[768,128]{1,0:T(8,128)(2,1)S(1)}, u32[]{:S(2)}, u32[]{:S(2)}) %collective-permute-start.1) | collective-permute-done | bytes 196640 | tf_op jit(solution)/shard_map/ppermute | solution.py:282
  13.0 0.1 shard_map.40
  13.2 3.7 %collective-permute-start.7 = (s16[528,128]{1,0:T(8,128)(2,1)S(1)}, s16[528,128]{1,0:T(8,128)(2,1)S(1)}, u32[]{:S(2)}, u32[]{:S(2)}) collective-permute-start(s16[528,128]{1,0:T(8,128)(2,1)S(1)} %get-tuple-element.27.after_ref), channel_id=1, source_target_pairs={{0,8},{4,12},{8,0},{12,4},{1,9},{5,13},{9,1},{13,5},{2,10},{6,14},... | collective-permute-start | bytes 405512 | tf_op jit(solution)/shard_map/ppermute | solution.py:282
  16.9 0.1 collective-permute-done.2.x_ref
  16.9 0.1 shard_map.41
  17.0 2.8 %collective-permute-start.8 = (s16[256,128]{1,0:T(8,128)(2,1)S(1)}, s16[256,128]{1,0:T(8,128)(2,1)S(1)}, u32[]{:S(2)}, u32[]{:S(2)}) collective-permute-start(s16[256,128]{1,0:T(8,128)(2,1)S(1)} %get-tuple-element.36), channel_id=1, source_target_pairs={{0,12},{4,8},{8,4},{12,0},{1,13},{5,9},{9,5},{13,1},{2,14},{6,10},... | collective-permute-start | bytes 196616 | tf_op jit(solution)/shard_map/ppermute | solution.py:282
  19.8 0.0 collective-permute-start.9
  19.8 0.0 collective-permute-done.3.refs_0_
  19.8 0.1 collective-permute-done.4.refs_1_
  19.8 0.1 shard_map.42
  20.0 1.5 %collective-permute-start.5 = (s16[224,128]{1,0:T(8,128)(2,1)S(1)}, s16[224,128]{1,0:T(8,128)(2,1)S(1)}, u32[]{:S(2)}, u32[]{:S(2)}) collective-permute-start(s16[224,128]{1,0:T(8,128)(2,1)S(1)} %get-tuple-element.34), channel_id=1, source_target_pairs={{0,2},{1,3},{2,0},{3,1},{4,6},{5,7},{6,4},{7,5},{8,10},{9,11},{10,... | collective-permute-start | bytes 172040 | tf_op jit(solution)/shard_map/ppermute | solution.py:282
  21.5 0.6 %collective-permute-start.6 = (s16[80,128]{1,0:T(8,128)(2,1)S(1)}, s16[80,128]{1,0:T(8,128)(2,1)S(1)}, u32[]{:S(2)}, u32[]{:S(2)}) collective-permute-start(s16[80,128]{1,0:T(8,128)(2,1)S(1)} %get-tuple-element.35), channel_id=1, source_target_pairs={{0,2},{1,3},{2,0},{3,1},{4,6},{5,7},{6,4},{7,5},{8,10},{9,11},{10,... | collective-permute-start | bytes 61448 | tf_op jit(solution)/shard_map/ppermute | solution.py:282
  22.1 3.2 %collective-permute-done.6.refs_1_ = s16[80,128]{1,0:T(8,128)(2,1)S(1)} collective-permute-done((s16[80,128]{1,0:T(8,128)(2,1)S(1)}, s16[80,128]{1,0:T(8,128)(2,1)S(1)}, u32[]{:S(2)}, u32[]{:S(2)}) %collective-permute-start.6) | collective-permute-done | bytes 20512 | tf_op jit(solution)/shard_map/ppermute | solution.py:282
  25.3 0.0 collective-permute-done.5.refs_0_
  25.3 0.0 collective-permute-done.8.refs_3_
  25.3 0.4 %collective-permute-done.9.refs_4_ = s16[256,128]{1,0:T(8,128)(2,1)S(1)} collective-permute-done((s16[256,128]{1,0:T(8,128)(2,1)S(1)}, s16[256,128]{1,0:T(8,128)(2,1)S(1)}, u32[]{:S(2)}, u32[]{:S(2)}) %collective-permute-start.9) | collective-permute-done | bytes 65568 | tf_op jit(solution)/shard_map/ppermute | solution.py:282
  25.6 0.3 collective-permute-done.7.refs_2_
  25.9 0.8 %shard_map.43 = f32[1,512,128]{2,1,0:T(8,128)} custom-call(f32[272,128]{1,0:T(8,128)S(1)} %get-tuple-element.32.keep_q, f32[240,128]{1,0:T(8,128)S(1)} %get-tuple-element.33.keep_p, s16[224,128]{1,0:T(8,128)(2,1)S(1)} %collective-permute-done.5.refs_0_, s16[80,128]{1,0:T(8,128)(2,1)S(1)} %collective-permute-done.6.refs_1_, ...), custom_call_target="tpu_custom_call" | custom-call | bytes 1048576 | tf_op jit(solution)/shard_map/pallas_call | solution.py:260
Async XLA Ops:
  0.0 4.5 %collective-permute-start = (bf16[16,4,128,128]{3,2,1,0:T(8,128)(2,1)}, bf16[16,4,128,128]{3,2,1,0:T(8,128)(2,1)S(1)}, u32[]{:S(2)}, u32[]{:S(2)}) collective-permute-start(bf16[16,4,128,128]{3,2,1,0:T(8,128)(2,1)} %blocks_ref.1), channel_id=1, source_target_pairs={{0,1},{1,0},{2,3},{3,2},{4,5},{5,4},{6,7},{7,6},{8,9},{9,8},{10,11... | collective-permute-start | bytes 6291464 | tf_op jit(solution)/shard_map/ppermute | solution.py:282
  4.9 8.1 %collective-permute-start.1 = (s16[768,128]{1,0:T(8,128)(2,1)S(1)}, s16[768,128]{1,0:T(8,128)(2,1)S(1)}, u32[]{:S(2)}, u32[]{:S(2)}) collective-permute-start(s16[768,128]{1,0:T(8,128)(2,1)S(1)} %get-tuple-element.23), channel_id=1, source_target_pairs={{0,2},{1,3},{2,0},{3,1},{4,6},{5,7},{6,4},{7,5},{8,10},{9,11},{10,... | collective-permute-start | bytes 589832 | tf_op jit(solution)/shard_map/ppermute | solution.py:282
  8.3 11.5 %collective-permute-start.3 = (s16[560,128]{1,0:T(8,128)(2,1)S(1)}, s16[560,128]{1,0:T(8,128)(2,1)S(1)}, u32[]{:S(2)}, u32[]{:S(2)}) collective-permute-start(s16[560,128]{1,0:T(8,128)(2,1)S(1)} %get-tuple-element.30), channel_id=1, source_target_pairs={{0,12},{4,8},{8,4},{12,0},{1,13},{5,9},{9,5},{13,1},{2,14},{6,10},... | collective-permute-start | bytes 430088 | tf_op jit(solution)/shard_map/ppermute | solution.py:282
  12.0 7.9 %collective-permute-start.4 = (s16[560,128]{1,0:T(8,128)(2,1)S(1)}, s16[560,128]{1,0:T(8,128)(2,1)S(1)}, u32[]{:S(2)}, u32[]{:S(2)}) collective-permute-start(s16[560,128]{1,0:T(8,128)(2,1)S(1)} %get-tuple-element.31), channel_id=1, source_target_pairs={{0,4},{4,0},{8,12},{12,8},{1,5},{5,1},{9,13},{13,9},{2,6},{6,2},{1... | collective-permute-start | bytes 430088 | tf_op jit(solution)/shard_map/ppermute | solution.py:282
  12.0 4.9 %collective-permute-start.2 = (s16[496,128]{1,0:T(8,128)(2,1)S(1)}, s16[496,128]{1,0:T(8,128)(2,1)S(1)}, u32[]{:S(2)}, u32[]{:S(2)}) collective-permute-start(s16[496,128]{1,0:T(8,128)(2,1)S(1)} %get-tuple-element.28), channel_id=1, source_target_pairs={{0,2},{1,3},{2,0},{3,1},{4,6},{5,7},{6,4},{7,5},{8,10},{9,11},{10,... | collective-permute-start | bytes 380936 | tf_op jit(solution)/shard_map/ppermute | solution.py:282
  13.2 12.7 %collective-permute-start.7 = (s16[528,128]{1,0:T(8,128)(2,1)S(1)}, s16[528,128]{1,0:T(8,128)(2,1)S(1)}, u32[]{:S(2)}, u32[]{:S(2)}) collective-permute-start(s16[528,128]{1,0:T(8,128)(2,1)S(1)} %get-tuple-element.27.after_ref), channel_id=1, source_target_pairs={{0,8},{4,12},{8,0},{12,4},{1,9},{5,13},{9,1},{13,5},{2,10},{6,14},... | collective-permute-start | bytes 405512 | tf_op jit(solution)/shard_map/ppermute | solution.py:282
  17.0 8.2 %collective-permute-start.8 = (s16[256,128]{1,0:T(8,128)(2,1)S(1)}, s16[256,128]{1,0:T(8,128)(2,1)S(1)}, u32[]{:S(2)}, u32[]{:S(2)}) collective-permute-start(s16[256,128]{1,0:T(8,128)(2,1)S(1)} %get-tuple-element.36), channel_id=1, source_target_pairs={{0,12},{4,8},{8,4},{12,0},{1,13},{5,9},{9,5},{13,1},{2,14},{6,10},... | collective-permute-start | bytes 196616 | tf_op jit(solution)/shard_map/ppermute | solution.py:282
  19.8 5.9 %collective-permute-start.9 = (s16[256,128]{1,0:T(8,128)(2,1)S(1)}, s16[256,128]{1,0:T(8,128)(2,1)S(1)}, u32[]{:S(2)}, u32[]{:S(2)}) collective-permute-start(s16[256,128]{1,0:T(8,128)(2,1)S(1)} %get-tuple-element.29.after_ref), channel_id=1, source_target_pairs={{0,4},{4,0},{8,12},{12,8},{1,5},{5,1},{9,13},{13,9},{2,6},{6,2},{1... | collective-permute-start | bytes 196616 | tf_op jit(solution)/shard_map/ppermute | solution.py:282
  20.0 5.3 %collective-permute-start.5 = (s16[224,128]{1,0:T(8,128)(2,1)S(1)}, s16[224,128]{1,0:T(8,128)(2,1)S(1)}, u32[]{:S(2)}, u32[]{:S(2)}) collective-permute-start(s16[224,128]{1,0:T(8,128)(2,1)S(1)} %get-tuple-element.34), channel_id=1, source_target_pairs={{0,2},{1,3},{2,0},{3,1},{4,6},{5,7},{6,4},{7,5},{8,10},{9,11},{10,... | collective-permute-start | bytes 172040 | tf_op jit(solution)/shard_map/ppermute | solution.py:282
  21.5 3.8 %collective-permute-start.6 = (s16[80,128]{1,0:T(8,128)(2,1)S(1)}, s16[80,128]{1,0:T(8,128)(2,1)S(1)}, u32[]{:S(2)}, u32[]{:S(2)}) collective-permute-start(s16[80,128]{1,0:T(8,128)(2,1)S(1)} %get-tuple-element.35), channel_id=1, source_target_pairs={{0,2},{1,3},{2,0},{3,1},{4,6},{5,7},{6,4},{7,5},{8,10},{9,11},{10,... | collective-permute-start | bytes 61448 | tf_op jit(solution)/shard_map/ppermute | solution.py:282

commit v7 on v5

--- a/solution.py
+++ b/solution.py
@@ -164,16 +164,16 @@
         add_products(plan_ref, 2 * quota + at, held, own_ref)
 
 
-def add_mate(plan_ref, mate_ref, sums_ref, group):
+def add_mate(plan_ref, mate_ref, far_ref, own_ref):
     quota = mate_ref.shape[0] // 4
     for at in range(quota):
-        add_products(plan_ref, group * quota + at, mate_ref, sums_ref)
+        add_products(plan_ref, quota + at, mate_ref, far_ref)
+        add_products(plan_ref, 3 * quota + at, mate_ref, own_ref)
 
 
 def split_kernel(plan_ref, mate_ref, far_in, own_in, *refs):
     *refs, far_ref, own_ref, tile = refs
-    add_mate(plan_ref, mate_ref, far_ref, 1)
-    add_mate(plan_ref, mate_ref, own_ref, 3)
+    add_mate(plan_ref, mate_ref, far_ref, own_ref)
     here = lax.axis_index("row")
     part = STRIP * far_ref.shape[1] // 4
     for held in early(part):
@@ -235,8 +235,7 @@
 
 
 def all_kernel(plan_ref, mate_ref, far_in, own_in, x_ref, far_ref, own_ref, tile):
-    add_mate(plan_ref, mate_ref, far_ref, 1)
-    add_mate(plan_ref, mate_ref, own_ref, 3)
+    add_mate(plan_ref, mate_ref, far_ref, own_ref)
     size = far_ref.shape[1]
     pack([far_ref[low : low + rows, :] for low, rows in groups_of(0, STRIP * size)], x_ref, tile)
 

time: 26.8 us -> 26.7 us (level)
  no operation moved by 1% of the time
where the time goes in v7:
time: 26.7 us; the launch traced here: 26.6 us
  starting transfers between devices  16.1 us (60%)
  waiting for transfers between devices  6.27 us (23%)
  Pallas kernels  4.19 us (16%)
    ppermute x10, starting transfers between devices, swap(): lax.ppermute(value, axis, [(i, i ^ apart) for i in range(lax.axis_size(ax...  16.1 us
    ppermute x10, waiting for transfers between devices, swap(): lax.ppermute(value, axis, [(i, i ^ apart) for i in range(lax.axis_size(ax...  6.27 us
    pallas_call x6, Pallas kernels, call(): pl.pallas_call(kernel, out_shape=outs, in_specs=specs, out_specs=jax.tree...  4.19 us
  transfers between devices with their start and end apart: 10, of which 4 were waited for; matrix products, arithmetic and copies ran while one was open for 0% of the time, Pallas kernels for 10%

profile of v7, /device:TPU:0, one launch (start us, length us, event | category | flops | bytes accessed | tf_op | source)
XLA Modules:
  0.0 26.6 jit_solution(13743117445761126040)
XLA Ops:
  0.0 0.5 %collective-permute-start = (bf16[16,4,128,128]{3,2,1,0:T(8,128)(2,1)}, bf16[16,4,128,128]{3,2,1,0:T(8,128)(2,1)S(1)}, u32[]{:S(2)}, u32[]{:S(2)}) collective-permute-start(bf16[16,4,128,128]{3,2,1,0:T(8,128)(2,1)} %blocks_ref.1), channel_id=1, source_target_pairs={{0,1},{1,0},{2,3},{3,2},{4,5},{5,4},{6,7},{7,6},{8,9},{9,8},{10,11... | collective-permute-start | bytes 6291464 | tf_op jit(solution)/shard_map/ppermute | solution.py:272
  0.5 2.3 %shard_map.37 = (s32[16,128]{1,0:T(8,128)S(4)}, f32[2176,128]{1,0:T(8,128)S(1)}, f32[2176,128]{1,0:T(8,128)S(1)}) custom-call(s32[4,64]{1,0:T(4,128)} %bitcast.1, s32[4]{0:T(128)} %low_hbm.1, bf16[16,4,128,128]{3,2,1,0:T(8,128)(2,1)} %blocks_ref.1), custom_call_target="tpu_custom_call" | custom-call | bytes 8388608 | tf_op jit(solution)/shard_map/pallas_call | solution.py:250
  2.7 1.7 %collective-permute-done.mate_ref = bf16[16,4,128,128]{3,2,1,0:T(8,128)(2,1)S(1)} collective-permute-done((bf16[16,4,128,128]{3,2,1,0:T(8,128)(2,1)}, bf16[16,4,128,128]{3,2,1,0:T(8,128)(2,1)S(1)}, u32[]{:S(2)}, u32[]{:S(2)}) %collective-permute-start) | collective-permute-done | bytes 2097184 | tf_op jit(solution)/shard_map/ppermute | solution.py:272
  4.5 0.7 %shard_map.38 = (s16[768,128]{1,0:T(8,128)(2,1)S(1)}, s16[496,128]{1,0:T(8,128)(2,1)S(1)}, s16[560,128]{1,0:T(8,128)(2,1)S(1)}, s16[560,128]{1,0:T(8,128)(2,1)S(...) custom-call(s32[16,128]{1,0:T(8,128)S(4)} %get-tuple-element.21.plan_ref.after, ...), custom_call_target="tpu_custom_call", output_to_operand_aliasing={{4}: (2, {}), {5}: (3, {})} | custom-call | bytes 1048576 | tf_op jit(solution)/shard_map/pallas_call | solution.py:250
  5.2 2.9 %collective-permute-start.1 = (s16[768,128]{1,0:T(8,128)(2,1)S(1)}, s16[768,128]{1,0:T(8,128)(2,1)S(1)}, u32[]{:S(2)}, u32[]{:S(2)}) collective-permute-start(s16[768,128]{1,0:T(8,128)(2,1)S(1)} %get-tuple-element.24), channel_id=1, source_target_pairs={{0,2},{1,3},{2,0},{3,1},{4,6},{5,7},{6,4},{7,5},{8,10},{9,11},{10,... | collective-permute-start | bytes 589832 | tf_op jit(solution)/shard_map/ppermute | solution.py:272
  8.1 3.6 %collective-permute-start.3 = (s16[560,128]{1,0:T(8,128)(2,1)S(1)}, s16[560,128]{1,0:T(8,128)(2,1)S(1)}, u32[]{:S(2)}, u32[]{:S(2)}) collective-permute-start(s16[560,128]{1,0:T(8,128)(2,1)S(1)} %get-tuple-element.30), channel_id=1, source_target_pairs={{0,12},{4,8},{8,4},{12,0},{1,13},{5,9},{9,5},{13,1},{2,14},{6,10},... | collective-permute-start | bytes 430088 | tf_op jit(solution)/shard_map/ppermute | solution.py:272
  11.7 0.0 collective-permute-start.4
  11.7 0.5 %collective-permute-start.2 = (s16[496,128]{1,0:T(8,128)(2,1)S(1)}, s16[496,128]{1,0:T(8,128)(2,1)S(1)}, u32[]{:S(2)}, u32[]{:S(2)}) collective-permute-start(s16[496,128]{1,0:T(8,128)(2,1)S(1)} %get-tuple-element.27), channel_id=1, source_target_pairs={{0,2},{1,3},{2,0},{3,1},{4,6},{5,7},{6,4},{7,5},{8,10},{9,11},{10,... | collective-permute-start | bytes 380936 | tf_op jit(solution)/shard_map/ppermute | solution.py:272
  12.3 1.1 %collective-permute-done.1.x_ref = s16[768,128]{1,0:T(8,128)(2,1)S(1)} collective-permute-done((s16[768,128]{1,0:T(8,128)(2,1)S(1)}, s16[768,128]{1,0:T(8,128)(2,1)S(1)}, u32[]{:S(2)}, u32[]{:S(2)}) %collective-permute-start.1) | collective-permute-done | bytes 196640 | tf_op jit(solution)/shard_map/ppermute | solution.py:272
  13.3 0.1 shard_map.39
  13.5 3.7 %collective-permute-start.7 = (s16[528,128]{1,0:T(8,128)(2,1)S(1)}, s16[528,128]{1,0:T(8,128)(2,1)S(1)}, u32[]{:S(2)}, u32[]{:S(2)}) collective-permute-start(s16[528,128]{1,0:T(8,128)(2,1)S(1)} %get-tuple-element.26.after_ref), channel_id=1, source_target_pairs={{0,8},{4,12},{8,0},{12,4},{1,9},{5,13},{9,1},{13,5},{2,10},{6,14},... | collective-permute-start | bytes 405512 | tf_op jit(solution)/shard_map/ppermute | solution.py:272
  17.2 0.0 collective-permute-done.2.x_ref
  17.2 0.1 shard_map.40
  17.3 2.8 %collective-permute-start.8 = (s16[256,128]{1,0:T(8,128)(2,1)S(1)}, s16[256,128]{1,0:T(8,128)(2,1)S(1)}, u32[]{:S(2)}, u32[]{:S(2)}) collective-permute-start(s16[256,128]{1,0:T(8,128)(2,1)S(1)} %get-tuple-element.36), channel_id=1, source_target_pairs={{0,12},{4,8},{8,4},{12,0},{1,13},{5,9},{9,5},{13,1},{2,14},{6,10},... | collective-permute-start | bytes 196616 | tf_op jit(solution)/shard_map/ppermute | solution.py:272
  20.1 0.0 collective-permute-start.9
  20.1 0.0 collective-permute-done.3.refs_0_
  20.1 0.0 collective-permute-done.4.refs_1_
  20.1 0.1 shard_map.41
  20.2 1.6 %collective-permute-start.5 = (s16[224,128]{1,0:T(8,128)(2,1)S(1)}, s16[224,128]{1,0:T(8,128)(2,1)S(1)}, u32[]{:S(2)}, u32[]{:S(2)}) collective-permute-start(s16[224,128]{1,0:T(8,128)(2,1)S(1)} %get-tuple-element.34), channel_id=1, source_target_pairs={{0,2},{1,3},{2,0},{3,1},{4,6},{5,7},{6,4},{7,5},{8,10},{9,11},{10,... | collective-permute-start | bytes 172040 | tf_op jit(solution)/shard_map/ppermute | solution.py:272
  21.8 0.5 %collective-permute-start.6 = (s16[80,128]{1,0:T(8,128)(2,1)S(1)}, s16[80,128]{1,0:T(8,128)(2,1)S(1)}, u32[]{:S(2)}, u32[]{:S(2)}) collective-permute-start(s16[80,128]{1,0:T(8,128)(2,1)S(1)} %get-tuple-element.35), channel_id=1, source_target_pairs={{0,2},{1,3},{2,0},{3,1},{4,6},{5,7},{6,4},{7,5},{8,10},{9,11},{10,... | collective-permute-start | bytes 61448 | tf_op jit(solution)/shard_map/ppermute | solution.py:272
  22.3 3.2 %collective-permute-done.6.refs_1_ = s16[80,128]{1,0:T(8,128)(2,1)S(1)} collective-permute-done((s16[80,128]{1,0:T(8,128)(2,1)S(1)}, s16[80,128]{1,0:T(8,128)(2,1)S(1)}, u32[]{:S(2)}, u32[]{:S(2)}) %collective-permute-start.6) | collective-permute-done | bytes 20512 | tf_op jit(solution)/shard_map/ppermute | solution.py:272
  25.6 0.0 collective-permute-done.5.refs_0_
  25.6 0.0 collective-permute-done.8.refs_3_
  25.6 0.2 collective-permute-done.9.refs_4_
  25.8 0.0 collective-permute-done.7.refs_2_
  25.8 0.8 %shard_map.42 = f32[1,512,128]{2,1,0:T(8,128)} custom-call(f32[272,128]{1,0:T(8,128)S(1)} %get-tuple-element.32.keep_q, f32[240,128]{1,0:T(8,128)S(1)} %get-tuple-element.33.keep_p, s16[224,128]{1,0:T(8,128)(2,1)S(1)} %collective-permute-done.5.refs_0_, s16[80,128]{1,0:T(8,128)(2,1)S(1)} %collective-permute-done.6.refs_1_, ...), custom_call_target="tpu_custom_call" | custom-call | bytes 1048576 | tf_op jit(solution)/shard_map/pallas_call | solution.py:250
Async XLA Ops:
  0.0 4.5 %collective-permute-start = (bf16[16,4,128,128]{3,2,1,0:T(8,128)(2,1)}, bf16[16,4,128,128]{3,2,1,0:T(8,128)(2,1)S(1)}, u32[]{:S(2)}, u32[]{:S(2)}) collective-permute-start(bf16[16,4,128,128]{3,2,1,0:T(8,128)(2,1)} %blocks_ref.1), channel_id=1, source_target_pairs={{0,1},{1,0},{2,3},{3,2},{4,5},{5,4},{6,7},{7,6},{8,9},{9,8},{10,11... | collective-permute-start | bytes 6291464 | tf_op jit(solution)/shard_map/ppermute | solution.py:272
  5.2 8.2 %collective-permute-start.1 = (s16[768,128]{1,0:T(8,128)(2,1)S(1)}, s16[768,128]{1,0:T(8,128)(2,1)S(1)}, u32[]{:S(2)}, u32[]{:S(2)}) collective-permute-start(s16[768,128]{1,0:T(8,128)(2,1)S(1)} %get-tuple-element.24), channel_id=1, source_target_pairs={{0,2},{1,3},{2,0},{3,1},{4,6},{5,7},{6,4},{7,5},{8,10},{9,11},{10,... | collective-permute-start | bytes 589832 | tf_op jit(solution)/shard_map/ppermute | solution.py:272
  8.1 11.9 %collective-permute-start.3 = (s16[560,128]{1,0:T(8,128)(2,1)S(1)}, s16[560,128]{1,0:T(8,128)(2,1)S(1)}, u32[]{:S(2)}, u32[]{:S(2)}) collective-permute-start(s16[560,128]{1,0:T(8,128)(2,1)S(1)} %get-tuple-element.30), channel_id=1, source_target_pairs={{0,12},{4,8},{8,4},{12,0},{1,13},{5,9},{9,5},{13,1},{2,14},{6,10},... | collective-permute-start | bytes 430088 | tf_op jit(solution)/shard_map/ppermute | solution.py:272
  11.7 8.3 %collective-permute-start.4 = (s16[560,128]{1,0:T(8,128)(2,1)S(1)}, s16[560,128]{1,0:T(8,128)(2,1)S(1)}, u32[]{:S(2)}, u32[]{:S(2)}) collective-permute-start(s16[560,128]{1,0:T(8,128)(2,1)S(1)} %get-tuple-element.31), channel_id=1, source_target_pairs={{0,4},{4,0},{8,12},{12,8},{1,5},{5,1},{9,13},{13,9},{2,6},{6,2},{1... | collective-permute-start | bytes 430088 | tf_op jit(solution)/shard_map/ppermute | solution.py:272
  11.7 5.4 %collective-permute-start.2 = (s16[496,128]{1,0:T(8,128)(2,1)S(1)}, s16[496,128]{1,0:T(8,128)(2,1)S(1)}, u32[]{:S(2)}, u32[]{:S(2)}) collective-permute-start(s16[496,128]{1,0:T(8,128)(2,1)S(1)} %get-tuple-element.27), channel_id=1, source_target_pairs={{0,2},{1,3},{2,0},{3,1},{4,6},{5,7},{6,4},{7,5},{8,10},{9,11},{10,... | collective-permute-start | bytes 380936 | tf_op jit(solution)/shard_map/ppermute | solution.py:272
  13.5 12.3 %collective-permute-start.7 = (s16[528,128]{1,0:T(8,128)(2,1)S(1)}, s16[528,128]{1,0:T(8,128)(2,1)S(1)}, u32[]{:S(2)}, u32[]{:S(2)}) collective-permute-start(s16[528,128]{1,0:T(8,128)(2,1)S(1)} %get-tuple-element.26.after_ref), channel_id=1, source_target_pairs={{0,8},{4,12},{8,0},{12,4},{1,9},{5,13},{9,1},{13,5},{2,10},{6,14},... | collective-permute-start | bytes 405512 | tf_op jit(solution)/shard_map/ppermute | solution.py:272
  17.3 8.3 %collective-permute-start.8 = (s16[256,128]{1,0:T(8,128)(2,1)S(1)}, s16[256,128]{1,0:T(8,128)(2,1)S(1)}, u32[]{:S(2)}, u32[]{:S(2)}) collective-permute-start(s16[256,128]{1,0:T(8,128)(2,1)S(1)} %get-tuple-element.36), channel_id=1, source_target_pairs={{0,12},{4,8},{8,4},{12,0},{1,13},{5,9},{9,5},{13,1},{2,14},{6,10},... | collective-permute-start | bytes 196616 | tf_op jit(solution)/shard_map/ppermute | solution.py:272
  20.1 5.7 %collective-permute-start.9 = (s16[256,128]{1,0:T(8,128)(2,1)S(1)}, s16[256,128]{1,0:T(8,128)(2,1)S(1)}, u32[]{:S(2)}, u32[]{:S(2)}) collective-permute-start(s16[256,128]{1,0:T(8,128)(2,1)S(1)} %get-tuple-element.28.after_ref), channel_id=1, source_target_pairs={{0,4},{4,0},{8,12},{12,8},{1,5},{5,1},{9,13},{13,9},{2,6},{6,2},{1... | collective-permute-start | bytes 196616 | tf_op jit(solution)/shard_map/ppermute | solution.py:272
  20.2 5.3 %collective-permute-start.5 = (s16[224,128]{1,0:T(8,128)(2,1)S(1)}, s16[224,128]{1,0:T(8,128)(2,1)S(1)}, u32[]{:S(2)}, u32[]{:S(2)}) collective-permute-start(s16[224,128]{1,0:T(8,128)(2,1)S(1)} %get-tuple-element.34), channel_id=1, source_target_pairs={{0,2},{1,3},{2,0},{3,1},{4,6},{5,7},{6,4},{7,5},{8,10},{9,11},{10,... | collective-permute-start | bytes 172040 | tf_op jit(solution)/shard_map/ppermute | solution.py:272
  21.8 3.8 %collective-permute-start.6 = (s16[80,128]{1,0:T(8,128)(2,1)S(1)}, s16[80,128]{1,0:T(8,128)(2,1)S(1)}, u32[]{:S(2)}, u32[]{:S(2)}) collective-permute-start(s16[80,128]{1,0:T(8,128)(2,1)S(1)} %get-tuple-element.35), channel_id=1, source_target_pairs={{0,2},{1,3},{2,0},{3,1},{4,6},{5,7},{6,4},{7,5},{8,10},{9,11},{10,... | collective-permute-start | bytes 61448 | tf_op jit(solution)/shard_map/ppermute | solution.py:272

commit v8 on v7

--- a/solution.py
+++ b/solution.py
@@ -14,7 +14,7 @@
 SPLIT = (240, 240, 512, 240)
 BLOCK = 128
 ORDER = (2, 3, 1)
-X_FIRST = ((2, 0), (1, 3))
+X_FIRST = ((0, 2), (1, 3))
 TAIL_CUT = 2
 TAIL_ROWS = 208
 

time: 26.7 us -> 26.7 us (level)
  no operation moved by 1% of the time
where the time goes in v8:
time: 26.7 us; the launch traced here: 26.6 us
  starting transfers between devices  16.1 us (60%)
  waiting for transfers between devices  6.27 us (23%)
  Pallas kernels  4.19 us (16%)
    ppermute x10, starting transfers between devices, swap(): lax.ppermute(value, axis, [(i, i ^ apart) for i in range(lax.axis_size(ax...  16.1 us
    ppermute x10, waiting for transfers between devices, swap(): lax.ppermute(value, axis, [(i, i ^ apart) for i in range(lax.axis_size(ax...  6.27 us
    pallas_call x6, Pallas kernels, call(): pl.pallas_call(kernel, out_shape=outs, in_specs=specs, out_specs=jax.tree...  4.19 us
  transfers between devices with their start and end apart: 10, of which 4 were waited for; matrix products, arithmetic and copies ran while one was open for 0% of the time, Pallas kernels for 10%

profile of v8, /device:TPU:0, one launch (start us, length us, event | category | flops | bytes accessed | tf_op | source)
XLA Modules:
  0.0 26.6 jit_solution(8726248309907125476)
XLA Ops:
  0.0 0.5 %collective-permute-start = (bf16[16,4,128,128]{3,2,1,0:T(8,128)(2,1)}, bf16[16,4,128,128]{3,2,1,0:T(8,128)(2,1)S(1)}, u32[]{:S(2)}, u32[]{:S(2)}) collective-permute-start(bf16[16,4,128,128]{3,2,1,0:T(8,128)(2,1)} %blocks_ref.1), channel_id=1, source_target_pairs={{0,1},{1,0},{2,3},{3,2},{4,5},{5,4},{6,7},{7,6},{8,9},{9,8},{10,11... | collective-permute-start | bytes 6291464 | tf_op jit(solution)/shard_map/ppermute | solution.py:272
  0.5 2.3 %shard_map.37 = (s32[16,128]{1,0:T(8,128)S(4)}, f32[2176,128]{1,0:T(8,128)S(1)}, f32[2176,128]{1,0:T(8,128)S(1)}) custom-call(s32[4,64]{1,0:T(4,128)} %bitcast.1, s32[4]{0:T(128)} %low_hbm.1, bf16[16,4,128,128]{3,2,1,0:T(8,128)(2,1)} %blocks_ref.1), custom_call_target="tpu_custom_call" | custom-call | bytes 8388608 | tf_op jit(solution)/shard_map/pallas_call | solution.py:250
  2.7 1.7 %collective-permute-done.mate_ref = bf16[16,4,128,128]{3,2,1,0:T(8,128)(2,1)S(1)} collective-permute-done((bf16[16,4,128,128]{3,2,1,0:T(8,128)(2,1)}, bf16[16,4,128,128]{3,2,1,0:T(8,128)(2,1)S(1)}, u32[]{:S(2)}, u32[]{:S(2)}) %collective-permute-start) | collective-permute-done | bytes 2097184 | tf_op jit(solution)/shard_map/ppermute | solution.py:272
  4.5 0.7 %shard_map.38 = (s16[768,128]{1,0:T(8,128)(2,1)S(1)}, s16[496,128]{1,0:T(8,128)(2,1)S(1)}, s16[560,128]{1,0:T(8,128)(2,1)S(1)}, s16[560,128]{1,0:T(8,128)(2,1)S(...) custom-call(s32[16,128]{1,0:T(8,128)S(4)} %get-tuple-element.21.plan_ref.after, ...), custom_call_target="tpu_custom_call", output_to_operand_aliasing={{4}: (2, {}), {5}: (3, {})} | custom-call | bytes 1048576 | tf_op jit(solution)/shard_map/pallas_call | solution.py:250
  5.2 2.9 %collective-permute-start.1 = (s16[768,128]{1,0:T(8,128)(2,1)S(1)}, s16[768,128]{1,0:T(8,128)(2,1)S(1)}, u32[]{:S(2)}, u32[]{:S(2)}) collective-permute-start(s16[768,128]{1,0:T(8,128)(2,1)S(1)} %get-tuple-element.24), channel_id=1, source_target_pairs={{0,2},{1,3},{2,0},{3,1},{4,6},{5,7},{6,4},{7,5},{8,10},{9,11},{10,... | collective-permute-start | bytes 589832 | tf_op jit(solution)/shard_map/ppermute | solution.py:272
  8.1 3.6 %collective-permute-start.3 = (s16[560,128]{1,0:T(8,128)(2,1)S(1)}, s16[560,128]{1,0:T(8,128)(2,1)S(1)}, u32[]{:S(2)}, u32[]{:S(2)}) collective-permute-start(s16[560,128]{1,0:T(8,128)(2,1)S(1)} %get-tuple-element.30), channel_id=1, source_target_pairs={{0,12},{4,8},{8,4},{12,0},{1,13},{5,9},{9,5},{13,1},{2,14},{6,10},... | collective-permute-start | bytes 430088 | tf_op jit(solution)/shard_map/ppermute | solution.py:272
  11.7 0.0 collective-permute-start.4
  11.7 0.5 %collective-permute-start.2 = (s16[496,128]{1,0:T(8,128)(2,1)S(1)}, s16[496,128]{1,0:T(8,128)(2,1)S(1)}, u32[]{:S(2)}, u32[]{:S(2)}) collective-permute-start(s16[496,128]{1,0:T(8,128)(2,1)S(1)} %get-tuple-element.27), channel_id=1, source_target_pairs={{0,2},{1,3},{2,0},{3,1},{4,6},{5,7},{6,4},{7,5},{8,10},{9,11},{10,... | collective-permute-start | bytes 380936 | tf_op jit(solution)/shard_map/ppermute | solution.py:272
  12.3 1.1 %collective-permute-done.1.x_ref = s16[768,128]{1,0:T(8,128)(2,1)S(1)} collective-permute-done((s16[768,128]{1,0:T(8,128)(2,1)S(1)}, s16[768,128]{1,0:T(8,128)(2,1)S(1)}, u32[]{:S(2)}, u32[]{:S(2)}) %collective-permute-start.1) | collective-permute-done | bytes 196640 | tf_op jit(solution)/shard_map/ppermute | solution.py:272
  13.3 0.1 shard_map.39
  13.5 3.7 %collective-permute-start.7 = (s16[528,128]{1,0:T(8,128)(2,1)S(1)}, s16[528,128]{1,0:T(8,128)(2,1)S(1)}, u32[]{:S(2)}, u32[]{:S(2)}) collective-permute-start(s16[528,128]{1,0:T(8,128)(2,1)S(1)} %get-tuple-element.35), channel_id=1, source_target_pairs={{0,8},{4,12},{8,0},{12,4},{1,9},{5,13},{9,1},{13,5},{2,10},{6,14},... | collective-permute-start | bytes 405512 | tf_op jit(solution)/shard_map/ppermute | solution.py:272
  17.1 0.0 collective-permute-done.2.x_ref
  17.1 0.1 shard_map.40
  17.3 2.8 %collective-permute-start.8 = (s16[256,128]{1,0:T(8,128)(2,1)S(1)}, s16[256,128]{1,0:T(8,128)(2,1)S(1)}, u32[]{:S(2)}, u32[]{:S(2)}) collective-permute-start(s16[256,128]{1,0:T(8,128)(2,1)S(1)} %get-tuple-element.36), channel_id=1, source_target_pairs={{0,12},{4,8},{8,4},{12,0},{1,13},{5,9},{9,5},{13,1},{2,14},{6,10},... | collective-permute-start | bytes 196616 | tf_op jit(solution)/shard_map/ppermute | solution.py:272
  20.1 0.0 collective-permute-start.9
  20.1 0.0 collective-permute-done.3.refs_0_
  20.1 0.0 collective-permute-done.4.refs_1_
  20.1 0.1 shard_map.41
  20.2 1.6 %collective-permute-start.5 = (s16[224,128]{1,0:T(8,128)(2,1)S(1)}, s16[224,128]{1,0:T(8,128)(2,1)S(1)}, u32[]{:S(2)}, u32[]{:S(2)}) collective-permute-start(s16[224,128]{1,0:T(8,128)(2,1)S(1)} %get-tuple-element.33), channel_id=1, source_target_pairs={{0,2},{1,3},{2,0},{3,1},{4,6},{5,7},{6,4},{7,5},{8,10},{9,11},{10,... | collective-permute-start | bytes 172040 | tf_op jit(solution)/shard_map/ppermute | solution.py:272
  21.8 0.5 %collective-permute-start.6 = (s16[80,128]{1,0:T(8,128)(2,1)S(1)}, s16[80,128]{1,0:T(8,128)(2,1)S(1)}, u32[]{:S(2)}, u32[]{:S(2)}) collective-permute-start(s16[80,128]{1,0:T(8,128)(2,1)S(1)} %get-tuple-element.34), channel_id=1, source_target_pairs={{0,2},{1,3},{2,0},{3,1},{4,6},{5,7},{6,4},{7,5},{8,10},{9,11},{10,... | collective-permute-start | bytes 61448 | tf_op jit(solution)/shard_map/ppermute | solution.py:272
  22.3 3.2 %collective-permute-done.6.refs_1_ = s16[80,128]{1,0:T(8,128)(2,1)S(1)} collective-permute-done((s16[80,128]{1,0:T(8,128)(2,1)S(1)}, s16[80,128]{1,0:T(8,128)(2,1)S(1)}, u32[]{:S(2)}, u32[]{:S(2)}) %collective-permute-start.6) | collective-permute-done | bytes 20512 | tf_op jit(solution)/shard_map/ppermute | solution.py:272
  25.6 0.0 collective-permute-done.5.refs_0_
  25.6 0.0 collective-permute-done.8.refs_3_
  25.6 0.2 collective-permute-done.9.refs_4_
  25.8 0.0 collective-permute-done.7.refs_2_
  25.8 0.8 %shard_map.42 = f32[1,512,128]{2,1,0:T(8,128)} custom-call(f32[272,128]{1,0:T(8,128)S(1)} %get-tuple-element.32.keep_q, f32[240,128]{1,0:T(8,128)S(1)} %get-tuple-element.26.after_ref.keep_p, s16[224,128]{1,0:T(8,128)(2,1)S(1)} %collective-permute-done.5.refs_0_, s16[80,128]{1,0:T(8,128)(2,1)S(1)} %collective-permute-done.6.refs_1_, ...), custom_call_target="tpu_custom_call" | custom-call | bytes 1048576 | tf_op jit(solution)/shard_map/pallas_call | solution.py:250
Async XLA Ops:
  0.0 4.5 %collective-permute-start = (bf16[16,4,128,128]{3,2,1,0:T(8,128)(2,1)}, bf16[16,4,128,128]{3,2,1,0:T(8,128)(2,1)S(1)}, u32[]{:S(2)}, u32[]{:S(2)}) collective-permute-start(bf16[16,4,128,128]{3,2,1,0:T(8,128)(2,1)} %blocks_ref.1), channel_id=1, source_target_pairs={{0,1},{1,0},{2,3},{3,2},{4,5},{5,4},{6,7},{7,6},{8,9},{9,8},{10,11... | collective-permute-start | bytes 6291464 | tf_op jit(solution)/shard_map/ppermute | solution.py:272
  5.2 8.1 %collective-permute-start.1 = (s16[768,128]{1,0:T(8,128)(2,1)S(1)}, s16[768,128]{1,0:T(8,128)(2,1)S(1)}, u32[]{:S(2)}, u32[]{:S(2)}) collective-permute-start(s16[768,128]{1,0:T(8,128)(2,1)S(1)} %get-tuple-element.24), channel_id=1, source_target_pairs={{0,2},{1,3},{2,0},{3,1},{4,6},{5,7},{6,4},{7,5},{8,10},{9,11},{10,... | collective-permute-start | bytes 589832 | tf_op jit(solution)/shard_map/ppermute | solution.py:272
  8.1 11.9 %collective-permute-start.3 = (s16[560,128]{1,0:T(8,128)(2,1)S(1)}, s16[560,128]{1,0:T(8,128)(2,1)S(1)}, u32[]{:S(2)}, u32[]{:S(2)}) collective-permute-start(s16[560,128]{1,0:T(8,128)(2,1)S(1)} %get-tuple-element.30), channel_id=1, source_target_pairs={{0,12},{4,8},{8,4},{12,0},{1,13},{5,9},{9,5},{13,1},{2,14},{6,10},... | collective-permute-start | bytes 430088 | tf_op jit(solution)/shard_map/ppermute | solution.py:272
  11.7 8.3 %collective-permute-start.4 = (s16[560,128]{1,0:T(8,128)(2,1)S(1)}, s16[560,128]{1,0:T(8,128)(2,1)S(1)}, u32[]{:S(2)}, u32[]{:S(2)}) collective-permute-start(s16[560,128]{1,0:T(8,128)(2,1)S(1)} %get-tuple-element.31), channel_id=1, source_target_pairs={{0,4},{4,0},{8,12},{12,8},{1,5},{5,1},{9,13},{13,9},{2,6},{6,2},{1... | collective-permute-start | bytes 430088 | tf_op jit(solution)/shard_map/ppermute | solution.py:272
  11.7 5.4 %collective-permute-start.2 = (s16[496,128]{1,0:T(8,128)(2,1)S(1)}, s16[496,128]{1,0:T(8,128)(2,1)S(1)}, u32[]{:S(2)}, u32[]{:S(2)}) collective-permute-start(s16[496,128]{1,0:T(8,128)(2,1)S(1)} %get-tuple-element.27), channel_id=1, source_target_pairs={{0,2},{1,3},{2,0},{3,1},{4,6},{5,7},{6,4},{7,5},{8,10},{9,11},{10,... | collective-permute-start | bytes 380936 | tf_op jit(solution)/shard_map/ppermute | solution.py:272
  13.5 12.3 %collective-permute-start.7 = (s16[528,128]{1,0:T(8,128)(2,1)S(1)}, s16[528,128]{1,0:T(8,128)(2,1)S(1)}, u32[]{:S(2)}, u32[]{:S(2)}) collective-permute-start(s16[528,128]{1,0:T(8,128)(2,1)S(1)} %get-tuple-element.35), channel_id=1, source_target_pairs={{0,8},{4,12},{8,0},{12,4},{1,9},{5,13},{9,1},{13,5},{2,10},{6,14},... | collective-permute-start | bytes 405512 | tf_op jit(solution)/shard_map/ppermute | solution.py:272
  17.3 8.3 %collective-permute-start.8 = (s16[256,128]{1,0:T(8,128)(2,1)S(1)}, s16[256,128]{1,0:T(8,128)(2,1)S(1)}, u32[]{:S(2)}, u32[]{:S(2)}) collective-permute-start(s16[256,128]{1,0:T(8,128)(2,1)S(1)} %get-tuple-element.36), channel_id=1, source_target_pairs={{0,12},{4,8},{8,4},{12,0},{1,13},{5,9},{9,5},{13,1},{2,14},{6,10},... | collective-permute-start | bytes 196616 | tf_op jit(solution)/shard_map/ppermute | solution.py:272
  20.1 5.7 %collective-permute-start.9 = (s16[256,128]{1,0:T(8,128)(2,1)S(1)}, s16[256,128]{1,0:T(8,128)(2,1)S(1)}, u32[]{:S(2)}, u32[]{:S(2)}) collective-permute-start(s16[256,128]{1,0:T(8,128)(2,1)S(1)} %get-tuple-element.28.after_ref), channel_id=1, source_target_pairs={{0,4},{4,0},{8,12},{12,8},{1,5},{5,1},{9,13},{13,9},{2,6},{6,2},{1... | collective-permute-start | bytes 196616 | tf_op jit(solution)/shard_map/ppermute | solution.py:272
  20.2 5.3 %collective-permute-start.5 = (s16[224,128]{1,0:T(8,128)(2,1)S(1)}, s16[224,128]{1,0:T(8,128)(2,1)S(1)}, u32[]{:S(2)}, u32[]{:S(2)}) collective-permute-start(s16[224,128]{1,0:T(8,128)(2,1)S(1)} %get-tuple-element.33), channel_id=1, source_target_pairs={{0,2},{1,3},{2,0},{3,1},{4,6},{5,7},{6,4},{7,5},{8,10},{9,11},{10,... | collective-permute-start | bytes 172040 | tf_op jit(solution)/shard_map/ppermute | solution.py:272
  21.8 3.8 %collective-permute-start.6 = (s16[80,128]{1,0:T(8,128)(2,1)S(1)}, s16[80,128]{1,0:T(8,128)(2,1)S(1)}, u32[]{:S(2)}, u32[]{:S(2)}) collective-permute-start(s16[80,128]{1,0:T(8,128)(2,1)S(1)} %get-tuple-element.34), channel_id=1, source_target_pairs={{0,2},{1,3},{2,0},{3,1},{4,6},{5,7},{6,4},{7,5},{8,10},{9,11},{10,... | collective-permute-start | bytes 61448 | tf_op jit(solution)/shard_map/ppermute | solution.py:272
